TPU v7x, 128 devices: a whole 4x4x4 slice. The times are simulated.
128 devices in a mesh: dp: 16 (over y_lo, z, core), tensor: 8 (over y_hi, x).
Axes of the slice: x: 4, y: 4 (y_hi: 2, y_lo: 2; y = y_hi * 2 + y_lo), z: 4, core: 2. Of those that a mesh axis runs over, the one named last changes fastest.
Arguments:
- resid: bfloat16 [2048, 4096], P('dp'), may hold values from -22 to 22
- teacher_mixed: bfloat16 [2048, 4096], P('dp'), may hold values from -6 to 6
- gain_mix: float32 [4096], replicated, may hold values from 0.5 to 1.5
- gain_mlp: float32 [4096], replicated, may hold values from 0.5 to 1.5
- w_c: bfloat16 [4096, 4096], P(None, 'tensor'), may hold values from -0.09375 to 0.09375
- w_b: bfloat16 [4096, 1024], P(None, 'tensor'), may hold values from -0.0078125 to 0.0078125
- w_x: bfloat16 [4096, 1024], P(None, 'tensor'), may hold values from -0.09375 to 0.09375
- w_dt: bfloat16 [4096, 32], P(None, 'tensor'), may hold values from -0.09375 to 0.09375
- dt_bias: float32 [32], P('tensor'), may hold values from -2 to 1
- decay_rate: float32 [32], P('tensor'), may hold values from 9.765625e-05 to 0.05
- skip: float32 [32], P('tensor'), may hold values from 0.5 to 1.5
- w_out: bfloat16 [4096, 4096], P('tensor'), may hold values from -0.0234375 to 0.0234375
- w_gate: bfloat16 [4096, 14336], P('dp', 'tensor'), may hold values from -0.09375 to 0.09375
- w_up: bfloat16 [4096, 14336], P('dp', 'tensor'), may hold values from -0.09375 to 0.09375
Outputs:
- grad_c: float32 [4096, 4096], P('dp', 'tensor')
- grad_b: float32 [4096, 1024], P('dp', 'tensor')
- grad_x: float32 [4096, 1024], P('dp', 'tensor')
- grad_dt: float32 [4096, 32], P('dp', 'tensor')
All inputs are finite; a program needn't handle non-finite values.
Results may differ from a plain program's by a relative error of at most 0.035.
Values may be sent and summed in bfloat16 or wider, within the bound.
A program may use at most 128 MiB of HBM per device.

v0:
```python
import math

import jax
import jax.numpy as jnp
from jax import lax
from jax.sharding import PartitionSpec as P

D = 4096
FF = 14336
HEAD = 128
STATE = 128


EPS = 1e-05
HIGH_ACCURACY = lax.Precision.HIGHEST


def carried_in(shard, axis, combine, identity, reverse):
    devices, mine = (lax.axis_size(axis), lax.axis_index(axis))
    everything = jax.tree.map(
        lambda part, kind: lax.all_gather(part.astype(kind), axis),
        shard,
        (jnp.bfloat16, jnp.bfloat16),
    )
    start = jax.tree.map(
        lambda part, zero: jnp.broadcast_to(jnp.asarray(zero, part.dtype), part.shape),
        shard,
        identity,
    )

    def hop(k, before):
        at = devices - 1 - k if reverse else k
        reached = at > mine if reverse else at < mine
        new = combine(
            before, jax.tree.map(lambda part, own: part[at].astype(own.dtype), everything, shard)
        )
        return jax.tree.map(lambda a, b: jnp.where(reached, a, b), new, before)

    return lax.fori_loop(0, devices, hop, start)


def norm_rows(rows, gain):
    scale = lax.rsqrt(jnp.mean(rows * rows, axis=-1, keepdims=True) + EPS)
    return (rows * scale * gain, scale)


def local_scan(state_readout, input_injection, value_rows, raw_step, bias, rate, retained_mask):
    step_size = jax.nn.softplus(raw_step + bias)
    log_decay = jnp.cumsum(-step_size * rate, axis=0)
    score_matrix = jnp.einsum(
        "mkfb,wkb->kfmw", state_readout, input_injection, precision=HIGH_ACCURACY
    )
    ordered = jnp.transpose(log_decay, (1, 2, 0))
    spread = ordered[:, :, :, None] - ordered[:, :, None, :]
    length = state_readout.shape[0]
    causal = jnp.arange(length)[:, None] >= jnp.arange(length)[None, :]
    weight_table = (
        jnp.exp(jnp.where(causal, spread, -jnp.inf))
        * score_matrix
        * jnp.transpose(step_size, (1, 2, 0))[:, :, None, :]
    )
    mixer_result = (
        jnp.einsum("djeh,hda->edja", weight_table, value_rows, precision=HIGH_ACCURACY)
        + retained_mask[None, :, :, None] * value_rows[:, :, None, :]
    )
    tail_weight = jnp.exp(log_decay[-1][None] - log_decay) * step_size
    carried = jnp.einsum(
        "tgr,tgn,tgp->grnp", tail_weight, input_injection, value_rows, precision=HIGH_ACCURACY
    )
    return (mixer_result, carried, log_decay)


def join_states(earlier, later):
    return (earlier[0] * later[0], later[0][:, :, None, None] * earlier[1] + later[1])


def back_product(left, right):
    return lax.dot_general(
        left, right, (((1,), (1,)), ((), ())), preferred_element_type=jnp.float32
    )


def local(
    resid,
    teacher_mixed,
    gain_mix,
    gain_mlp,
    w_c,
    w_b,
    w_x,
    w_dt,
    dt_bias,
    decay_rate,
    skip,
    w_out,
    w_gate,
    w_up,
):
    tokens = resid.shape[0]
    heads = w_dt.shape[1]
    groups = w_b.shape[1] // STATE
    ratio = heads // groups
    normed, _ = norm_rows(resid.astype(jnp.float32), gain_mix)
    normed_in = normed.astype(jnp.bfloat16)
    state_readout = jnp.dot(normed_in, w_c, preferred_element_type=jnp.float32).reshape(
        tokens, groups, ratio, STATE
    )
    input_injection = jnp.dot(normed_in, w_b, preferred_element_type=jnp.float32).reshape(
        tokens, groups, STATE
    )
    value_rows = jnp.dot(normed_in, w_x, preferred_element_type=jnp.float32).reshape(
        tokens, groups, HEAD
    )
    raw_step = jnp.dot(normed_in, w_dt, preferred_element_type=jnp.float32).reshape(
        tokens, groups, ratio
    )
    bias = dt_bias.reshape(groups, ratio)
    rate = decay_rate.reshape(groups, ratio)
    retained_mask = skip.reshape(groups, ratio)
    teacher_normed, _ = norm_rows(teacher_mixed.astype(jnp.float32), gain_mlp)
    teacher_in = teacher_normed.astype(jnp.bfloat16)
    gate_full, up_full = (
        lax.all_gather(w_gate, "dp", axis=0, tiled=True),
        lax.all_gather(w_up, "dp", axis=0, tiled=True),
    )
    teacher_gate = jnp.dot(teacher_in, gate_full, preferred_element_type=jnp.float32)
    teacher_up = jnp.dot(teacher_in, up_full, preferred_element_type=jnp.float32)
    target = jax.nn.silu(teacher_gate) * teacher_up

    def mixer_of(read_part, inject_part, value_part, raw_part):
        return local_scan(read_part, inject_part, value_part, raw_part, bias, rate, retained_mask)

    (mixer_result, carried, log_decay), pullback = jax.vjp(
        mixer_of, state_readout, input_injection, value_rows, raw_step
    )
    decay = jnp.exp(log_decay[-1])
    identity = (jnp.ones_like(decay), jnp.zeros_like(carried))
    _, entering = carried_in((decay, carried), "dp", join_states, identity, False)
    growth = jnp.exp(log_decay)
    through = jnp.einsum("tgrn,grnp->tgrp", state_readout, entering, precision=HIGH_ACCURACY)
    mixer_result = mixer_result + growth[..., None] * through
    mixer_out = mixer_result.reshape(tokens, heads * HEAD).astype(jnp.bfloat16)
    mixed_cols = lax.psum_scatter(
        jnp.dot(mixer_out, w_out, preferred_element_type=jnp.float32).astype(jnp.bfloat16),
        "tensor",
        scatter_dimension=1,
        tiled=True,
    ).astype(jnp.float32)
    width = mixed_cols.shape[1]
    offset = lax.axis_index("tensor") * width
    stream = lax.dynamic_slice_in_dim(resid, offset, width, 1).astype(jnp.float32) + mixed_cols
    squares = lax.psum(jnp.sum(stream * stream, axis=1, keepdims=True), "tensor")
    scale_mid = lax.rsqrt(squares / D + EPS)
    gain_part = lax.dynamic_slice_in_dim(gain_mlp, offset, width, 0)
    normed_part = stream * scale_mid * gain_part
    normed_mid = lax.all_gather(normed_part.astype(jnp.bfloat16), "tensor", axis=1, tiled=True)
    gate = jnp.dot(normed_mid, gate_full, preferred_element_type=jnp.float32)
    up = jnp.dot(normed_mid, up_full, preferred_element_type=jnp.float32)
    student = jax.nn.silu(gate) * up
    hidden_grad = 2.0 / math.sqrt(FF) * (student - target)
    sigma = jax.nn.sigmoid(gate)
    gate_grad = (hidden_grad * up * sigma * (1.0 + gate * (1.0 - sigma))).astype(jnp.bfloat16)
    up_grad = (hidden_grad * gate * sigma).astype(jnp.bfloat16)
    mid_grad = lax.psum_scatter(
        (back_product(gate_grad, gate_full) + back_product(up_grad, up_full)).astype(jnp.bfloat16),
        "tensor",
        scatter_dimension=1,
        tiled=True,
    ).astype(jnp.float32)
    gained = mid_grad * gain_part
    inner = lax.psum(jnp.sum(gained * stream, axis=1, keepdims=True), "tensor")
    stream_grad = scale_mid * gained - stream * scale_mid**3 * (inner / D)
    delta = lax.all_gather(stream_grad.astype(jnp.bfloat16), "tensor", axis=1, tiled=True)
    out_grad = back_product(delta, w_out).reshape(tokens, groups, ratio, HEAD)
    read_enter = growth[..., None] * jnp.einsum(
        "tgrp,grnp->tgrn", out_grad, entering, precision=HIGH_ACCURACY
    )
    decay_grad = growth * jnp.sum(out_grad * through, axis=-1)
    local_grad = jnp.einsum(
        "tgr,tgrn,tgrp->grnp", growth, state_readout, out_grad, precision=HIGH_ACCURACY
    )
    _, behind = carried_in((decay, local_grad), "dp", join_states, identity, True)
    decay_grad = decay_grad.at[-1].add(decay * jnp.sum(behind * entering, axis=(2, 3)))
    read_grad, inject_grad, value_grad, step_grad = pullback((out_grad, behind, decay_grad))
    read_grad = read_grad + read_enter
    deltas = (
        read_grad.reshape(tokens, heads * STATE).astype(jnp.bfloat16),
        inject_grad.reshape(tokens, groups * STATE).astype(jnp.bfloat16),
        value_grad.reshape(tokens, groups * HEAD).astype(jnp.bfloat16),
        step_grad.reshape(tokens, heads).astype(jnp.bfloat16),
    )
    terms = [
        lax.dot_general(
            normed_in, item, (((0,), (0,)), ((), ())), preferred_element_type=jnp.float32
        )
        for item in deltas
    ]
    grad_c, grad_b, grad_x, grad_dt = (
        lax.psum_scatter(
            terms[0].astype(jnp.bfloat16), "dp", scatter_dimension=0, tiled=True
        ).astype(jnp.float32),
        lax.psum_scatter(
            terms[1].astype(jnp.bfloat16), "dp", scatter_dimension=0, tiled=True
        ).astype(jnp.float32),
        lax.psum_scatter(
            terms[2].astype(jnp.bfloat16), "dp", scatter_dimension=0, tiled=True
        ).astype(jnp.float32),
        lax.psum_scatter(
            terms[3].astype(jnp.bfloat16), "dp", scatter_dimension=0, tiled=True
        ).astype(jnp.float32),
    )
    return (grad_c, grad_b, grad_x, grad_dt)


def solution(mesh):
    in_specs = (
        P("dp", None),
        P("dp", None),
        P(),
        P(),
        P(None, "tensor"),
        P(None, "tensor"),
        P(None, "tensor"),
        P(None, "tensor"),
        P("tensor"),
        P("tensor"),
        P("tensor"),
        P("tensor", None),
        P("dp", "tensor"),
        P("dp", "tensor"),
    )
    out_specs = (P("dp", "tensor"), P("dp", "tensor"), P("dp", "tensor"), P("dp", "tensor"))
    return jax.shard_map(local, mesh=mesh, in_specs=in_specs, out_specs=out_specs, check_vma=False)
```

profile of v0, /device:TPU:1, one launch (start us, length us, event | category | flops | bytes accessed | tf_op | source)
XLA Modules:
  0.0 900.8 jit_solution(9976792930568782345)
XLA Ops:
  7.3 1.7 fusion.5
  8.9 1.8 convolution_add_fusion.1
  13.0 1.3 fusion.17
  14.7 22.2 %all_gather.30 = bf16[16,1,4]{2,1,0:T(2,128)(2,1)S(1)} all-gather(bf16[1,1,4]{2,1,0:T(2,128)(2,1)S(1)} %copy.88), channel_id=1, replica_groups=mesh['dp'=16,'tensor'=8] {'dp'}, dimensions={0}, use_global_device_ids=true | all-gather | bytes 136 | tf_op jit(solution)/shard_map/all_gather | solution.py:21
  36.9 4.0 fusion.119
  41.5 10.7 %all-gather.17.cloned.1.call-done = bf16[16,4,128,128]{3,2,1,0:T(8,128)(2,1)} async-done(((bf16[1,4,128,128]{3,2,1,0:T(8,128)(2,1)}), bf16[16,4,128,128]{3,2,1,0:T(8,128)(2,1)}) %all-gather.17.cloned.1.call-update) | async-done | bytes 2097168 | tf_op jit(solution)/shard_map/all_gather | solution.py:21
  52.2 16.8 %while.31 = (s32[]{:T(128)}, f32[1,4,128,128]{3,2,1,0:T(8,128)S(1)}, s32[]{:T(128)}, bf16[16,1,4]{2,1,0:T(2,128)(2,1)S(1)}, bf16[16,1,4,128,128]{4,3,2,1,0:T(8,128)(2,1)}, /*index=5*/s32[]{:T(128)}, s32[]{:T(128)}) while((s32[]{:T(128)}, f32[1,4,128,128]{3,2,1,0:T(8,128)S(1)}, s32[]{:T(128)}, bf16[16,1,4]{2,1,0:T(2,128)(2,1)S(1)}, ...), condition=%wide.region_3.4_spmd.clone, body=%wide.region_2.3_spmd.clone.sunk | while | flops 327688 | bytes 655505 | solution.py:39
  52.2 1.0 fusion.162
  53.3 1.0 fusion.162
  54.3 1.0 fusion.162
  55.4 1.0 fusion.162
  56.4 1.0 fusion.162
  57.5 1.0 fusion.162
  58.5 1.0 fusion.162
  59.6 1.0 fusion.162
  60.6 1.0 fusion.162
  61.7 1.0 fusion.162
  62.7 1.0 fusion.162
  63.8 1.0 fusion.162
  64.8 1.0 fusion.162
  65.9 1.0 fusion.162
  66.9 1.0 fusion.162
  68.0 1.0 fusion.162
  70.2 3.9 convolution_convert_fusion.3
  74.3 69.8 %reduce-scatter.9.cloned.1.call-done = bf16[128,512]{1,0:T(8,128)(2,1)} async-done(((bf16[128,4096]{1,0:T(8,128)(2,1)}), bf16[128,512]{1,0:T(8,128)(2,1)}) %reduce-scatter.9.cloned.1.call-update) | async-done | bytes 131088 | tf_op jit(solution)/shard_map/reduce_scatter | solution.py:143
  144.1 1.0 multiply_reduce_fusion.4
  145.1 17.7 %psum.14 = f32[128,1]{0,1:T(1,128)S(1)} all-reduce(f32[128,1]{0,1:T(1,128)S(1)} %bitcast.302), channel_id=1, replica_groups=mesh['dp'=16,'tensor'=8] {'tensor'}, use_global_device_ids=true, to_apply=%region_6.7 | all-reduce | flops 128 | bytes 1024 | tf_op jit(solution)/shard_map/psum | solution.py:152
  162.8 1.7 multiply_convert_fusion.4
  166.2 49.4 %all-gather.9.cloned.1.call-done = bf16[128,4096]{1,0:T(8,128)(2,1)} async-done(((bf16[128,512]{1,0:T(8,128)(2,1)}), bf16[128,4096]{1,0:T(8,128)(2,1)}) %all-gather.9.cloned.1.call-update) | async-done | bytes 1048592 | tf_op jit(solution)/shard_map/all_gather | solution.py:156
  215.7 84.1 %all-gather.13.cloned.1.call-done = bf16[4096,1792]{1,0:T(8,128)(2,1)} async-done(((bf16[256,1792]{1,0:T(8,128)(2,1)}), bf16[4096,1792]{1,0:T(8,128)(2,1)}) %all-gather.13.cloned.1.call-update) | async-done | bytes 14680080 | tf_op jit(solution)/shard_map/all_gather | solution.py:124
  299.8 8.5 fusion.130
  308.3 75.9 %all-gather.11.cloned.1.call-done = bf16[4096,1792]{1,0:T(8,128)(2,1)} async-done(((bf16[256,1792]{1,0:T(8,128)(2,1)}), bf16[4096,1792]{1,0:T(8,128)(2,1)}) %all-gather.11.cloned.1.call-update) | async-done | bytes 14680080 | tf_op jit(solution)/shard_map/all_gather | solution.py:123
  384.2 8.7 fusion.129
  392.9 1.3 copy-done.2
  394.2 5.4 fusion.30
  399.7 6.0 fusion.4
  405.7 10.3 %fusion.24 = f32[128,4096]{1,0:T(8,128)S(1)} fusion(bf16[4096,1792]{1,0:T(8,128)(2,1)} %all-gather.11.cloned.1.call-done, f32[128,1792]{1,0:T(8,128)S(1)} %copy-done.4, f32[128,1792]{1,0:T(8,128)} %fusion.4, f32[128,1792]{1,0:T(8,128)S(1)} %copy-done.6), kind=kOutput, calls=%fused_computation.53 | convolution fusion | flops 1881341952 | bytes 19529728 | tf_op jit(solution)/shard_map/dot_general | solution.py:78
  416.1 11.5 %fusion.2 = bf16[128,4096]{1,0:T(8,128)(2,1)} fusion(f32[128,4096]{1,0:T(8,128)S(1)} %fusion.24, bf16[4096,1792]{1,0:T(8,128)(2,1)} %all-gather.13.cloned.1.call-done, f32[128,1792]{1,0:T(8,128)} %fusion.4, f32[128,1792]{1,0:T(8,128)S(1)} %copy-done.4), kind=kOutput, calls=%fused_computation.8 | convolution fusion | flops 1881473024 | bytes 19660800 | tf_op jit(solution)/shard_map/dot_general | solution.py:78
  427.7 70.8 %reduce-scatter.11.cloned.1.call-done = bf16[128,512]{1,0:T(8,128)(2,1)} async-done(((bf16[128,4096]{1,0:T(8,128)(2,1)}), bf16[128,512]{1,0:T(8,128)(2,1)}) %reduce-scatter.11.cloned.1.call-update) | async-done | bytes 131088 | tf_op jit(solution)/shard_map/reduce_scatter | solution.py:164
  498.5 1.0 multiply_reduce_fusion.3
  499.5 17.8 %psum.15 = f32[128,1]{0,1:T(1,128)S(1)} all-reduce(f32[128,1]{0,1:T(1,128)S(1)} %bitcast.303), channel_id=1, replica_groups=mesh['dp'=16,'tensor'=8] {'tensor'}, use_global_device_ids=true, to_apply=%region_10.11 | all-reduce | flops 128 | bytes 1024 | tf_op jit(solution)/shard_map/psum | solution.py:171
  517.3 1.7 subtract_convert_fusion
  519.1 51.0 %all-gather.15.cloned.1.call-done = bf16[128,4096]{1,0:T(8,128)(2,1)} async-done(((bf16[128,512]{1,0:T(8,128)(2,1)}), bf16[128,4096]{1,0:T(8,128)(2,1)}) %all-gather.15.cloned.1.call-update) | async-done | bytes 1048592 | tf_op jit(solution)/shard_map/all_gather | solution.py:173
  570.1 4.0 fusion.131
  574.2 1.1 convolution_convert_fusion.5
  576.3 1.2 fusion.89
  577.6 32.7 %all-gather.19.cloned.1.call-done = bf16[64,128,128]{2,1,0:T(8,128)(2,1)} async-done(((bf16[4,128,128]{2,1,0:T(8,128)(2,1)}), bf16[64,128,128]{2,1,0:T(8,128)(2,1)}) %all-gather.19.cloned.1.call-update) | async-done | bytes 2097168 | tf_op jit(solution)/shard_map/all_gather | solution.py:21
  610.3 26.6 %while.32 = (s32[]{:T(128)}, f32[1,4,128,128]{3,2,1,0:T(8,128)S(1)}, s32[]{:T(128)}, bf16[16,1,4]{2,1,0:T(2,128)(2,1)}, bf16[16,1,4,128,128]{4,3,2,1,0:T(8,128)(...) while((s32[]{:T(128)}, f32[1,4,128,128]{3,2,1,0:T(8,128)S(1)}, s32[]{:T(128)}, ...), condition=%wide.region_13.14_spmd.clone, body=%wide.region_12.13_spmd.clone.sunk | while | flops 327692 | bytes 655567 | solution.py:39
  610.9 1.0 fusion.163
  612.6 1.0 fusion.163
  614.4 1.0 fusion.163
  638.2 1.1 fusion.128
  639.4 1.1 convolution_convert_fusion.4
  640.5 1.4 copy.130
  643.2 1.6 convolution_convert_fusion.1
  645.7 1.6 convolution_convert_fusion.2
  648.8 3.3 convolution_convert_fusion
  652.1 47.3 %reduce-scatter.19.cloned.1.call-done = bf16[256,4]{1,0:T(8,128)(2,1)} async-done(((bf16[4096,4]{1,0:T(8,128)(2,1)}), bf16[256,4]{1,0:T(8,128)(2,1)}) %reduce-scatter.19.cloned.1.call-update) | async-done | bytes 2064
  700.9 61.0 %reduce-scatter.17.cloned.1.call-done = bf16[256,128]{1,0:T(8,128)(2,1)} async-done(((bf16[4096,128]{1,0:T(8,128)(2,1)}), bf16[256,128]{1,0:T(8,128)(2,1)}) %reduce-scatter.17.cloned.1.call-update) | async-done | bytes 65552 | tf_op jit(solution)/shard_map/reduce_scatter | solution.py:205
  761.9 1.5 convert_element_type.214
  763.4 61.0 %reduce-scatter.15.cloned.1.call-done = bf16[256,128]{1,0:T(8,128)(2,1)} async-done(((bf16[4096,128]{1,0:T(8,128)(2,1)}), bf16[256,128]{1,0:T(8,128)(2,1)}) %reduce-scatter.15.cloned.1.call-update) | async-done | bytes 65552 | tf_op jit(solution)/shard_map/reduce_scatter | solution.py:202
  824.4 1.5 convert_element_type.210
  825.9 66.3 %reduce-scatter.13.cloned.1.call-done = bf16[256,512]{1,0:T(8,128)(2,1)} async-done(((bf16[4096,512]{1,0:T(8,128)(2,1)}), bf16[256,512]{1,0:T(8,128)(2,1)}) %reduce-scatter.13.cloned.1.call-update) | async-done | bytes 262160 | tf_op jit(solution)/shard_map/reduce_scatter | solution.py:199
  892.2 1.8 convert_element_type.206
  (195 shorter events, 37.2 us)
Async XLA Ops:
  7.2 4.7 copy-start
  7.2 4.7 copy-start.3
  7.2 4.7 copy-start.16
  7.2 3.5 copy-start.34
  7.2 45.0 %all-gather.17.cloned.1.call-start = ((), (), s32[]{:S(2)}) async-start(), calls=%async_computation.15 | async-start | bytes 2228224 | tf_op jit(solution)/shard_map/all_gather | solution.py:21
  8.9 28.0 %copy-start.27 = (f32[128]{0:T(128)}, f32[128]{0:T(128)S(1)}, u32[]{:S(2)}) copy-start(f32[128]{0:T(128)S(1)} %add_rsqrt_fusion.2) | copy-start | bytes 1540
  8.9 3.5 copy-start.35
  10.7 0.7 copy-start.25
  11.3 0.5 copy-start.30
  11.9 1.1 copy-start.23
  11.9 57.7 %copy-start.21 = (f32[128,4]{0,1:T(4,128)}, f32[128,4]{0,1:T(4,128)S(1)}, u32[]{:S(2)}) copy-start(f32[128,4]{0,1:T(4,128)S(1)} %get-tuple-element.339) | copy-start | bytes 6148
  12.4 28.5 %copy-start.12 = (f32[128,128]{1,0:T(8,128)}, f32[128,128]{1,0:T(8,128)S(1)}, u32[]{:S(2)}) copy-start(f32[128,128]{1,0:T(8,128)S(1)} %fusion.121) | copy-start | bytes 196612
  13.0 56.7 %copy-start.14 = (f32[128,128]{1,0:T(8,128)}, f32[128,128]{1,0:T(8,128)S(1)}, u32[]{:S(2)}) copy-start(f32[128,128]{1,0:T(8,128)S(1)} %fusion.123) | copy-start | bytes 196612
  14.4 129.7 %reduce-scatter.9.cloned.1.call-start = ((), (), s32[]{:S(2)}) async-start(), calls=%async_computation.6 | async-start | bytes 1179648 | tf_op jit(solution)/shard_map/reduce_scatter | solution.py:143
  36.9 32.8 %copy-start.17 = (pred[128,128]{1,0:T(8,128)(4,1)}, pred[128,128]{1,0:T(8,128)(4,1)S(1)}, u32[]{:S(2)}) copy-start(pred[128,128]{1,0:T(8,128)(4,1)S(1)} %iota_compare_fusion) | copy-start | bytes 49156
  41.5 28.2 %copy-start.7 = (f32[1,4,128,128]{3,2,1,0:T(8,128)}, f32[1,4,128,128]{3,2,1,0:T(8,128)S(1)}, u32[]{:S(2)}) copy-start(f32[1,4,128,128]{3,2,1,0:T(8,128)S(1)} %convolution_bitcast_fusion.4) | copy-start | bytes 786436
  52.2 17.5 %copy-start.32 = (f32[4]{0:T(128)S(1)}, f32[4]{0:T(128)}, u32[]{:S(2)}) copy-start(f32[4]{0:T(128)} %param.30) | copy-start | bytes 52
  69.0 1.2 copy-start.29
  69.6 4.5 copy-start.9
  70.2 4.0 copy-start.20
  74.1 91.8 %copy-start.5 = (bf16[128,4096]{1,0:T(8,128)(2,1)S(1)}, bf16[128,4096]{1,0:T(8,128)(2,1)}, u32[]{:S(2)}) copy-start(bf16[128,4096]{1,0:T(8,128)(2,1)} %param.21) | copy-start | bytes 3145732
  74.2 141.5 %all-gather.9.cloned.1.call-start = ((), (), s32[]{:S(2)}) async-start(), calls=%async_computation.7 | async-start | bytes 1179648 | tf_op jit(solution)/shard_map/all_gather | solution.py:156
  164.5 135.3 %all-gather.13.cloned.1.call-start = ((), (), s32[]{:S(2)}) async-start(), calls=%async_computation.9 | async-start | bytes 15597568 | tf_op jit(solution)/shard_map/all_gather | solution.py:124
  165.1 219.1 %all-gather.11.cloned.1.call-start = ((), (), s32[]{:S(2)}) async-start(), calls=%async_computation.8 | async-start | bytes 15597568 | tf_op jit(solution)/shard_map/all_gather | solution.py:123
  165.7 332.8 %reduce-scatter.11.cloned.1.call-start = ((), (), s32[]{:S(2)}) async-start(), calls=%async_computation.10 | async-start | bytes 1179648 | tf_op jit(solution)/shard_map/reduce_scatter | solution.py:164
  384.2 10.0 %copy-start.2 = (bf16[4096,1792]{1,0:T(8,128)(2,1)S(1)}, bf16[4096,1792]{1,0:T(8,128)(2,1)}, u32[]{:S(2)}) copy-start(bf16[4096,1792]{1,0:T(8,128)(2,1)} %all-gather.11.cloned.1.call-done) | copy-start | bytes 44040196
  384.2 15.4 %slice-start = ((s8[14680064]{0:T(1024)(128)(4,1)}), s8[4194304]{0:T(1024)(128)(4,1)S(1)}, s32[]{:S(2)}) async-start(s8[14680064]{0:T(1024)(128)(4,1)} %bitcast.286), calls=%async_computation.18 | async-start | bytes 8388608
  384.2 15.4 %slice-start.1 = ((s8[14680064]{0:T(1024)(128)(4,1)}), s8[4194304]{0:T(1024)(128)(4,1)S(1)}, s32[]{:S(2)}) async-start(s8[14680064]{0:T(1024)(128)(4,1)} %bitcast.286), calls=%async_computation.19 | async-start | bytes 8388608
  394.2 5.4 slice-start.2
  394.2 5.4 slice-start.3
  399.7 6.1 copy-start.4
  399.7 6.0 copy-start.6
  416.0 82.5 %copy-start.11 = (bf16[128,512]{1,0:T(8,128)(2,1)S(1)}, bf16[128,512]{1,0:T(8,128)(2,1)}, u32[]{:S(2)}) copy-start(bf16[128,512]{1,0:T(8,128)(2,1)} %reduce-scatter.9.cloned.1.call-done) | copy-start | bytes 393220
  427.6 142.5 %all-gather.15.cloned.1.call-start = ((), (), s32[]{:S(2)}) async-start(), calls=%async_computation.11 | async-start | bytes 1179648 | tf_op jit(solution)/shard_map/all_gather | solution.py:173
  519.0 55.2 %copy-start.22 = (f32[128,4]{0,1:T(4,128)S(1)}, f32[128,4]{0,1:T(4,128)}, u32[]{:S(2)}) copy-start(f32[128,4]{0,1:T(4,128)} %copy-done.21) | copy-start | bytes 6148
  519.0 56.3 %copy-start.13 = (f32[128,128]{1,0:T(8,128)S(1)}, f32[128,128]{1,0:T(8,128)}, u32[]{:S(2)}) copy-start(f32[128,128]{1,0:T(8,128)} %copy-done.12) | copy-start | bytes 196612
  519.0 56.5 %copy-start.10 = (f32[128,1,4,128]{0,3,2,1:T(8,128)S(1)}, f32[128,1,4,128]{0,3,2,1:T(8,128)}, u32[]{:S(2)}) copy-start(f32[128,1,4,128]{0,3,2,1:T(8,128)} %copy-done.9) | copy-start | bytes 786436
  519.0 56.5 %copy-start.33 = (f32[4]{0:T(128)S(1)}, f32[4]{0:T(128)}, u32[]{:S(2)}) copy-start(f32[4]{0:T(128)} %param.30) | copy-start | bytes 52
  519.1 57.3 %copy-start.8 = (f32[1,4,128,128]{3,2,1,0:T(8,128)S(1)}, f32[1,4,128,128]{3,2,1,0:T(8,128)}, u32[]{:S(2)}) copy-start(f32[1,4,128,128]{3,2,1,0:T(8,128)} %copy-done.7) | copy-start | bytes 786436
  519.1 57.3 %copy-start.15 = (f32[128,128]{1,0:T(8,128)S(1)}, f32[128,128]{1,0:T(8,128)}, u32[]{:S(2)}) copy-start(f32[128,128]{1,0:T(8,128)} %copy-done.14) | copy-start | bytes 196612
  519.1 57.2 %copy-start.18 = (pred[128,128]{1,0:T(8,128)(4,1)S(1)}, pred[128,128]{1,0:T(8,128)(4,1)}, u32[]{:S(2)}) copy-start(pred[128,128]{1,0:T(8,128)(4,1)} %copy-done.17) | copy-start | bytes 49156
  519.1 91.2 %all-gather.19.cloned.1.call-start = ((), (), s32[]{:S(2)}) async-start(), calls=%async_computation.16 | async-start | bytes 2228224 | tf_op jit(solution)/shard_map/all_gather | solution.py:21
  575.3 124.1 %reduce-scatter.19.cloned.1.call-start = ((), (), s32[]{:S(2)}) async-start(), calls=%async_computation.17 | async-start | bytes 1114112
  577.6 59.5 %copy-start.24 = (f32[128,4]{0,1:T(4,128)S(1)}, f32[128,4]{0,1:T(4,128)}, u32[]{:S(2)}) copy-start(f32[128,4]{0,1:T(4,128)} %copy-done.23) | copy-start | bytes 6148
  610.3 27.3 %copy-start.26 = (f32[128,4]{0,1:T(4,128)S(1)}, f32[128,4]{0,1:T(4,128)}, u32[]{:S(2)}) copy-start(f32[128,4]{0,1:T(4,128)} %copy-done.25) | copy-start | bytes 6148
  610.3 27.3 %copy-start.31 = (f32[4]{0:T(128)S(1)}, f32[4]{0:T(128)}, u32[]{:S(2)}) copy-start(f32[4]{0:T(128)} %copy-done.30) | copy-start | bytes 52
  610.3 29.1 %copy-start.28 = (f32[128]{0:T(128)S(1)}, f32[128]{0:T(128)}, u32[]{:S(2)}) copy-start(f32[128]{0:T(128)} %copy-done.27) | copy-start | bytes 1540
  639.3 2.7 copy-start.19
  642.0 119.9 %reduce-scatter.17.cloned.1.call-start = ((), (), s32[]{:S(2)}) async-start(), calls=%async_computation.14 | async-start | bytes 1114112 | tf_op jit(solution)/shard_map/reduce_scatter | solution.py:205
  644.8 179.6 %reduce-scatter.15.cloned.1.call-start = ((), (), s32[]{:S(2)}) async-start(), calls=%async_computation.13 | async-start | bytes 1114112 | tf_op jit(solution)/shard_map/reduce_scatter | solution.py:202
  647.3 244.9 %reduce-scatter.13.cloned.1.call-start = ((), (), s32[]{:S(2)}) async-start(), calls=%async_computation.12 | async-start | bytes 4456448 | tf_op jit(solution)/shard_map/reduce_scatter | solution.py:199
  652.1 241.9 %copy-start.1 = (bf16[4096,128]{1,0:T(8,128)(2,1)S(1)}, bf16[4096,128]{1,0:T(8,128)(2,1)}, u32[]{:S(2)}) copy-start(bf16[4096,128]{1,0:T(8,128)(2,1)} %param.25) | copy-start | bytes 3145732
Sparse Core Ops, SparseCore 0:
  14.5 37.6 all-gather.16
  74.3 69.7 reduce-scatter.8
  164.6 50.9 all-gather.8
  217.3 82.4 all-gather.12
  301.4 82.7 all-gather.10
  427.7 70.7 reduce-scatter.10
  519.1 50.9 all-gather.14
  575.4 34.8 all-gather.18
  642.1 57.2 reduce-scatter.18
  701.7 60.1 reduce-scatter.16
  764.3 60.1 reduce-scatter.14
  826.8 65.3 reduce-scatter.12
where the time goes:
time: 905 us; the launch traced here: 901 us
  waiting for transfers between devices  681 us (75%)
  matrix products  81.6 us (9%)
  other arithmetic  58.1 us (6%)
  blocking collectives  57.6 us (6%)
  between operations  14.8 us (2%)
    all_gather x1, waiting for transfers between devices, local(): lax.all_gather(w_up, 'dp', axis=0, tiled=True)  84.1 us
    all_gather x1, waiting for transfers between devices, local(): lax.all_gather(w_gate, 'dp', axis=0, tiled=True)  75.9 us
    reduce_scatter x1, waiting for transfers between devices, local(): lax.psum_scatter((back_product(gate_grad, gate_full) + back_product(up_gr...  70.8 us
    reduce_scatter x1, waiting for transfers between devices, local(): lax.psum_scatter(jnp.dot(mixer_out, w_out, preferred_element_type=jnp.flo...  69.8 us
    reduce_scatter x1, waiting for transfers between devices, local(): lax.psum_scatter(terms[0].astype(jnp.bfloat16), 'dp', scatter_dimension=0...  66.3 us
    reduce_scatter x1, waiting for transfers between devices, local(): lax.psum_scatter(terms[1].astype(jnp.bfloat16), 'dp', scatter_dimension=0...  61 us
    reduce_scatter x1, waiting for transfers between devices, local(): lax.psum_scatter(terms[2].astype(jnp.bfloat16), 'dp', scatter_dimension=0...  61 us
    all_gather x1, waiting for transfers between devices, local(): lax.all_gather(stream_grad.astype(jnp.bfloat16), 'tensor', axis=1, tiled=...  51 us
  transfers between devices with their start and end apart: 12, of which 12 were waited for; matrix products, arithmetic and copies ran while one was open for 3% of the time, Pallas kernels for 0%

commit v1 on v0

v1 whole, which is shorter than its diff:
```python
import functools
import math

import jax
import jax.numpy as jnp
from jax import lax
from jax.experimental import pallas as pl
from jax.experimental.pallas import tpu as pltpu
from jax.sharding import PartitionSpec as P

D = 4096
FF = 14336
EPS = 1e-05
T = 128
HEADS = 4
DP = 16
TP = 8
HID = 1792
ROWS = 256
WIDTH = 512
PACK = 896
F32 = jnp.float32
BF16 = jnp.bfloat16
MESH = pl.DeviceIdType.MESH
MIB = 1024 * 1024

LEGS = {
    "RO": ("R", 0, 0, "full", 0, -1),
    "LO": ("L", 0, 0, "full", 0, 1),
    "YO": ("Y", 0, 0, "full", 1, 0),
    "RQ": ("R", 1, 0, "Q", 1, -1),
    "LQ": ("L", 1, 0, "Q", 1, 1),
    "RA": ("R", 0, -1, "A", 0, 2),
    "LB": ("L", 0, 1, "B", 0, 2),
    "YL": ("Y", 0, -1, "P", 1, -1),
    "YR": ("Y", 0, 1, "P", 1, 1),
    "RQA": ("R", 1, -1, "QA", 1, 2),
    "LQB": ("L", 1, 1, "QB", 1, 2),
    "YO2": ("Y", 0, 2, "P", 1, 2),
}
ORDER = list(LEGS)
NSEM = 2 * len(ORDER) + 1


def place():
    me = lax.axis_index("dp")
    return me, me // 8, (me % 8) // 2, me % 2


def barrier_all(axis, size):
    me = lax.axis_index(axis)
    sem = pltpu.get_barrier_semaphore()
    for k in range(1, size):
        pl.semaphore_signal(
            sem, inc=1, device_id={axis: (me + k) % size}, device_id_type=MESH
        )
    pl.semaphore_wait(sem, size - 1)


class Gather:
    def __init__(self, piece, rows, p, qa, send, recv):
        self.piece, self.send, self.recv = piece, send, recv
        self.me, self.y, self.z, self.c = place()
        half = rows // 2
        self.rows = {
            "full": (0, rows),
            "P": (0, p),
            "Q": (p, rows - p),
            "A": (0, half),
            "B": (half, rows - half),
            "QA": (p, qa),
            "QB": (p + qa, rows - p - qa),
        }

    def block(self, flip, dz, core):
        y = (1 - self.y) if flip else self.y
        return y * 8 + ((self.z + dz + 4) % 4) * 2 + core

    def target(self, name):
        if name == "R":
            return self.block(0, 1, self.c)
        if name == "L":
            return self.block(0, -1, self.c)
        if name == "Y":
            return self.block(1, 0, self.c)
        return self.block(0, 0, 1 - self.c)

    def copy(self, ref, sem, to):
        return pltpu.make_async_remote_copy(
            src_ref=ref,
            dst_ref=ref,
            send_sem=self.send.at[sem],
            recv_sem=self.recv.at[sem],
            device_id={"dp": to},
            device_id_type=MESH,
        )

    def leg(self, name):
        to, flip, dz, rows, _, _ = LEGS[name]
        ref = self.piece(self.block(flip, dz, self.c), *self.rows[rows])
        return self.copy(ref, ORDER.index(name), self.target(to))

    def landed(self, name):
        to, _, _, rows, flip, dz = LEGS[name]
        ref = self.piece(self.block(flip, dz, self.c), *self.rows[rows])
        return self.copy(ref, ORDER.index(name), self.target(to))

    def side(self, name, core):
        if name == "own":
            flip, dz, rows, sem = 0, 0, "full", len(ORDER)
        else:
            _, _, _, rows, flip, dz = LEGS[name]
            sem = len(ORDER) + 1 + ORDER.index(name)
        ref = self.piece(self.block(flip, dz, core), *self.rows[rows])
        return self.copy(ref, sem, self.target("S"))

    def begin(self):
        for name in ("RO", "LO", "YO"):
            self.leg(name).start()
        self.side("own", self.c).start()

    def arrive(self, name, *then):
        self.landed(name).wait_recv()
        for other in then:
            self.leg(other).start()
        self.side(name, self.c).start()

    def side_arrive(self, *names):
        for name in names:
            self.side(name, 1 - self.c).wait_recv()

    def finish(self):
        for name in ORDER:
            self.leg(name).wait_send()
        for name in ["own"] + ORDER:
            self.side(name, self.c).wait_send()


def run_gather(g, use):
    g.arrive("YO", "RQ", "LQ")
    g.arrive("RO", "RA", "YL")
    g.arrive("LO", "LB", "YR")
    g.side_arrive("own")
    use(0, 0)
    g.side_arrive("YO")
    use(1, 0)
    g.arrive("RQ", "RQA")
    g.arrive("LQ", "LQB")
    g.arrive("RA", "YO2")
    g.arrive("LB")
    g.side_arrive("RO")
    use(0, -1)
    g.arrive("YL")
    g.arrive("YR")
    g.side_arrive("LO")
    use(0, 1)
    g.arrive("RQA")
    g.arrive("LQB")
    g.arrive("YO2")
    g.side_arrive("RA", "LB")
    use(0, 2)
    g.side_arrive("RQ", "YL")
    use(1, -1)
    g.side_arrive("LQ", "YR")
    use(1, 1)
    g.side_arrive("RQA", "LQB", "YO2")
    use(1, 2)


def iota(axis):
    return lax.broadcasted_iota(jnp.int32, (T, T), axis)


def mm(a, b):
    return jnp.dot(a.astype(BF16), b.astype(BF16), preferred_element_type=F32)


def mm_t(a, b):
    return lax.dot_general(
        a.astype(BF16), b.astype(BF16), (((1,), (1,)), ((), ())), preferred_element_type=F32
    )


def softplus(v):
    return jnp.maximum(v, 0.0) + jnp.log1p(jnp.exp(-jnp.abs(v)))


def steps_of(raw, params):
    step = softplus(raw + params[0:1, :])
    lower = (iota(0) >= iota(1)).astype(F32)
    decay = jnp.dot(
        lower, -step * params[1:2, :], preferred_element_type=F32, precision=lax.Precision.HIGHEST
    )
    return step, decay, jnp.transpose(step), jnp.transpose(decay)


def head(k):
    return slice(k * 128, (k + 1) * 128)


class States:
    def __init__(self, slots, sums, send, recv):
        self.slots, self.sums, self.send, self.recv = slots, sums, send, recv
        self.me, self.y, self.z, self.c = place()
        self.m = self.me % 8

    def peer(self, k):
        at = (self.m + k) % 8
        return pltpu.make_async_remote_copy(
            src_ref=self.slots.at[self.m],
            dst_ref=self.slots.at[self.m],
            send_sem=self.send.at[k - 1],
            recv_sem=self.recv.at[k - 1],
            device_id={"dp": self.y * 8 + at},
            device_id_type=MESH,
        )

    def from_peer(self, k):
        at = (self.m - k + 8) % 8
        return pltpu.make_async_remote_copy(
            src_ref=self.slots.at[at],
            dst_ref=self.slots.at[at],
            send_sem=self.send.at[k - 1],
            recv_sem=self.recv.at[k - 1],
            device_id={"dp": self.y * 8 + at},
            device_id_type=MESH,
        )

    def across(self):
        return pltpu.make_async_remote_copy(
            src_ref=self.sums.at[0],
            dst_ref=self.sums.at[1],
            send_sem=self.send.at[7],
            recv_sem=self.recv.at[7],
            device_id={"dp": (1 - self.y) * 8 + self.m},
            device_id_type=MESH,
        )

    def begin(self):
        for k in range(1, 8):
            self.peer(k).start()

    def gathered(self):
        for k in range(1, 8):
            self.from_peer(k).wait_recv()

    def finish(self):
        for k in range(1, 8):
            self.peer(k).wait_send()
        self.across().wait_send()


def front_kernel(
    resid, teacher, gain_mix, gain_mlp, w_c, w_b, w_x, w_dt, params, w_gate, w_up,
    w_all, cols, mixer_out, target, read_out, inject_out, value_out, raw_out, enter_out, decays,
    held, v_resid, v_teacher, v_wc, v_wb, v_wx, v_wdt, nin, tin, acc, proj, state, sums, through,
    in_sem, out_sem, g_send, g_recv, s_send, s_recv, d_send, d_recv, c_send, c_recv,
):
    me, y, z, c = place()
    m = me % 8
    own = [
        pltpu.make_async_copy(w_gate, held.at[me, 0], in_sem.at[0]),
        pltpu.make_async_copy(w_up, held.at[me, 1], in_sem.at[1]),
    ]
    loads = [
        pltpu.make_async_copy(src, dst, in_sem.at[2 + k])
        for k, (src, dst) in enumerate(
            ((resid, v_resid), (w_c, v_wc), (w_b, v_wb), (w_x, v_wx), (w_dt, v_wdt), (teacher, v_teacher))
        )
    ]
    for copy in own + loads:
        copy.start()
    barrier_all("dp", DP)
    for copy in own:
        copy.wait()
    gather = Gather(
        lambda j, start, size: held.at[j, :, pl.ds(start, size), :], ROWS, 112, 64, g_send, g_recv
    )
    gather.begin()

    def norm(source, gain, put):
        def square(k, total):
            part = source[:, pl.ds(pl.multiple_of(k * 256, 256), 256)].astype(F32)
            return total + jnp.sum(part * part, axis=1, keepdims=True)

        scale = lax.rsqrt(lax.fori_loop(0, 16, square, jnp.zeros((T, 1), F32)) / D + EPS)

        def write(k, _):
            at = pl.ds(pl.multiple_of(k * 256, 256), 256)
            put(k, (source[:, at].astype(F32) * scale * gain[:, at]).astype(BF16))
            return 0

        lax.fori_loop(0, 16, write, 0)

    def put_nin(k, value):
        nin[k] = value

    def put_tin(k, value):
        tin[k] = value

    loads[0].wait()
    norm(v_resid, gain_mix, put_nin)

    def column_copy(k):
        to = (me + k) % DP
        return pltpu.make_async_remote_copy(
            src_ref=nin.at[to],
            dst_ref=cols.at[me],
            send_sem=c_send.at[k - 1],
            recv_sem=c_recv.at[k - 1],
            device_id={"dp": to},
            device_id_type=MESH,
        )

    def column_landed(k):
        at = (me - k + DP) % DP
        return pltpu.make_async_remote_copy(
            src_ref=nin.at[at],
            dst_ref=cols.at[at],
            send_sem=c_send.at[k - 1],
            recv_sem=c_recv.at[k - 1],
            device_id={"dp": at},
            device_id_type=MESH,
        )

    for k in range(1, DP):
        column_copy(k).start()
    cols[me] = nin[me]

    for copy in loads[1:5]:
        copy.wait()
    proj[...] = jnp.zeros_like(proj)

    def project(k, _):
        at = pl.ds(pl.multiple_of(k * 256, 256), 256)
        rows = nin[k]
        proj[:, 0:512] += jnp.dot(rows, v_wc[at, :], preferred_element_type=F32)
        proj[:, 512:640] += jnp.dot(rows, v_wb[at, :], preferred_element_type=F32)
        proj[:, 640:768] += jnp.dot(rows, v_wx[at, :], preferred_element_type=F32)
        proj[:, 768:896] += jnp.dot(rows, v_wdt[at, :], preferred_element_type=F32)
        return 0

    lax.fori_loop(0, 16, project, 0)
    read_out[...] = proj[:, 0:512].astype(BF16)
    inject = proj[:, 512:640]
    values = proj[:, 640:768]
    inject_out[...] = inject.astype(BF16)
    value_out[...] = values.astype(BF16)
    raw_out[...] = proj[:, 768:896]
    step, decay, step_t, decay_t = steps_of(proj[:, 768:896], params)
    causal = iota(0) >= iota(1)
    inject_t = jnp.transpose(inject)
    for h in range(HEADS):
        row, col, step_row = decay_t[h : h + 1, :], decay[:, h : h + 1], step_t[h : h + 1, :]
        last = row[:, T - 1 : T]
        weight = jnp.exp(jnp.where(causal, col - row, -1e30)) * step_row
        weight = weight * mm_t(read_out[:, head(h)], inject)
        through[:, head(h)] = mm(weight, values) + params[2:3, h : h + 1] * values
        state[m, :, head(h)] = mm(inject_t * (jnp.exp(last - row) * step_row), values).astype(BF16)
    decays[m] = jnp.broadcast_to(decay[T - 1 : T, :], (8, 128))

    states = States(state, sums, s_send, s_recv)
    ends = States(decays, None, d_send, d_recv)
    states.begin()
    ends.begin()

    loads[5].wait()
    norm(v_teacher, gain_mlp, put_tin)
    acc[...] = jnp.zeros_like(acc)
    ends.gathered()
    states.gathered()

    def weights():
        run_in, run_all = jnp.zeros((1, 128), F32), jnp.zeros((1, 128), F32)
        inside, whole = [None] * 8, [None] * 8
        for j in reversed(range(8)):
            reached = (j < m).astype(F32)
            inside[j] = reached * jnp.exp(run_in)
            whole[j] = jnp.exp(run_all)
            end = decays[j, 0:1, :]
            run_in = run_in + reached * end
            run_all = run_all + end
        return inside, whole, jnp.exp(run_in)

    inside, whole, lead = weights()
    for h in range(HEADS):
        total = jnp.zeros((128, 128), F32)
        for j in range(8):
            total = total + whole[j][:, h : h + 1] * state[j, :, head(h)].astype(F32)
        sums[0, :, head(h)] = total.astype(BF16)
    states.across().start()
    states.across().wait_recv()
    after = (y == 1).astype(F32)
    for h in range(HEADS):
        total = (after * lead[:, h : h + 1]) * sums[1, :, head(h)].astype(F32)
        for j in range(8):
            total = total + inside[j][:, h : h + 1] * state[j, :, head(h)].astype(F32)
        entering = total.astype(BF16)
        enter_out[:, head(h)] = entering
        grown = jnp.exp(decay[:, h : h + 1]) * mm(read_out[:, head(h)], entering)
        mixer_out[:, head(h)] = (through[:, head(h)] + grown).astype(BF16)

    def out_copy(j):
        return pltpu.make_async_copy(held.at[j], w_all.at[j], out_sem.at[j])

    def use(flip, dz):
        base = gather.block(flip, dz, 0)

        def one(i, _):
            j = base + i
            out_copy(j).start()
            rows = tin[j]
            acc[0] += jnp.dot(rows, held[j, 0], preferred_element_type=F32)
            acc[1] += jnp.dot(rows, held[j, 1], preferred_element_type=F32)
            return 0

        lax.fori_loop(0, 2, one, 0)

    run_gather(gather, use)

    def aim(k, _):
        at = pl.ds(pl.multiple_of(k * 256, 256), 256)
        gate = acc[0, :, at]
        target[:, at] = gate * jax.nn.sigmoid(gate) * acc[1, :, at]
        return 0

    lax.fori_loop(0, HID // 256, aim, 0)
    gather.finish()
    states.finish()
    for k in range(1, 8):
        ends.peer(k).wait_send()
    for k in range(1, DP):
        column_copy(k).wait_send()
        column_landed(k).wait_recv()
    for j in range(DP):
        out_copy(j).wait()


def middle_kernel(
    mixer_out, w_out, gain_mlp, resid, target, w_all,
    out_grad,
    held, v_out, v_resid, v_target, p_send, p_recv, strm, xs, g_up, g_gate, q_send, q_recv, gained_all, delta,
    in_sem, w_sem, send, recv,
):
    t = lax.axis_index("tensor")
    copies = [
        pltpu.make_async_copy(w_out, v_out, in_sem.at[0]),
        pltpu.make_async_copy(
            resid.at[:, pl.ds(pl.multiple_of(t * WIDTH, WIDTH), WIDTH)], v_resid, in_sem.at[1]
        ),
        pltpu.make_async_copy(target, v_target, in_sem.at[2]),
    ]
    w_copies = [pltpu.make_async_copy(w_all.at[j], held.at[j], w_sem.at[j]) for j in range(DP)]
    for copy in copies:
        copy.start()
    for copy in w_copies:
        copy.start()
    barrier_all("tensor", TP)

    def move(phase, k, src, dst):
        return pltpu.make_async_remote_copy(
            src_ref=src,
            dst_ref=dst,
            send_sem=send.at[phase, k - 1],
            recv_sem=recv.at[phase, k - 1],
            device_id={"tensor": (t + k) % TP},
            device_id_type=MESH,
        )

    def columns(p):
        return pl.ds(pl.multiple_of(p * WIDTH, WIDTH), WIDTH)

    def out_part(p):
        return jnp.dot(mixer_out[...], v_out[:, columns(p)], preferred_element_type=F32)

    copies[0].wait()
    for k in range(1, TP):
        p_send[k - 1] = out_part((t + k) % TP).astype(BF16)
        move(0, k, p_send.at[k - 1], p_recv.at[k - 1]).start()
    copies[1].wait()
    stream = out_part(t) + v_resid[...].astype(F32)
    for k in range(1, TP):
        move(0, k, p_send.at[k - 1], p_recv.at[k - 1]).wait_recv()
        stream = stream + p_recv[k - 1].astype(F32)
    strm[t] = stream.astype(BF16)
    for k in range(1, TP):
        move(1, k, strm.at[t], strm.at[t]).start()
    for k in range(1, TP):
        at = (t - k + TP) % TP
        move(1, k, strm.at[at], strm.at[at]).wait_recv()

    def square(p, total):
        part = strm[p].astype(F32)
        return total + jnp.sum(part * part, axis=1, keepdims=True)

    scale = lax.rsqrt(lax.fori_loop(0, TP, square, jnp.zeros((T, 1), F32)) / D + EPS)

    def write(p, _):
        part = (strm[p].astype(F32) * scale * gain_mlp[:, columns(p)]).astype(BF16)
        xs[2 * p] = part[:, 0:256]
        xs[2 * p + 1] = part[:, 256:512]
        return 0

    lax.fori_loop(0, TP, write, 0)
    copies[2].wait()
    for copy in w_copies:
        copy.wait()

    def hidden(n, _):
        at = pl.ds(pl.multiple_of(n * 256, 256), 256)
        gate = jnp.zeros((T, 256), F32)
        up = jnp.zeros((T, 256), F32)
        for k in range(DP):
            gate = gate + jnp.dot(xs[k], held[k, 0, :, at], preferred_element_type=F32)
            up = up + jnp.dot(xs[k], held[k, 1, :, at], preferred_element_type=F32)
        sigma = jax.nn.sigmoid(gate)
        silu = gate * sigma
        grad = (2.0 / math.sqrt(FF)) * (silu * up - v_target[:, at])
        g_gate[:, at] = (grad * up * sigma * (1.0 + gate * (1.0 - sigma))).astype(BF16)
        g_up[:, at] = (grad * silu).astype(BF16)
        return 0

    lax.fori_loop(0, HID // 256, hidden, 0)

    def back(p):
        return jnp.concatenate(
            [
                mm_t(g_gate[...], held[2 * p + i, 0]) + mm_t(g_up[...], held[2 * p + i, 1])
                for i in range(2)
            ],
            axis=1,
        )

    def back_send(k, _):
        q_send[k - 1] = back((t + k) % TP).astype(BF16)
        move(2, k, q_send.at[k - 1], q_recv.at[k - 1]).start()
        return 0

    lax.fori_loop(1, TP, back_send, 0)
    mid = back(t)
    for k in range(1, TP):
        move(2, k, q_send.at[k - 1], q_recv.at[k - 1]).wait_recv()
        mid = mid + q_recv[k - 1].astype(F32)
    gained_all[t] = (mid * gain_mlp[:, columns(t)]).astype(BF16)
    for k in range(1, TP):
        move(3, k, gained_all.at[t], gained_all.at[t]).start()
    for k in range(1, TP):
        at = (t - k + TP) % TP
        move(3, k, gained_all.at[at], gained_all.at[at]).wait_recv()

    def product(p, total):
        return total + jnp.sum(
            gained_all[p].astype(F32) * strm[p].astype(F32), axis=1, keepdims=True
        )

    inner = lax.fori_loop(0, TP, product, jnp.zeros((T, 1), F32))
    pull = scale * scale * scale * (inner / D)
    out_grad[...] = jnp.zeros_like(out_grad)

    def project(p, _):
        delta[...] = (gained_all[p].astype(F32) * scale - strm[p].astype(F32) * pull).astype(BF16)
        out_grad[...] += mm_t(delta[...], v_out[:, columns(p)])
        return 0

    lax.fori_loop(0, TP, project, 0)
    for k in range(1, TP):
        move(0, k, p_send.at[k - 1], p_recv.at[k - 1]).wait_send()
        move(1, k, strm.at[t], strm.at[t]).wait_send()
        move(2, k, q_send.at[k - 1], q_recv.at[k - 1]).wait_send()
        move(3, k, gained_all.at[t], gained_all.at[t]).wait_send()


def back_kernel(
    out_grad, read, inject_in, value_in, raw, params, enter, decays, cols,
    grad_c, grad_b, grad_x, grad_dt,
    packed, state, sums, acc, cols_t, dread, dinject, dvalue,
    g_send, g_recv, s_send, s_recv,
):
    me, y, z, c = place()
    m = me % 8
    inject, values = inject_in[...].astype(F32), value_in[...].astype(F32)
    step, decay, step_t, decay_t = steps_of(raw[...], params)
    growth, growth_t = jnp.exp(decay), jnp.exp(decay_t)
    for h in range(HEADS):
        read_t = jnp.transpose(read[:, head(h)].astype(F32))
        state[m, :, head(h)] = mm(read_t * growth_t[h : h + 1, :], out_grad[:, head(h)]).astype(BF16)
    barrier_all("dp", DP)
    states = States(state, sums, s_send, s_recv)
    states.begin()

    causal = iota(0) >= iota(1)
    lanes = lax.broadcasted_iota(jnp.int32, (1, 128), 1)
    dinject[...] = jnp.zeros_like(dinject)
    dvalue[...] = jnp.zeros_like(dvalue)
    step_rows, decay_rows, decay_cols = [], [], []
    for h in range(HEADS):
        row, col, step_row = decay_t[h : h + 1, :], decay[:, h : h + 1], step_t[h : h + 1, :]
        read_h, grad_h = read[:, head(h)], out_grad[:, head(h)]
        enter_h = enter[:, head(h)]
        fade = jnp.exp(jnp.where(causal, col - row, -1e30))
        score = mm_t(read_h, inject)
        plain = fade * score
        dweight = mm_t(grad_h, values)
        direct = dweight * plain
        dscore = dweight * fade * step_row
        weight = plain * step_row
        through = mm_t(grad_h, enter_h)
        dread[:, head(h)] = mm(dscore, inject) + growth[:, h : h + 1] * through
        dinject[...] += mm(jnp.transpose(dscore), read_h)
        dvalue[...] += mm(jnp.transpose(weight), grad_h) + params[2:3, h : h + 1] * grad_h
        column = jnp.sum(direct, axis=0, keepdims=True)
        step_rows.append(column)
        decay_rows.append(-column * step_row)
        along = growth[:, h : h + 1] * jnp.sum(
            through * read_h.astype(F32), axis=1, keepdims=True
        )
        decay_cols.append(jnp.sum(direct * step_row, axis=1, keepdims=True) + along)

    def turn(k, _):
        cols_t[k] = jnp.transpose(cols[k].astype(F32)).astype(BF16)
        return 0

    lax.fori_loop(0, DP, turn, 0)
    states.gathered()
    run_in, run_all = jnp.zeros((1, 128), F32), jnp.zeros((1, 128), F32)
    inside, whole = [None] * 8, [None] * 8
    for j in range(8):
        reached = (j > m).astype(F32)
        inside[j] = reached * jnp.exp(run_in)
        whole[j] = jnp.exp(run_all)
        end = decays[j, 0:1, :]
        run_in = run_in + reached * end
        run_all = run_all + end
    lead = jnp.exp(run_in)
    for h in range(HEADS):
        total = jnp.zeros((128, 128), F32)
        for j in range(8):
            total = total + whole[j][:, h : h + 1] * state[j, :, head(h)].astype(F32)
        sums[0, :, head(h)] = total.astype(BF16)
    states.across().start()
    states.across().wait_recv()
    before = (y == 0).astype(F32)
    dstep = jnp.zeros((T, 128), F32)
    ddecay = jnp.zeros((T, 128), F32)
    step_parts, decay_parts = [], []
    for h in range(HEADS):
        row, step_row = decay_t[h : h + 1, :], step_t[h : h + 1, :]
        last = row[:, T - 1 : T]
        behind = (before * lead[:, h : h + 1]) * sums[1, :, head(h)].astype(F32)
        for j in range(8):
            behind = behind + inside[j][:, h : h + 1] * state[j, :, head(h)].astype(F32)
        tail_col = jnp.exp(decay[T - 1 : T, h : h + 1] - decay[:, h : h + 1])
        scaled_col = tail_col * step[:, h : h + 1]
        pulled = mm_t(values, behind)
        dinject[...] += scaled_col * pulled
        dvalue[...] += scaled_col * mm(inject, behind)
        drawn = tail_col * jnp.sum(inject * pulled, axis=1, keepdims=True)
        moved = drawn * step[:, h : h + 1]
        kept = jnp.exp(last) * jnp.sum(
            jnp.sum(behind * enter[:, head(h)].astype(F32), axis=1, keepdims=True),
            axis=0,
            keepdims=True,
        )
        end = kept + jnp.sum(moved, axis=0, keepdims=True)
        onehot = (lanes == h).astype(F32)
        final = (lax.broadcasted_iota(jnp.int32, (T, 1), 0) == T - 1).astype(F32)
        dstep = dstep + drawn * onehot
        ddecay = ddecay + (decay_cols[h] - moved + final * end) * onehot
    zero = jnp.zeros((128 - HEADS, 128), F32)
    dstep = dstep + jnp.transpose(jnp.concatenate(step_rows + [zero], axis=0))
    ddecay = ddecay + jnp.transpose(jnp.concatenate(decay_rows + [zero], axis=0))
    upper = (iota(0) <= iota(1)).astype(F32)
    later = jnp.dot(
        upper, ddecay, preferred_element_type=F32, precision=lax.Precision.HIGHEST
    )
    dstep = dstep - params[1:2, :] * later
    draw = dstep * jax.nn.sigmoid(raw[...] + params[0:1, :])
    packed[me, :, 0:512] = dread[...].astype(BF16)
    packed[me, :, 512:640] = dinject[...].astype(BF16)
    packed[me, :, 640:768] = dvalue[...].astype(BF16)
    packed[me, :, 768:896] = draw.astype(BF16)

    gather = Gather(lambda j, start, size: packed.at[j, pl.ds(start, size), :], T, 48, 48, g_send, g_recv)
    gather.begin()
    acc[...] = jnp.zeros_like(acc)

    def use(flip, dz):
        base = gather.block(flip, dz, 0)

        def one(i, _):
            acc[...] += jnp.dot(cols_t[base + i], packed[base + i], preferred_element_type=F32)
            return 0

        lax.fori_loop(0, 2, one, 0)

    run_gather(gather, use)
    grad_c[...] = acc[:, 0:512]
    grad_b[...] = acc[:, 512:640]
    grad_x[...] = acc[:, 640:768]
    grad_dt[...] = acc[:, 768:896]
    gather.finish()
    states.finish()


VM = pl.BlockSpec(memory_space=pltpu.VMEM)
ANY = pl.BlockSpec(memory_space=pl.ANY)
DMA = pltpu.SemaphoreType.DMA


def struct(shape, dtype):
    return jax.ShapeDtypeStruct(shape, dtype)


def params_of(number):
    return pltpu.CompilerParams(
        collective_id=number, has_side_effects=True, vmem_limit_bytes=60 * MIB
    )


def local(
    resid, teacher_mixed, gain_mix, gain_mlp, w_c, w_b, w_x, w_dt, dt_bias, decay_rate, skip, w_out,
    w_gate, w_up,
):
    w_dt_wide = jnp.pad(w_dt, ((0, 0), (0, 128 - HEADS)))
    scalars = jnp.pad(jnp.stack([dt_bias, decay_rate, skip]), ((0, 5), (0, 128 - HEADS)))
    gain_mix, gain_mlp = gain_mix.reshape(1, D), gain_mlp.reshape(1, D)
    w_all, cols, mixer_out, target, read, inject, values, raw, enter, decays = pl.pallas_call(
        front_kernel,
        out_shape=(
            struct((DP, 2, ROWS, HID), BF16),
            struct((DP, T, 256), BF16),
            struct((T, WIDTH), BF16),
            struct((T, HID), F32),
            struct((T, WIDTH), BF16),
            struct((T, 128), BF16),
            struct((T, 128), BF16),
            struct((T, 128), F32),
            struct((128, WIDTH), BF16),
            struct((8, 8, 128), F32),
        ),
        in_specs=[ANY, ANY, VM, VM, ANY, ANY, ANY, ANY, VM, ANY, ANY],
        out_specs=(ANY,) + (VM,) * 9,
        scratch_shapes=[
            pltpu.VMEM((DP, 2, ROWS, HID), BF16),
            pltpu.VMEM((T, D), BF16),
            pltpu.VMEM((T, D), BF16),
            pltpu.VMEM((D, 512), BF16),
            pltpu.VMEM((D, 128), BF16),
            pltpu.VMEM((D, 128), BF16),
            pltpu.VMEM((D, 128), BF16),
            pltpu.VMEM((16, T, 256), BF16),
            pltpu.VMEM((16, T, 256), BF16),
            pltpu.VMEM((2, T, HID), F32),
            pltpu.VMEM((T, PACK), F32),
            pltpu.VMEM((8, 128, WIDTH), BF16),
            pltpu.VMEM((2, 128, WIDTH), BF16),
            pltpu.VMEM((T, WIDTH), F32),
            DMA((8,)),
            DMA((DP,)),
            DMA((NSEM,)),
            DMA((NSEM,)),
            DMA((8,)),
            DMA((8,)),
            DMA((8,)),
            DMA((8,)),
            DMA((DP,)),
            DMA((DP,)),
        ],
        compiler_params=params_of(0),
        name="front",
    )(resid, teacher_mixed, gain_mix, gain_mlp, w_c, w_b, w_x, w_dt_wide, scalars, w_gate, w_up)
    out_grad = pl.pallas_call(
        middle_kernel,
        out_shape=struct((T, WIDTH), F32),
        in_specs=[VM, ANY, VM, ANY, ANY, ANY],
        out_specs=VM,
        scratch_shapes=[
            pltpu.VMEM((DP, 2, ROWS, HID), BF16),
            pltpu.VMEM((512, D), BF16),
            pltpu.VMEM((T, WIDTH), BF16),
            pltpu.VMEM((T, HID), F32),
            pltpu.VMEM((TP - 1, T, WIDTH), BF16),
            pltpu.VMEM((TP - 1, T, WIDTH), BF16),
            pltpu.VMEM((TP, T, WIDTH), BF16),
            pltpu.VMEM((16, T, 256), BF16),
            pltpu.VMEM((T, HID), BF16),
            pltpu.VMEM((T, HID), BF16),
            pltpu.VMEM((TP - 1, T, WIDTH), BF16),
            pltpu.VMEM((TP - 1, T, WIDTH), BF16),
            pltpu.VMEM((TP, T, WIDTH), BF16),
            pltpu.VMEM((T, WIDTH), BF16),
            DMA((4,)),
            DMA((DP,)),
            DMA((4, TP - 1)),
            DMA((4, TP - 1)),
        ],
        compiler_params=params_of(1),
        name="middle",
    )(mixer_out, w_out, gain_mlp, resid, target, w_all)
    grad_c, grad_b, grad_x, grad_dt = pl.pallas_call(
        back_kernel,
        out_shape=(
            struct((ROWS, 512), F32),
            struct((ROWS, 128), F32),
            struct((ROWS, 128), F32),
            struct((ROWS, 128), F32),
        ),
        in_specs=[VM] * 9,
        out_specs=(VM,) * 4,
        scratch_shapes=[
            pltpu.VMEM((DP, T, PACK), BF16),
            pltpu.VMEM((8, 128, WIDTH), BF16),
            pltpu.VMEM((2, 128, WIDTH), BF16),
            pltpu.VMEM((ROWS, PACK), F32),
            pltpu.VMEM((DP, 256, T), BF16),
            pltpu.VMEM((T, WIDTH), F32),
            pltpu.VMEM((T, 128), F32),
            pltpu.VMEM((T, 128), F32),
            DMA((NSEM,)),
            DMA((NSEM,)),
            DMA((8,)),
            DMA((8,)),
        ],
        compiler_params=params_of(2),
        name="back",
    )(out_grad, read, inject, values, raw, scalars, enter, decays, cols)
    return grad_c, grad_b, grad_x, grad_dt[:, 0:HEADS]


def solution(mesh):
    in_specs = (
        P("dp", None),
        P("dp", None),
        P(),
        P(),
        P(None, "tensor"),
        P(None, "tensor"),
        P(None, "tensor"),
        P(None, "tensor"),
        P("tensor"),
        P("tensor"),
        P("tensor"),
        P("tensor", None),
        P("dp", "tensor"),
        P("dp", "tensor"),
    )
    out_specs = (P("dp", "tensor"), P("dp", "tensor"), P("dp", "tensor"), P("dp", "tensor"))
    return jax.shard_map(local, mesh=mesh, in_specs=in_specs, out_specs=out_specs, check_vma=False)
```

time: 905 us -> 288 us (0.32)
  waiting for transfers between devices: 681 us -> 0 us
  Pallas kernels: 0 us -> 276 us
  matrix products: 81.6 us -> 0 us
  blocking collectives: 57.6 us -> 0 us
  other arithmetic: 58.1 us -> 1.29 us
  between operations: 14.8 us -> 0.66 us
    reduce_scatter x5 -> x0, waiting for transfers between devices: 329 us -> none  [the longest x1 70.8 us: local(): lax.psum_scatter((back_product(gate_grad, gate_full) + back_product(up_gr...]
    all_gather x6 -> x0, waiting for transfers between devices: 304 us -> none  [the longest x1 84.1 us: local(): lax.all_gather(w_up, 'dp', axis=0, tiled=True)]
    pallas_call x0 -> x3, Pallas kernels: none -> 276 us  [the longest x1 148 us: local(): pl.pallas_call(front_kernel, out_shape=(struct((DP, 2, ROWS, HID), BF16),...]
    dot_general x28 -> x0, matrix products: 81.6 us -> none  [the longest x3 25.9 us: back_product(): lax.dot_general(left, right, (((1,), (1,)), ((), ())), preferred_element_...]
    unnamed x13 -> x0, waiting for transfers between devices: 48.5 us -> none
    psum x2 -> x0, blocking collectives: 35.5 us -> none  [the longest x1 17.8 us: local(): inner = lax.psum(jnp.sum(gained * stream, axis=1, keepdims=True), 'tensor')]
    select_n x32 -> x0, other arithmetic: 32.3 us -> none  [hop(): return jax.tree.map(lambda a, b: jnp.where(reached, a, b), new, before)]
    all_gather x1 -> x0, blocking collectives: 22.2 us -> none  [carried_in(): lax.all_gather(part.astype(kind), axis)]
  transfers between devices with their start and end apart: 12 -> 0, of which waited for: 12 -> 0; matrix products, arithmetic and copies ran while one was open for 3% -> 0% of each run, Pallas kernels for 0% -> 0%
where the time goes in v1:
time: 288 us; the launch traced here: 287 us
  Pallas kernels  276 us (96%)
  local copies, waits for them, and re-layouts  9.02 us (3%)
    pallas_call x1, Pallas kernels, local(): pl.pallas_call(front_kernel, out_shape=(struct((DP, 2, ROWS, HID), BF16),...  148 us
    pallas_call x1, Pallas kernels, local(): pl.pallas_call(middle_kernel, out_shape=struct((T, WIDTH), F32), in_specs...  81.1 us
    pallas_call x1, Pallas kernels, local(): pl.pallas_call(back_kernel, out_shape=(struct((ROWS, 512), F32), struct((...  46.7 us
    unnamed x5, local copies, waits for them, and re-layouts  7.85 us

profile of v1, /device:TPU:1, one launch (start us, length us, event | category | flops | bytes accessed | tf_op | source)
XLA Modules:
  0.0 287.2 jit_solution(5155036739582264408)
XLA Ops:
  0.6 1.3 select_maximum_fusion.params
  1.9 1.3 copy.18
  3.2 1.2 pad.8.w_dt
  4.4 148.5 %front.1 = (bf16[16,2,256,1792]{3,2,1,0:T(8,128)(2,1)}, bf16[16,128,256]{2,1,0:T(8,128)(2,1)}, bf16[128,512]{1,0:T(8,128)(2,1)}, f32[128,1792]{1,0:T(8,128)}, bf...) custom-call(bf16[128,4096]{1,0:T(8,128)(2,1)} %resid.3, ...), custom_call_target="tpu_custom_call" | custom-call | tf_op jit(solution)/shard_map/front/pallas_call | solution.py:727
  152.8 81.1 %middle.1.out_grad = f32[128,512]{1,0:T(8,128)} custom-call(bf16[128,512]{1,0:T(8,128)(2,1)} %get-tuple-element.18.mixer_out, bf16[512,4096]{1,0:T(8,128)(2,1)} %w_out.1, f32[1,4096]{1,0:T(1,128)} %bitcast.8, bf16[128,4096]{1,0:T(8,128)(2,1)} %resid.3, f32[128,1792]{1,0:T(8,128)} %get-tuple-element.19.target, bf16[16,2,256,1792]{3,2,1,0:T(8,128)(2,1)} %get-tuple-element.20.w_all), custom_call_target="tpu_custom_call" | custom-call | tf_op jit(solution)/shard_map/middle/pallas_call | solution.py:772
  233.9 46.7 %back.1 = (f32[256,512]{1,0:T(8,128)}, f32[256,128]{1,0:T(8,128)}, f32[256,128]{1,0:T(8,128)}, f32[256,128]{1,0:T(8,128)}) custom-call(f32[128,512]{1,0:T(8,128)} %middle.1.out_grad, bf16[128,512]{1,0:T(8,128)(2,1)} %get-tuple-element.21.read, bf16[128,128]{1,0:T(8,128)(2,1)} %get-tuple-element.22.inject_in, bf16[128,128]{1,0:T(8,128)(2,1)} %get-tuple-element.23.value_in, ...), custom_call_target="tpu_custom_call" | custom-call | tf_op jit(solution)/shard_map/back/pallas_call | solution.py:800
  280.6 1.6 copy.19
  282.2 1.9 copy.23
  284.1 1.6 copy.24
  285.6 1.6 copy.25

commit v2 on v0

v2 whole, which is shorter than its diff:
```python
import math
from types import SimpleNamespace

import jax
import jax.numpy as jnp
from jax import lax
from jax.experimental import pallas as pl
from jax.experimental.pallas import tpu as pltpu
from jax.sharding import PartitionSpec as P

D = 4096
FF = 14336
EPS = 1e-05
T = 128
HEADS = 4
DP = 16
TP = 8
HID = 1792
ROWS = 256
WIDTH = 512
PACK = 896
F32 = jnp.float32
BF16 = jnp.bfloat16
MESH = pl.DeviceIdType.MESH
MIB = 1024 * 1024

LEGS = {
    "RO": ("R", 0, 0, "full", 0, -1),
    "LO": ("L", 0, 0, "full", 0, 1),
    "YO": ("Y", 0, 0, "full", 1, 0),
    "RQ": ("R", 1, 0, "Q", 1, -1),
    "LQ": ("L", 1, 0, "Q", 1, 1),
    "RA": ("R", 0, -1, "A", 0, 2),
    "LB": ("L", 0, 1, "B", 0, 2),
    "YL": ("Y", 0, -1, "P", 1, -1),
    "YR": ("Y", 0, 1, "P", 1, 1),
    "RQA": ("R", 1, -1, "QA", 1, 2),
    "LQB": ("L", 1, 1, "QB", 1, 2),
    "YO2": ("Y", 0, 2, "P", 1, 2),
}
ORDER = list(LEGS)
NSEM = 2 * len(ORDER) + 1


def place():
    me = lax.axis_index("dp")
    return me, me // 8, (me % 8) // 2, me % 2


class Gather:
    def __init__(self, piece, rows, p, qa, send, recv):
        self.piece, self.send, self.recv = piece, send, recv
        self.me, self.y, self.z, self.c = place()
        half = rows // 2
        self.rows = {
            "full": (0, rows),
            "P": (0, p),
            "Q": (p, rows - p),
            "A": (0, half),
            "B": (half, rows - half),
            "QA": (p, qa),
            "QB": (p + qa, rows - p - qa),
        }

    def block(self, flip, dz, core):
        y = (1 - self.y) if flip else self.y
        return y * 8 + ((self.z + dz + 4) % 4) * 2 + core

    def target(self, name):
        if name == "R":
            return self.block(0, 1, self.c)
        if name == "L":
            return self.block(0, -1, self.c)
        if name == "Y":
            return self.block(1, 0, self.c)
        return self.block(0, 0, 1 - self.c)

    def copy(self, ref, sem, to):
        return pltpu.make_async_remote_copy(
            src_ref=ref,
            dst_ref=ref,
            send_sem=self.send.at[sem],
            recv_sem=self.recv.at[sem],
            device_id={"dp": to},
            device_id_type=MESH,
        )

    def leg(self, name):
        to, flip, dz, rows, _, _ = LEGS[name]
        ref = self.piece(self.block(flip, dz, self.c), *self.rows[rows])
        return self.copy(ref, ORDER.index(name), self.target(to))

    def landed(self, name):
        to, _, _, rows, flip, dz = LEGS[name]
        ref = self.piece(self.block(flip, dz, self.c), *self.rows[rows])
        return self.copy(ref, ORDER.index(name), self.target(to))

    def side(self, name, core):
        if name == "own":
            flip, dz, rows, sem = 0, 0, "full", len(ORDER)
        else:
            _, _, _, rows, flip, dz = LEGS[name]
            sem = len(ORDER) + 1 + ORDER.index(name)
        ref = self.piece(self.block(flip, dz, core), *self.rows[rows])
        return self.copy(ref, sem, self.target("S"))

    def begin(self):
        for name in ("RO", "LO", "YO"):
            self.leg(name).start()
        self.side("own", self.c).start()

    def arrive(self, name, *then):
        self.landed(name).wait_recv()
        for other in then:
            self.leg(other).start()
        self.side(name, self.c).start()

    def side_arrive(self, *names):
        for name in names:
            self.side(name, 1 - self.c).wait_recv()

    def finish(self):
        for name in ORDER:
            self.leg(name).wait_send()
        for name in ["own"] + ORDER:
            self.side(name, self.c).wait_send()


def iota(axis):
    return lax.broadcasted_iota(jnp.int32, (T, T), axis)


def mm(a, b):
    return jnp.dot(a.astype(BF16), b.astype(BF16), preferred_element_type=F32)


def mm_t(a, b):
    return lax.dot_general(
        a.astype(BF16), b.astype(BF16), (((1,), (1,)), ((), ())), preferred_element_type=F32
    )


def softplus(v):
    return jnp.maximum(v, 0.0) + jnp.log1p(jnp.exp(-jnp.abs(v)))


def steps_of(raw, params):
    step = softplus(raw + params[0:1, :])
    lower = (iota(0) >= iota(1)).astype(F32)
    decay = jnp.dot(
        lower, -step * params[1:2, :], preferred_element_type=F32, precision=lax.Precision.HIGHEST
    )
    return step, decay, jnp.transpose(step), jnp.transpose(decay)


def head(k):
    return slice(k * 128, (k + 1) * 128)


class States:
    def __init__(self, slots, sums, send, recv):
        self.slots, self.sums, self.send, self.recv = slots, sums, send, recv
        self.me, self.y, self.z, self.c = place()
        self.m = self.me % 8

    def peer(self, k):
        at = (self.m + k) % 8
        return pltpu.make_async_remote_copy(
            src_ref=self.slots.at[self.m],
            dst_ref=self.slots.at[self.m],
            send_sem=self.send.at[k - 1],
            recv_sem=self.recv.at[k - 1],
            device_id={"dp": self.y * 8 + at},
            device_id_type=MESH,
        )

    def from_peer(self, k):
        at = (self.m - k + 8) % 8
        return pltpu.make_async_remote_copy(
            src_ref=self.slots.at[at],
            dst_ref=self.slots.at[at],
            send_sem=self.send.at[k - 1],
            recv_sem=self.recv.at[k - 1],
            device_id={"dp": self.y * 8 + at},
            device_id_type=MESH,
        )

    def across(self):
        return pltpu.make_async_remote_copy(
            src_ref=self.sums.at[0],
            dst_ref=self.sums.at[1],
            send_sem=self.send.at[7],
            recv_sem=self.recv.at[7],
            device_id={"dp": (1 - self.y) * 8 + self.m},
            device_id_type=MESH,
        )

    def begin(self):
        for k in range(1, 8):
            self.peer(k).start()

    def gathered(self):
        for k in range(1, 8):
            self.from_peer(k).wait_recv()

    def finish(self):
        for k in range(1, 8):
            self.peer(k).wait_send()
        self.across().wait_send()


def spread(scalars):
    lane = lax.broadcasted_iota(jnp.int32, (1, 128), 1)
    row = jnp.zeros((1, 128), F32)
    for h in range(HEADS):
        row = jnp.where(lane == h, scalars[h], row)
    return row


SCRATCH = {
    "held": pltpu.VMEM((DP, 2, ROWS, HID), BF16),
    "v_wc": pltpu.VMEM((D, 512), BF16),
    "v_wb": pltpu.VMEM((D, 128), BF16),
    "v_wx": pltpu.VMEM((D, 128), BF16),
    "v_wdt": pltpu.VMEM((HEADS, D), BF16),
    "v_out": pltpu.VMEM((512, D), BF16),
    "v_resid": pltpu.VMEM((T, WIDTH), BF16),
    "nin": pltpu.VMEM((T, D), BF16),
    "nin_t": pltpu.VMEM((DP, 256, T), BF16),
    "cols": pltpu.VMEM((DP, 256, T), BF16),
    "lhs": pltpu.VMEM((2 * T, D), BF16),
    "acc": pltpu.VMEM((2, 2 * T, HID), F32),
    "proj": pltpu.VMEM((T, PACK), F32),
    "read": pltpu.VMEM((T, WIDTH), BF16),
    "state": pltpu.VMEM((8, 128, WIDTH), BF16),
    "sums": pltpu.VMEM((2, 128, WIDTH), BF16),
    "decays": pltpu.VMEM((8, 8, 128), F32),
    "enter": pltpu.VMEM((128, WIDTH), BF16),
    "through": pltpu.VMEM((T, WIDTH), F32),
    "mixer_out": pltpu.VMEM((T, WIDTH), BF16),
    "fade": pltpu.VMEM((HEADS, T, T), F32),
    "plain": pltpu.VMEM((HEADS, T, T), F32),
    "p_send": pltpu.VMEM((TP - 1, T, WIDTH), BF16),
    "p_recv": pltpu.VMEM((TP - 1, T, WIDTH), BF16),
    "strm": pltpu.VMEM((TP, T, WIDTH), BF16),
    "gained": pltpu.VMEM((TP, T, WIDTH), BF16),
    "g_gate": pltpu.VMEM((T, HID), BF16),
    "g_up": pltpu.VMEM((T, HID), BF16),
    "out_grad": pltpu.VMEM((T, WIDTH), F32),
    "b_state": pltpu.VMEM((8, 128, WIDTH), BF16),
    "b_sums": pltpu.VMEM((2, 128, WIDTH), BF16),
    "packed": pltpu.VMEM((DP, T, PACK), BF16),
    "dread": pltpu.VMEM((T, WIDTH), F32),
    "dinject": pltpu.VMEM((T, 128), F32),
    "dvalue": pltpu.VMEM((T, 128), F32),
    "in_sem": pltpu.SemaphoreType.DMA((10,)),
    "g_send": pltpu.SemaphoreType.DMA((NSEM,)),
    "g_recv": pltpu.SemaphoreType.DMA((NSEM,)),
    "h_send": pltpu.SemaphoreType.DMA((NSEM,)),
    "h_recv": pltpu.SemaphoreType.DMA((NSEM,)),
    "s_send": pltpu.SemaphoreType.DMA((8,)),
    "s_recv": pltpu.SemaphoreType.DMA((8,)),
    "d_send": pltpu.SemaphoreType.DMA((8,)),
    "d_recv": pltpu.SemaphoreType.DMA((8,)),
    "b_send": pltpu.SemaphoreType.DMA((8,)),
    "b_recv": pltpu.SemaphoreType.DMA((8,)),
    "c_send": pltpu.SemaphoreType.DMA((DP - 1,)),
    "c_recv": pltpu.SemaphoreType.DMA((DP - 1,)),
    "t_send": pltpu.SemaphoreType.DMA((4, TP - 1)),
    "t_recv": pltpu.SemaphoreType.DMA((4, TP - 1)),
}


def chunk(k, size=256):
    return pl.ds(pl.multiple_of(k * size, size), size)


def columns(p):
    return chunk(p, WIDTH)


def normalise(ref, rows, gain):
    def square(k, total):
        part = ref[rows, chunk(k)].astype(F32)
        return total + jnp.sum(part * part, axis=1, keepdims=True)

    scale = lax.rsqrt(lax.fori_loop(0, 16, square, jnp.zeros((T, 1), F32)) / D + EPS)

    def write(k, _):
        ref[rows, chunk(k)] = (ref[rows, chunk(k)].astype(F32) * scale * gain[:, chunk(k)]).astype(BF16)
        return 0

    lax.fori_loop(0, 16, write, 0)


def state_weights(decays, m, forward):
    run_in, run_all = jnp.zeros((1, 128), F32), jnp.zeros((1, 128), F32)
    inside, whole = [None] * 8, [None] * 8
    for j in reversed(range(8)) if forward else range(8):
        reached = ((j < m) if forward else (j > m)).astype(F32)
        inside[j] = reached * jnp.exp(run_in)
        whole[j] = jnp.exp(run_all)
        end = decays[j, 0:1, :]
        run_in = run_in + reached * end
        run_all = run_all + end
    return inside, whole, jnp.exp(run_in)


def combine(state, weights, h):
    total = jnp.zeros((128, 128), F32)
    for j in range(8):
        total = total + weights[j][:, h : h + 1] * state[j, :, head(h)].astype(F32)
    return total


def whole_kernel(
    resid, teacher, gain_mix, gain_mlp, w_c, w_b, w_x, w_dt, bias, rate, skip, w_out, w_gate, w_up, out, *scratch
):
    s = SimpleNamespace(**dict(zip(SCRATCH, scratch)))
    me, y, z, c = place()
    m = me % 8
    t = lax.axis_index("tensor")
    top, low = pl.ds(0, T), pl.ds(T, T)
    pairs = (
        (w_gate, s.held.at[me, 0]),
        (w_up, s.held.at[me, 1]),
        (resid, s.nin),
        (w_c, s.v_wc),
        (w_b, s.v_wb),
        (w_x, s.v_wx),
        (w_dt, s.v_wdt),
        (teacher, s.lhs.at[top, :]),
        (w_out, s.v_out),
        (resid.at[:, columns(t)], s.v_resid),
    )
    loads = [pltpu.make_async_copy(a, b, s.in_sem.at[k]) for k, (a, b) in enumerate(pairs)]
    for copy in loads:
        copy.start()
    sem = pltpu.get_barrier_semaphore()
    for k in range(1, DP):
        pl.semaphore_signal(sem, inc=1, device_id={"dp": (me + k) % DP}, device_id_type=MESH)
    for k in range(1, TP):
        pl.semaphore_signal(sem, inc=1, device_id={"tensor": (t + k) % TP}, device_id_type=MESH)
    pl.semaphore_wait(sem, DP + TP - 2)
    loads[0].wait()
    loads[1].wait()
    gather = Gather(
        lambda j, start, size: s.held.at[j, :, pl.ds(start, size), :], ROWS, 112, 64, s.g_send, s.g_recv
    )
    gather.begin()

    bias_row, rate_row, skip_row = spread(bias), spread(rate), spread(skip)
    params = jnp.concatenate([bias_row, rate_row, skip_row, jnp.zeros((5, 128), F32)], axis=0)
    loads[2].wait()
    normalise(s.nin, slice(None), gain_mix)
    for copy in loads[3:7]:
        copy.wait()
    s.proj[...] = jnp.zeros_like(s.proj)

    def project(k, _):
        rows = s.nin[:, chunk(k)]
        s.proj[:, 0:512] += jnp.dot(rows, s.v_wc[chunk(k), :], preferred_element_type=F32)
        s.proj[:, 512:640] += jnp.dot(rows, s.v_wb[chunk(k), :], preferred_element_type=F32)
        s.proj[:, 640:768] += jnp.dot(rows, s.v_wx[chunk(k), :], preferred_element_type=F32)
        s.proj[:, 768 : 768 + HEADS] += mm_t(rows, s.v_wdt[:, chunk(k)])
        return 0

    lax.fori_loop(0, 16, project, 0)
    s.read[...] = s.proj[:, 0:512].astype(BF16)
    inject, values = s.proj[:, 512:640], s.proj[:, 640:768]
    raw = s.proj[:, 768:896]
    step, decay, step_t, decay_t = steps_of(raw, params)
    causal = iota(0) >= iota(1)
    inject_t = jnp.transpose(inject)
    for h in range(HEADS):
        row, col, step_row = decay_t[h : h + 1, :], decay[:, h : h + 1], step_t[h : h + 1, :]
        last = row[:, T - 1 : T]
        s.fade[h] = jnp.exp(jnp.where(causal, col - row, -1e30))
        s.plain[h] = s.fade[h] * mm_t(s.read[:, head(h)], inject)
        s.through[:, head(h)] = mm(s.plain[h] * step_row, values) + skip_row[:, h : h + 1] * values
        s.state[m, :, head(h)] = mm(inject_t * (jnp.exp(last - row) * step_row), values).astype(BF16)
    s.decays[m] = jnp.broadcast_to(decay[T - 1 : T, :], (8, 128))
    states = States(s.state, s.sums, s.s_send, s.s_recv)
    ends = States(s.decays, None, s.d_send, s.d_recv)
    ends.begin()
    states.begin()

    loads[7].wait()
    normalise(s.lhs, top, gain_mlp)

    def turn(k, _):
        s.nin_t[k] = jnp.transpose(s.nin[:, chunk(k)].astype(F32)).astype(BF16)
        return 0

    lax.fori_loop(0, DP, turn, 0)
    s.acc[...] = jnp.zeros_like(s.acc)
    ends.gathered()
    states.gathered()
    inside, whole, lead = state_weights(s.decays, m, True)
    for h in range(HEADS):
        s.sums[0, :, head(h)] = combine(s.state, whole, h).astype(BF16)
    states.across().start()
    states.across().wait_recv()
    after = (y == 1).astype(F32)
    for h in range(HEADS):
        total = combine(s.state, inside, h)
        total = total + (after * lead[:, h : h + 1]) * s.sums[1, :, head(h)].astype(F32)
        entering = total.astype(BF16)
        s.enter[:, head(h)] = entering
        grown = jnp.exp(decay[:, h : h + 1]) * mm(s.read[:, head(h)], entering)
        s.mixer_out[:, head(h)] = (s.through[:, head(h)] + grown).astype(BF16)

    def move(phase, k, src, dst):
        return pltpu.make_async_remote_copy(
            src_ref=src,
            dst_ref=dst,
            send_sem=s.t_send.at[phase, k - 1],
            recv_sem=s.t_recv.at[phase, k - 1],
            device_id={"tensor": (t + k) % TP},
            device_id_type=MESH,
        )

    def part_move(phase, k):
        return move(phase, k, s.p_send.at[k - 1], s.p_recv.at[k - 1])

    def out_part(p):
        return jnp.dot(s.mixer_out[...], s.v_out[:, columns(p)], preferred_element_type=F32)

    loads[8].wait()
    loads[9].wait()

    def out_send(k, _):
        s.p_send[k - 1] = out_part((t + k) % TP).astype(BF16)
        part_move(0, k).start()
        return 0

    lax.fori_loop(1, TP, out_send, 0)
    stream = out_part(t) + s.v_resid[...].astype(F32)
    gather.arrive("YO", "RQ", "LQ")
    gather.arrive("RO", "RA", "YL")
    gather.arrive("LO", "LB", "YR")
    for k in range(1, TP):
        part_move(0, k).wait_recv()
        stream = stream + s.p_recv[k - 1].astype(F32)
    s.strm[t] = stream.astype(BF16)
    for k in range(1, TP):
        move(1, k, s.strm.at[t], s.strm.at[t]).start()
    for k in range(1, TP):
        at = (t - k + TP) % TP
        move(1, k, s.strm.at[at], s.strm.at[at]).wait_recv()

    def square(p, total):
        part = s.strm[p].astype(F32)
        return total + jnp.sum(part * part, axis=1, keepdims=True)

    scale = lax.rsqrt(lax.fori_loop(0, TP, square, jnp.zeros((T, 1), F32)) / D + EPS)

    def write(p, _):
        s.lhs[low, columns(p)] = (s.strm[p].astype(F32) * scale * gain_mlp[:, columns(p)]).astype(BF16)
        return 0

    lax.fori_loop(0, TP, write, 0)

    def use(flip, dz):
        base = gather.block(flip, dz, 0)

        def one(n, _):
            at = chunk(n)
            first, second = s.lhs[:, chunk(base)], s.lhs[:, chunk(base + 1)]
            for g in range(2):
                s.acc[g, :, at] += jnp.dot(
                    first, s.held[base, g, :, at], preferred_element_type=F32
                ) + jnp.dot(second, s.held[base + 1, g, :, at], preferred_element_type=F32)
            return 0

        lax.fori_loop(0, HID // 256, one, 0)

    gather.side_arrive("own")
    use(0, 0)
    gather.side_arrive("YO")
    use(1, 0)
    gather.arrive("RQ", "RQA")
    gather.arrive("LQ", "LQB")
    gather.arrive("RA", "YO2")
    gather.arrive("LB")
    gather.side_arrive("RO")
    use(0, -1)
    gather.arrive("YL")
    gather.arrive("YR")
    gather.side_arrive("LO")
    use(0, 1)
    gather.side_arrive("RA", "LB")
    use(0, 2)
    gather.arrive("RQA")
    gather.arrive("LQB")
    gather.arrive("YO2")
    gather.side_arrive("RQ", "YL")
    use(1, -1)
    gather.side_arrive("LQ", "YR")
    use(1, 1)
    gather.side_arrive("RQA", "LQB", "YO2")
    use(1, 2)

    def column_copy(k):
        to = (me + k) % DP
        return pltpu.make_async_remote_copy(
            src_ref=s.nin_t.at[to],
            dst_ref=s.cols.at[me],
            send_sem=s.c_send.at[k - 1],
            recv_sem=s.c_recv.at[k - 1],
            device_id={"dp": to},
            device_id_type=MESH,
        )

    def column_landed(k):
        at = (me - k + DP) % DP
        return pltpu.make_async_remote_copy(
            src_ref=s.nin_t.at[at],
            dst_ref=s.cols.at[at],
            send_sem=s.c_send.at[k - 1],
            recv_sem=s.c_recv.at[k - 1],
            device_id={"dp": at},
            device_id_type=MESH,
        )

    for k in range(1, DP):
        column_copy(k).start()
    s.cols[me] = s.nin_t[me]

    def hidden(n, _):
        at = chunk(n)
        aim_gate = s.acc[0, top, at]
        aim = aim_gate * jax.nn.sigmoid(aim_gate) * s.acc[1, top, at]
        gate, up = s.acc[0, low, at], s.acc[1, low, at]
        sigma = jax.nn.sigmoid(gate)
        silu = gate * sigma
        grad = (2.0 / math.sqrt(FF)) * (silu * up - aim)
        s.g_gate[:, at] = (grad * up * sigma * (1.0 + gate * (1.0 - sigma))).astype(BF16)
        s.g_up[:, at] = (grad * silu).astype(BF16)
        return 0

    lax.fori_loop(0, HID // 256, hidden, 0)

    def back(p):
        return jnp.concatenate(
            [
                mm_t(s.g_gate[...], s.held[2 * p + i, 0]) + mm_t(s.g_up[...], s.held[2 * p + i, 1])
                for i in range(2)
            ],
            axis=1,
        )

    for k in range(1, TP):
        part_move(0, k).wait_send()

    def back_send(k, _):
        s.p_send[k - 1] = back((t + k) % TP).astype(BF16)
        part_move(2, k).start()
        return 0

    lax.fori_loop(1, TP, back_send, 0)
    mid = back(t)
    for k in range(1, TP):
        part_move(2, k).wait_recv()
        mid = mid + s.p_recv[k - 1].astype(F32)
    s.gained[t] = (mid * gain_mlp[:, columns(t)]).astype(BF16)
    for k in range(1, TP):
        move(3, k, s.gained.at[t], s.gained.at[t]).start()
    for k in range(1, TP):
        at = (t - k + TP) % TP
        move(3, k, s.gained.at[at], s.gained.at[at]).wait_recv()

    def product(p, total):
        return total + jnp.sum(s.gained[p].astype(F32) * s.strm[p].astype(F32), axis=1, keepdims=True)

    inner = lax.fori_loop(0, TP, product, jnp.zeros((T, 1), F32))
    pull = scale * scale * scale * (inner / D)
    s.out_grad[...] = jnp.zeros_like(s.out_grad)

    def unproject(p, _):
        delta = (s.gained[p].astype(F32) * scale - s.strm[p].astype(F32) * pull).astype(BF16)
        s.out_grad[...] += mm_t(delta, s.v_out[:, columns(p)])
        return 0

    lax.fori_loop(0, TP, unproject, 0)

    inject, values = s.proj[:, 512:640], s.proj[:, 640:768]
    raw = s.proj[:, 768:896]
    step, decay, step_t, decay_t = steps_of(raw, params)
    growth, growth_t = jnp.exp(decay), jnp.exp(decay_t)
    for h in range(HEADS):
        read_t = jnp.transpose(s.read[:, head(h)].astype(F32))
        s.b_state[m, :, head(h)] = mm(read_t * growth_t[h : h + 1, :], s.out_grad[:, head(h)]).astype(BF16)
    states_back = States(s.b_state, s.b_sums, s.b_send, s.b_recv)
    states_back.begin()
    lanes = lax.broadcasted_iota(jnp.int32, (1, 128), 1)
    s.dinject[...] = jnp.zeros_like(s.dinject)
    s.dvalue[...] = jnp.zeros_like(s.dvalue)
    step_rows, decay_rows, decay_cols = [], [], []
    for h in range(HEADS):
        step_row = step_t[h : h + 1, :]
        read_h, grad_h = s.read[:, head(h)], s.out_grad[:, head(h)]
        dweight = mm_t(grad_h, values)
        direct = dweight * s.plain[h]
        dscore = dweight * s.fade[h] * step_row
        weight = s.plain[h] * step_row
        through = mm_t(grad_h, s.enter[:, head(h)])
        s.dread[:, head(h)] = mm(dscore, inject) + growth[:, h : h + 1] * through
        s.dinject[...] += mm(jnp.transpose(dscore), read_h)
        s.dvalue[...] += mm(jnp.transpose(weight), grad_h) + skip_row[:, h : h + 1] * grad_h
        column = jnp.sum(direct, axis=0, keepdims=True)
        step_rows.append(column)
        decay_rows.append(-column * step_row)
        along = growth[:, h : h + 1] * jnp.sum(through * read_h.astype(F32), axis=1, keepdims=True)
        decay_cols.append(jnp.sum(direct * step_row, axis=1, keepdims=True) + along)
    states_back.gathered()
    inside, whole, lead = state_weights(s.decays, m, False)
    for h in range(HEADS):
        s.b_sums[0, :, head(h)] = combine(s.b_state, whole, h).astype(BF16)
    states_back.across().start()
    states_back.across().wait_recv()
    before = (y == 0).astype(F32)
    dstep = jnp.zeros((T, 128), F32)
    ddecay = jnp.zeros((T, 128), F32)
    for h in range(HEADS):
        behind = combine(s.b_state, inside, h)
        behind = behind + (before * lead[:, h : h + 1]) * s.b_sums[1, :, head(h)].astype(F32)
        tail_col = jnp.exp(decay[T - 1 : T, h : h + 1] - decay[:, h : h + 1])
        scaled_col = tail_col * step[:, h : h + 1]
        pulled = mm_t(values, behind)
        s.dinject[...] += scaled_col * pulled
        s.dvalue[...] += scaled_col * mm(inject, behind)
        drawn = tail_col * jnp.sum(inject * pulled, axis=1, keepdims=True)
        moved = drawn * step[:, h : h + 1]
        kept = jnp.exp(decay[T - 1 : T, h : h + 1]) * jnp.sum(
            jnp.sum(behind * s.enter[:, head(h)].astype(F32), axis=1, keepdims=True), axis=0, keepdims=True
        )
        end = kept + jnp.sum(moved, axis=0, keepdims=True)
        onehot = (lanes == h).astype(F32)
        final = (lax.broadcasted_iota(jnp.int32, (T, 1), 0) == T - 1).astype(F32)
        dstep = dstep + drawn * onehot
        ddecay = ddecay + (decay_cols[h] - moved + final * end) * onehot
    zero = jnp.zeros((128 - HEADS, 128), F32)
    dstep = dstep + jnp.transpose(jnp.concatenate(step_rows + [zero], axis=0))
    ddecay = ddecay + jnp.transpose(jnp.concatenate(decay_rows + [zero], axis=0))
    upper = (iota(0) <= iota(1)).astype(F32)
    later = jnp.dot(upper, ddecay, preferred_element_type=F32, precision=lax.Precision.HIGHEST)
    draw = (dstep - rate_row * later) * jax.nn.sigmoid(raw + bias_row)
    s.packed[me, :, 0:512] = s.dread[...].astype(BF16)
    s.packed[me, :, 512:640] = s.dinject[...].astype(BF16)
    s.packed[me, :, 640:768] = s.dvalue[...].astype(BF16)
    s.packed[me, :, 768:896] = draw.astype(BF16)

    last = Gather(lambda j, start, size: s.packed.at[j, pl.ds(start, size), :], T, 48, 48, s.h_send, s.h_recv)
    last.begin()
    out[...] = jnp.zeros_like(out)
    for k in range(1, DP):
        column_landed(k).wait_recv()

    def add(flip, dz):
        base = last.block(flip, dz, 0)
        out[...] += jnp.dot(s.cols[base], s.packed[base], preferred_element_type=F32) + jnp.dot(
            s.cols[base + 1], s.packed[base + 1], preferred_element_type=F32
        )

    last.arrive("YO", "RQ", "LQ")
    last.arrive("RO", "RA", "YL")
    last.arrive("LO", "LB", "YR")
    last.side_arrive("own")
    add(0, 0)
    last.side_arrive("YO")
    add(1, 0)
    last.arrive("RQ", "RQA")
    last.arrive("LQ", "LQB")
    last.arrive("RA", "YO2")
    last.arrive("LB")
    last.arrive("YL")
    last.arrive("YR")
    last.side_arrive("RO")
    add(0, -1)
    last.side_arrive("LO")
    add(0, 1)
    last.arrive("RQA")
    last.arrive("LQB")
    last.arrive("YO2")
    last.side_arrive("RA", "LB")
    add(0, 2)
    last.side_arrive("RQ", "YL")
    add(1, -1)
    last.side_arrive("LQ", "YR")
    add(1, 1)
    last.side_arrive("RQA", "LQB", "YO2")
    add(1, 2)

    gather.finish()
    last.finish()
    states.finish()
    states_back.finish()
    for k in range(1, 8):
        ends.peer(k).wait_send()
    for k in range(1, DP):
        column_copy(k).wait_send()
    for k in range(1, TP):
        move(1, k, s.strm.at[t], s.strm.at[t]).wait_send()
        part_move(2, k).wait_send()
        move(3, k, s.gained.at[t], s.gained.at[t]).wait_send()


def split_kernel(packed, grad_c, grad_b, grad_x, grad_dt):
    grad_c[...] = packed[:, 0:512]
    grad_b[...] = packed[:, 512:640]
    grad_x[...] = packed[:, 640:768]
    grad_dt[...] = packed[:, 768 : 768 + HEADS]


VM = pl.BlockSpec(memory_space=pltpu.VMEM)
SM = pl.BlockSpec(memory_space=pltpu.SMEM)
ANY = pl.BlockSpec(memory_space=pl.ANY)


def struct(shape, dtype):
    return jax.ShapeDtypeStruct(shape, dtype)


def local(
    resid, teacher_mixed, gain_mix, gain_mlp, w_c, w_b, w_x, w_dt, dt_bias, decay_rate, skip, w_out,
    w_gate, w_up,
):
    gain_mix, gain_mlp = gain_mix.reshape(1, D), gain_mlp.reshape(1, D)
    packed = pl.pallas_call(
        whole_kernel,
        out_shape=struct((ROWS, PACK), F32),
        in_specs=[ANY, ANY, VM, VM, ANY, ANY, ANY, ANY, SM, SM, SM, ANY, ANY, ANY],
        out_specs=VM,
        scratch_shapes=list(SCRATCH.values()),
        compiler_params=pltpu.CompilerParams(
            collective_id=0, has_side_effects=True, vmem_limit_bytes=63 * MIB
        ),
        name="whole",
    )(
        resid, teacher_mixed, gain_mix, gain_mlp, w_c, w_b, w_x, w_dt.T, dt_bias, decay_rate, skip, w_out,
        w_gate, w_up,
    )
    return pl.pallas_call(
        split_kernel,
        out_shape=(
            struct((ROWS, 512), F32),
            struct((ROWS, 128), F32),
            struct((ROWS, 128), F32),
            struct((ROWS, HEADS), F32),
        ),
        in_specs=[VM],
        out_specs=(VM,) * 4,
        name="split",
    )(packed)


def solution(mesh):
    in_specs = (
        P("dp", None),
        P("dp", None),
        P(),
        P(),
        P(None, "tensor"),
        P(None, "tensor"),
        P(None, "tensor"),
        P(None, "tensor"),
        P("tensor"),
        P("tensor"),
        P("tensor"),
        P("tensor", None),
        P("dp", "tensor"),
        P("dp", "tensor"),
    )
    out_specs = (P("dp", "tensor"), P("dp", "tensor"), P("dp", "tensor"), P("dp", "tensor"))
    return jax.shard_map(local, mesh=mesh, in_specs=in_specs, out_specs=out_specs, check_vma=False)
```

time: 905 us -> 244 us (0.27)
  waiting for transfers between devices: 681 us -> 0 us
  Pallas kernels: 0 us -> 242 us
  matrix products: 81.6 us -> 0 us
  other arithmetic: 58.1 us -> 0 us
  blocking collectives: 57.6 us -> 0 us
  between operations: 14.8 us -> 0.65 us
    reduce_scatter x5 -> x0, waiting for transfers between devices: 329 us -> none  [the longest x1 70.8 us: local(): lax.psum_scatter((back_product(gate_grad, gate_full) + back_product(up_gr...]
    all_gather x6 -> x0, waiting for transfers between devices: 304 us -> none  [the longest x1 84.1 us: local(): lax.all_gather(w_up, 'dp', axis=0, tiled=True)]
    pallas_call x0 -> x2, Pallas kernels: none -> 242 us  [the longest x1 239 us: local(): pl.pallas_call(whole_kernel, out_shape=struct((ROWS, PACK), F32), in_spec...]
    dot_general x28 -> x0, matrix products: 81.6 us -> none  [the longest x3 25.9 us: back_product(): lax.dot_general(left, right, (((1,), (1,)), ((), ())), preferred_element_...]
    unnamed x13 -> x0, waiting for transfers between devices: 48.5 us -> none
    psum x2 -> x0, blocking collectives: 35.5 us -> none  [the longest x1 17.8 us: local(): inner = lax.psum(jnp.sum(gained * stream, axis=1, keepdims=True), 'tensor')]
    select_n x32 -> x0, other arithmetic: 32.3 us -> none  [hop(): return jax.tree.map(lambda a, b: jnp.where(reached, a, b), new, before)]
    all_gather x1 -> x0, blocking collectives: 22.2 us -> none  [carried_in(): lax.all_gather(part.astype(kind), axis)]
  transfers between devices with their start and end apart: 12 -> 0, of which waited for: 12 -> 0; matrix products, arithmetic and copies ran while one was open for 3% -> 0% of each run, Pallas kernels for 0% -> 0%
where the time goes in v2:
time: 244 us
  Pallas kernels  242 us (99%)
    pallas_call x1, Pallas kernels, local(): pl.pallas_call(whole_kernel, out_shape=struct((ROWS, PACK), F32), in_spec...  239 us

profile of v2, /device:TPU:1, one launch (start us, length us, event | category | flops | bytes accessed | tf_op | source)
XLA Modules:
  0.0 243.8 jit_solution(9472016003878608613)
XLA Ops:
  0.6 239.5 %whole.1.packed = f32[256,896]{1,0:T(8,128)} custom-call(bf16[128,4096]{1,0:T(8,128)(2,1)} %resid.1, bf16[128,4096]{1,0:T(8,128)(2,1)} %teacher.1, f32[1,4096]{1,0:T(1,128)} %bitcast.4, f32[1,4096]{1,0:T(1,128)} %bitcast.5, bf16[4096,512]{1,0:T(8,128)(2,1)} %w_c.1, bf16[4096,128]{1,0:T(8,128)(2,1)} %w_b.1, bf16[4096,128]{1,0:T(8,128)(2,1)} %w_x.1, ...), custom_call_target="tpu_custom_call" | custom-call | tf_op jit(solution)/shard_map/whole/pallas_call | solution.py:730
  240.1 2.1 split.1
  242.2 1.6 copy.18

commit v3 on v2

--- a/solution.py
+++ b/solution.py
@@ -38,8 +38,24 @@
     "LQB": ("L", 1, 1, "QB", 1, 2),
     "YO2": ("Y", 0, 2, "P", 1, 2),
 }
-ORDER = list(LEGS)
-NSEM = 2 * len(ORDER) + 1
+HALVES = {
+    "RO1": ("R", 0, 0, "A", 0, -1),
+    "RO2": ("R", 0, 0, "B", 0, -1),
+    "LO1": ("L", 0, 0, "A", 0, 1),
+    "LO2": ("L", 0, 0, "B", 0, 1),
+    "YO1": ("Y", 0, 0, "A", 1, 0),
+    "YO2": ("Y", 0, 0, "B", 1, 0),
+    "RX1": ("R", 1, 0, "A", 1, -1),
+    "RX2": ("R", 1, 0, "B", 1, -1),
+    "LX1": ("L", 1, 0, "A", 1, 1),
+    "LX2": ("L", 1, 0, "B", 1, 1),
+    "RA": ("R", 0, -1, "A", 0, 2),
+    "LB": ("L", 0, 1, "B", 0, 2),
+    "RXA": ("R", 1, -1, "A", 1, 2),
+    "LXB": ("L", 1, 1, "B", 1, 2),
+}
+NSEM = 2 * len(LEGS) + 1
+NSEM_HALF = 2 * len(HALVES) + 1
 
 
 def place():
@@ -48,8 +64,9 @@
 
 
 class Gather:
-    def __init__(self, piece, rows, p, qa, send, recv):
-        self.piece, self.send, self.recv = piece, send, recv
+    def __init__(self, legs, piece, rows, p, qa, send, recv, give=None):
+        self.legs, self.order = legs, list(legs)
+        self.piece, self.send, self.recv, self.give = piece, send, recv, give
         self.me, self.y, self.z, self.c = place()
         half = rows // 2
         self.rows = {
@@ -75,9 +92,9 @@
             return self.block(1, 0, self.c)
         return self.block(0, 0, 1 - self.c)
 
-    def copy(self, ref, sem, to):
+    def copy(self, src, ref, sem, to):
         return pltpu.make_async_remote_copy(
-            src_ref=ref,
+            src_ref=src,
             dst_ref=ref,
             send_sem=self.send.at[sem],
             recv_sem=self.recv.at[sem],
@@ -86,26 +103,29 @@
         )
 
     def leg(self, name):
-        to, flip, dz, rows, _, _ = LEGS[name]
+        to, flip, dz, rows, _, _ = self.legs[name]
         ref = self.piece(self.block(flip, dz, self.c), *self.rows[rows])
-        return self.copy(ref, ORDER.index(name), self.target(to))
+        src = ref
+        if to == "Y" and self.give is not None:
+            src = self.give(*self.rows[rows])
+        return self.copy(src, ref, self.order.index(name), self.target(to))
 
     def landed(self, name):
-        to, _, _, rows, flip, dz = LEGS[name]
+        to, _, _, rows, flip, dz = self.legs[name]
         ref = self.piece(self.block(flip, dz, self.c), *self.rows[rows])
-        return self.copy(ref, ORDER.index(name), self.target(to))
+        return self.copy(ref, ref, self.order.index(name), self.target(to))
 
     def side(self, name, core):
         if name == "own":
-            flip, dz, rows, sem = 0, 0, "full", len(ORDER)
+            flip, dz, rows, sem = 0, 0, "full", len(self.order)
         else:
-            _, _, _, rows, flip, dz = LEGS[name]
-            sem = len(ORDER) + 1 + ORDER.index(name)
+            _, _, _, rows, flip, dz = self.legs[name]
+            sem = len(self.order) + 1 + self.order.index(name)
         ref = self.piece(self.block(flip, dz, core), *self.rows[rows])
-        return self.copy(ref, sem, self.target("S"))
-
-    def begin(self):
-        for name in ("RO", "LO", "YO"):
+        return self.copy(ref, ref, sem, self.target("S"))
+
+    def begin(self, *names):
+        for name in names:
             self.leg(name).start()
         self.side("own", self.c).start()
 
@@ -120,9 +140,9 @@
             self.side(name, 1 - self.c).wait_recv()
 
     def finish(self):
-        for name in ORDER:
+        for name in self.order:
             self.leg(name).wait_send()
-        for name in ["own"] + ORDER:
+        for name in ["own"] + self.order:
             self.side(name, self.c).wait_send()
 
 
@@ -218,7 +238,8 @@
 
 
 SCRATCH = {
-    "held": pltpu.VMEM((DP, 2, ROWS, HID), BF16),
+    "held": pltpu.VMEM((DP, ROWS, HID), BF16),
+    "give": pltpu.VMEM((ROWS, HID), BF16),
     "v_wc": pltpu.VMEM((D, 512), BF16),
     "v_wb": pltpu.VMEM((D, 128), BF16),
     "v_wx": pltpu.VMEM((D, 128), BF16),
@@ -228,8 +249,8 @@
     "nin": pltpu.VMEM((T, D), BF16),
     "nin_t": pltpu.VMEM((DP, 256, T), BF16),
     "cols": pltpu.VMEM((DP, 256, T), BF16),
-    "lhs": pltpu.VMEM((2 * T, D), BF16),
-    "acc": pltpu.VMEM((2, 2 * T, HID), F32),
+    "lhs": pltpu.VMEM((4 * T, D), BF16),
+    "acc": pltpu.VMEM((4 * T, HID), F32),
     "proj": pltpu.VMEM((T, PACK), F32),
     "read": pltpu.VMEM((T, WIDTH), BF16),
     "state": pltpu.VMEM((8, 128, WIDTH), BF16),
@@ -240,12 +261,11 @@
     "mixer_out": pltpu.VMEM((T, WIDTH), BF16),
     "fade": pltpu.VMEM((HEADS, T, T), F32),
     "plain": pltpu.VMEM((HEADS, T, T), F32),
-    "p_send": pltpu.VMEM((TP - 1, T, WIDTH), BF16),
-    "p_recv": pltpu.VMEM((TP - 1, T, WIDTH), BF16),
-    "strm": pltpu.VMEM((TP, T, WIDTH), BF16),
+    "p_send": pltpu.VMEM((2, TP, T, WIDTH), BF16),
+    "p_recv": pltpu.VMEM((2, TP, T, WIDTH), BF16),
+    "strm": pltpu.VMEM((2, TP, T, WIDTH), BF16),
     "gained": pltpu.VMEM((TP, T, WIDTH), BF16),
-    "g_gate": pltpu.VMEM((T, HID), BF16),
-    "g_up": pltpu.VMEM((T, HID), BF16),
+    "grads": pltpu.VMEM((2 * T, HID), BF16),
     "out_grad": pltpu.VMEM((T, WIDTH), F32),
     "b_state": pltpu.VMEM((8, 128, WIDTH), BF16),
     "b_sums": pltpu.VMEM((2, 128, WIDTH), BF16),
@@ -253,9 +273,11 @@
     "dread": pltpu.VMEM((T, WIDTH), F32),
     "dinject": pltpu.VMEM((T, 128), F32),
     "dvalue": pltpu.VMEM((T, 128), F32),
-    "in_sem": pltpu.SemaphoreType.DMA((10,)),
-    "g_send": pltpu.SemaphoreType.DMA((NSEM,)),
-    "g_recv": pltpu.SemaphoreType.DMA((NSEM,)),
+    "in_sem": pltpu.SemaphoreType.DMA((12,)),
+    "g_send": pltpu.SemaphoreType.DMA((NSEM_HALF,)),
+    "g_recv": pltpu.SemaphoreType.DMA((NSEM_HALF,)),
+    "a_send": pltpu.SemaphoreType.DMA((2,)),
+    "a_recv": pltpu.SemaphoreType.DMA((2,)),
     "h_send": pltpu.SemaphoreType.DMA((NSEM,)),
     "h_recv": pltpu.SemaphoreType.DMA((NSEM,)),
     "s_send": pltpu.SemaphoreType.DMA((8,)),
@@ -266,8 +288,8 @@
     "b_recv": pltpu.SemaphoreType.DMA((8,)),
     "c_send": pltpu.SemaphoreType.DMA((DP - 1,)),
     "c_recv": pltpu.SemaphoreType.DMA((DP - 1,)),
-    "t_send": pltpu.SemaphoreType.DMA((4, TP - 1)),
-    "t_recv": pltpu.SemaphoreType.DMA((4, TP - 1)),
+    "t_send": pltpu.SemaphoreType.DMA((4, DP)),
+    "t_recv": pltpu.SemaphoreType.DMA((4, DP)),
 }
 
 
@@ -320,16 +342,22 @@
     me, y, z, c = place()
     m = me % 8
     t = lax.axis_index("tensor")
-    top, low = pl.ds(0, T), pl.ds(T, T)
+    other = (1 - y) * 8 + m
+    half = HID // 2
+    keep = pl.ds(pl.multiple_of(y * half, 128), half)
+    rest = pl.ds(pl.multiple_of((1 - y) * half, 128), half)
+    mine = pl.ds(pl.multiple_of(y * T, T), T)
     pairs = (
-        (w_gate, s.held.at[me, 0]),
-        (w_up, s.held.at[me, 1]),
+        (w_gate.at[:, keep], s.held.at[me, :, 0:half]),
+        (w_up.at[:, keep], s.held.at[me, :, half:HID]),
+        (w_gate.at[:, rest], s.give.at[:, 0:half]),
+        (w_up.at[:, rest], s.give.at[:, half:HID]),
         (resid, s.nin),
         (w_c, s.v_wc),
         (w_b, s.v_wb),
         (w_x, s.v_wx),
         (w_dt, s.v_wdt),
-        (teacher, s.lhs.at[top, :]),
+        (teacher, s.lhs.at[mine, :]),
         (w_out, s.v_out),
         (resid.at[:, columns(t)], s.v_resid),
     )
@@ -340,20 +368,30 @@
     for k in range(1, DP):
         pl.semaphore_signal(sem, inc=1, device_id={"dp": (me + k) % DP}, device_id_type=MESH)
     for k in range(1, TP):
-        pl.semaphore_signal(sem, inc=1, device_id={"tensor": (t + k) % TP}, device_id_type=MESH)
-    pl.semaphore_wait(sem, DP + TP - 2)
-    loads[0].wait()
-    loads[1].wait()
+        for dp in (me, other):
+            pl.semaphore_signal(
+                sem, inc=1, device_id={"dp": dp, "tensor": (t + k) % TP}, device_id_type=MESH
+            )
+    pl.semaphore_wait(sem, DP - 1 + 2 * (TP - 1))
+    for copy in loads[0:4]:
+        copy.wait()
     gather = Gather(
-        lambda j, start, size: s.held.at[j, :, pl.ds(start, size), :], ROWS, 112, 64, s.g_send, s.g_recv
+        HALVES,
+        lambda j, start, size: s.held.at[j, pl.ds(start, size), :],
+        ROWS,
+        112,
+        64,
+        s.g_send,
+        s.g_recv,
+        lambda start, size: s.give.at[pl.ds(start, size), :],
     )
-    gather.begin()
+    gather.begin("RO1", "LO2", "YO1", "YO2")
 
     bias_row, rate_row, skip_row = spread(bias), spread(rate), spread(skip)
     params = jnp.concatenate([bias_row, rate_row, skip_row, jnp.zeros((5, 128), F32)], axis=0)
-    loads[2].wait()
+    loads[4].wait()
     normalise(s.nin, slice(None), gain_mix)
-    for copy in loads[3:7]:
+    for copy in loads[5:9]:
         copy.wait()
     s.proj[...] = jnp.zeros_like(s.proj)
 
@@ -384,16 +422,39 @@
     ends = States(s.decays, None, s.d_send, s.d_recv)
     ends.begin()
     states.begin()
-
-    loads[7].wait()
-    normalise(s.lhs, top, gain_mlp)
-
-    def turn(k, _):
-        s.nin_t[k] = jnp.transpose(s.nin[:, chunk(k)].astype(F32)).astype(BF16)
-        return 0
-
-    lax.fori_loop(0, DP, turn, 0)
-    s.acc[...] = jnp.zeros_like(s.acc)
+    gather.leg("RO2").start()
+    gather.leg("LO1").start()
+
+    loads[9].wait()
+    normalise(s.lhs, mine, gain_mlp)
+    gather.arrive("RO1", "RA")
+    gather.arrive("LO2", "LB")
+    gather.arrive("YO1", "RX1")
+    gather.arrive("YO2", "LX2", "RX2", "LX1")
+
+    def teacher_move(k):
+        ref = s.lhs.at[pl.ds(pl.multiple_of(y * T + k * (T // 2), T // 2), T // 2), :]
+        return pltpu.make_async_remote_copy(
+            src_ref=ref,
+            dst_ref=ref,
+            send_sem=s.a_send.at[k],
+            recv_sem=s.a_recv.at[k],
+            device_id={"dp": other},
+            device_id_type=MESH,
+        )
+
+    def teacher_landed(k):
+        ref = s.lhs.at[pl.ds(pl.multiple_of((1 - y) * T + k * (T // 2), T // 2), T // 2), :]
+        return pltpu.make_async_remote_copy(
+            src_ref=ref,
+            dst_ref=ref,
+            send_sem=s.a_send.at[k],
+            recv_sem=s.a_recv.at[k],
+            device_id={"dp": other},
+            device_id_type=MESH,
+        )
+
+    teacher_move(0).start()
     ends.gathered()
     states.gathered()
     inside, whole, lead = state_weights(s.decays, m, True)
@@ -410,96 +471,143 @@
         grown = jnp.exp(decay[:, h : h + 1]) * mm(s.read[:, head(h)], entering)
         s.mixer_out[:, head(h)] = (s.through[:, head(h)] + grown).astype(BF16)
 
-    def move(phase, k, src, dst):
+    def move(phase, ky, kt, src, dst):
         return pltpu.make_async_remote_copy(
             src_ref=src,
             dst_ref=dst,
-            send_sem=s.t_send.at[phase, k - 1],
-            recv_sem=s.t_recv.at[phase, k - 1],
-            device_id={"tensor": (t + k) % TP},
+            send_sem=s.t_send.at[phase, ky * TP + kt],
+            recv_sem=s.t_recv.at[phase, ky * TP + kt],
+            device_id={"dp": other if ky else me, "tensor": (t + kt) % TP},
             device_id_type=MESH,
         )
 
-    def part_move(phase, k):
-        return move(phase, k, s.p_send.at[k - 1], s.p_recv.at[k - 1])
+    def out_move(kt):
+        return move(0, 0, kt, s.p_send.at[0, kt], s.p_recv.at[0, kt])
+
+    def stream_move(ky, kt):
+        return move(1, ky, kt, s.strm.at[y, t], s.strm.at[y, t])
+
+    def stream_landed(ky, kt):
+        at = s.strm.at[(1 - y) if ky else y, (t - kt + TP) % TP]
+        return move(1, ky, kt, at, at)
+
+    def mid_move(ky, kt):
+        return move(2, ky, kt, s.p_send.at[(1 - y) if ky else y, kt], s.p_recv.at[ky, kt])
+
+    def gained_move(kt):
+        return move(3, 0, kt, s.gained.at[t], s.gained.at[t])
+
+    def gained_landed(kt):
+        at = s.gained.at[(t - kt + TP) % TP]
+        return move(3, 0, kt, at, at)
+
+    peers = [(ky, kt) for kt in range(TP) for ky in range(2) if ky + kt > 0]
 
     def out_part(p):
         return jnp.dot(s.mixer_out[...], s.v_out[:, columns(p)], preferred_element_type=F32)
 
-    loads[8].wait()
-    loads[9].wait()
+    loads[10].wait()
+    loads[11].wait()
 
     def out_send(k, _):
-        s.p_send[k - 1] = out_part((t + k) % TP).astype(BF16)
-        part_move(0, k).start()
+        s.p_send[0, k] = out_part((t + k) % TP).astype(BF16)
+        out_move(k).start()
         return 0
 
     lax.fori_loop(1, TP, out_send, 0)
+    teacher_move(1).start()
     stream = out_part(t) + s.v_resid[...].astype(F32)
-    gather.arrive("YO", "RQ", "LQ")
-    gather.arrive("RO", "RA", "YL")
-    gather.arrive("LO", "LB", "YR")
+    gather.arrive("RO2")
+    gather.arrive("LO1")
     for k in range(1, TP):
-        part_move(0, k).wait_recv()
-        stream = stream + s.p_recv[k - 1].astype(F32)
-    s.strm[t] = stream.astype(BF16)
-    for k in range(1, TP):
-        move(1, k, s.strm.at[t], s.strm.at[t]).start()
-    for k in range(1, TP):
-        at = (t - k + TP) % TP
-        move(1, k, s.strm.at[at], s.strm.at[at]).wait_recv()
-
-    def square(p, total):
-        part = s.strm[p].astype(F32)
-        return total + jnp.sum(part * part, axis=1, keepdims=True)
-
-    scale = lax.rsqrt(lax.fori_loop(0, TP, square, jnp.zeros((T, 1), F32)) / D + EPS)
-
-    def write(p, _):
-        s.lhs[low, columns(p)] = (s.strm[p].astype(F32) * scale * gain_mlp[:, columns(p)]).astype(BF16)
-        return 0
-
-    lax.fori_loop(0, TP, write, 0)
+        out_move(k).wait_recv()
+        stream = stream + s.p_recv[0, k].astype(F32)
+    s.strm[y, t] = stream.astype(BF16)
+    for ky, kt in peers:
+        stream_move(ky, kt).start()
+
+    upper_rows, lower_rows = pl.ds(0, 2 * T), pl.ds(2 * T, 2 * T)
 
     def use(flip, dz):
         base = gather.block(flip, dz, 0)
 
         def one(n, _):
             at = chunk(n)
-            first, second = s.lhs[:, chunk(base)], s.lhs[:, chunk(base + 1)]
-            for g in range(2):
-                s.acc[g, :, at] += jnp.dot(
-                    first, s.held[base, g, :, at], preferred_element_type=F32
-                ) + jnp.dot(second, s.held[base + 1, g, :, at], preferred_element_type=F32)
+            s.acc[upper_rows, at] += jnp.dot(
+                s.lhs[upper_rows, chunk(base)], s.held[base, :, at], preferred_element_type=F32
+            ) + jnp.dot(
+                s.lhs[upper_rows, chunk(base + 1)], s.held[base + 1, :, at], preferred_element_type=F32
+            )
             return 0
 
         lax.fori_loop(0, HID // 256, one, 0)
 
+    def turn(k, _):
+        s.nin_t[k] = jnp.transpose(s.nin[:, chunk(k)].astype(F32)).astype(BF16)
+        return 0
+
+    lax.fori_loop(0, DP, turn, 0)
+    s.acc[upper_rows, :] = jnp.zeros((2 * T, HID), F32)
+    gather.arrive("RX1", "RXA")
+    gather.arrive("LX2", "LXB")
+    gather.arrive("RA")
+    gather.arrive("LB")
+    teacher_landed(0).wait_recv()
+    teacher_landed(1).wait_recv()
     gather.side_arrive("own")
     use(0, 0)
-    gather.side_arrive("YO")
+    gather.side_arrive("YO1", "YO2")
     use(1, 0)
-    gather.arrive("RQ", "RQA")
-    gather.arrive("LQ", "LQB")
-    gather.arrive("RA", "YO2")
-    gather.arrive("LB")
-    gather.side_arrive("RO")
+    gather.side_arrive("RO1", "RO2")
     use(0, -1)
-    gather.arrive("YL")
-    gather.arrive("YR")
-    gather.side_arrive("LO")
+    gather.side_arrive("LO1", "LO2")
     use(0, 1)
     gather.side_arrive("RA", "LB")
     use(0, 2)
-    gather.arrive("RQA")
-    gather.arrive("LQB")
-    gather.arrive("YO2")
-    gather.side_arrive("RQ", "YL")
+    gather.arrive("RX2")
+    gather.arrive("LX1")
+    gather.side_arrive("RX1", "RX2")
     use(1, -1)
-    gather.side_arrive("LQ", "YR")
+    gather.side_arrive("LX1", "LX2")
     use(1, 1)
-    gather.side_arrive("RQA", "LQB", "YO2")
+    for ky, kt in peers:
+        stream_landed(ky, kt).wait_recv()
+
+    def square(p, totals):
+        parts = [s.strm[yy, p].astype(F32) for yy in range(2)]
+        return tuple(
+            total + jnp.sum(part * part, axis=1, keepdims=True) for total, part in zip(totals, parts)
+        )
+
+    none = jnp.zeros((T, 1), F32)
+    squares = lax.fori_loop(0, TP, square, (none, none))
+    scales = [lax.rsqrt(total / D + EPS) for total in squares]
+    scale = jnp.where(y == 0, scales[0], scales[1])
+
+    def write(p, _):
+        for yy in range(2):
+            s.lhs[pl.ds((2 + yy) * T, T), columns(p)] = (
+                s.strm[yy, p].astype(F32) * scales[yy] * gain_mlp[:, columns(p)]
+            ).astype(BF16)
+        return 0
+
+    lax.fori_loop(0, TP, write, 0)
+    gather.arrive("RXA")
+    gather.arrive("LXB")
+    gather.side_arrive("RXA", "LXB")
     use(1, 2)
+
+    def student(n, _):
+        at = chunk(n)
+        total = jnp.zeros((2 * T, 256), F32)
+        for j in range(DP):
+            total = total + jnp.dot(
+                s.lhs[lower_rows, pl.ds(j * 256, 256)], s.held[j, :, at], preferred_element_type=F32
+            )
+        s.acc[lower_rows, at] = total
+        return 0
+
+    lax.fori_loop(0, HID // 256, student, 0)
 
     def column_copy(k):
         to = (me + k) % DP
@@ -523,62 +631,61 @@
             device_id_type=MESH,
         )
 
+    def hidden(n, _):
+        at, beside = chunk(n, 128), pl.ds(pl.multiple_of(half + n * 128, 128), 128)
+        aim_gate = s.acc[upper_rows, at]
+        aim = aim_gate * jax.nn.sigmoid(aim_gate) * s.acc[upper_rows, beside]
+        gate, up = s.acc[lower_rows, at], s.acc[lower_rows, beside]
+        sigma = jax.nn.sigmoid(gate)
+        silu = gate * sigma
+        grad = (2.0 / math.sqrt(FF)) * (silu * up - aim)
+        s.grads[:, at] = (grad * up * sigma * (1.0 + gate * (1.0 - sigma))).astype(BF16)
+        s.grads[:, beside] = (grad * silu).astype(BF16)
+        return 0
+
+    lax.fori_loop(0, half // 128, hidden, 0)
+
+    for k in range(1, TP):
+        out_move(k).wait_send()
+
+    def back(kt):
+        p = (t + kt) % TP
+        for i in range(2):
+            part = mm_t(s.grads[...], s.held[2 * p + i]).astype(BF16)
+            for yy in range(2):
+                s.p_send[yy, kt, :, i * 256 : (i + 1) * 256] = part[yy * T : (yy + 1) * T, :]
+
+    def back_send(kt, _):
+        back(kt)
+        mid_move(0, kt).start()
+        mid_move(1, kt).start()
+        return 0
+
+    lax.fori_loop(1, TP, back_send, 0)
+    back(0)
+    mid_move(1, 0).start()
     for k in range(1, DP):
         column_copy(k).start()
     s.cols[me] = s.nin_t[me]
-
-    def hidden(n, _):
-        at = chunk(n)
-        aim_gate = s.acc[0, top, at]
-        aim = aim_gate * jax.nn.sigmoid(aim_gate) * s.acc[1, top, at]
-        gate, up = s.acc[0, low, at], s.acc[1, low, at]
-        sigma = jax.nn.sigmoid(gate)
-        silu = gate * sigma
-        grad = (2.0 / math.sqrt(FF)) * (silu * up - aim)
-        s.g_gate[:, at] = (grad * up * sigma * (1.0 + gate * (1.0 - sigma))).astype(BF16)
-        s.g_up[:, at] = (grad * silu).astype(BF16)
-        return 0
-
-    lax.fori_loop(0, HID // 256, hidden, 0)
-
-    def back(p):
-        return jnp.concatenate(
-            [
-                mm_t(s.g_gate[...], s.held[2 * p + i, 0]) + mm_t(s.g_up[...], s.held[2 * p + i, 1])
-                for i in range(2)
-            ],
-            axis=1,
-        )
-
-    for k in range(1, TP):
-        part_move(0, k).wait_send()
-
-    def back_send(k, _):
-        s.p_send[k - 1] = back((t + k) % TP).astype(BF16)
-        part_move(2, k).start()
-        return 0
-
-    lax.fori_loop(1, TP, back_send, 0)
-    mid = back(t)
-    for k in range(1, TP):
-        part_move(2, k).wait_recv()
-        mid = mid + s.p_recv[k - 1].astype(F32)
+    mid = s.p_send[y, 0].astype(F32)
+    for ky, kt in peers:
+        mid_move(ky, kt).wait_recv()
+        mid = mid + s.p_recv[ky, kt].astype(F32)
     s.gained[t] = (mid * gain_mlp[:, columns(t)]).astype(BF16)
     for k in range(1, TP):
-        move(3, k, s.gained.at[t], s.gained.at[t]).start()
+        gained_move(k).start()
     for k in range(1, TP):
-        at = (t - k + TP) % TP
-        move(3, k, s.gained.at[at], s.gained.at[at]).wait_recv()
+        gained_landed(k).wait_recv()
 
     def product(p, total):
-        return total + jnp.sum(s.gained[p].astype(F32) * s.strm[p].astype(F32), axis=1, keepdims=True)
+        return total + jnp.sum(s.gained[p].astype(F32) * s.strm[y, p].astype(F32), axis=1, keepdims=True)
 
     inner = lax.fori_loop(0, TP, product, jnp.zeros((T, 1), F32))
     pull = scale * scale * scale * (inner / D)
     s.out_grad[...] = jnp.zeros_like(s.out_grad)
 
     def unproject(p, _):
-        delta = (s.gained[p].astype(F32) * scale - s.strm[p].astype(F32) * pull).astype(BF16)
+        delta = (s.gained[p].astype(F32) * scale - s.strm[y, p].astype(F32) * pull).astype(BF16)
         s.out_grad[...] += mm_t(delta, s.v_out[:, columns(p)])
         return 0
 
@@ -651,8 +758,10 @@
     s.packed[me, :, 640:768] = s.dvalue[...].astype(BF16)
     s.packed[me, :, 768:896] = draw.astype(BF16)
 
-    last = Gather(lambda j, start, size: s.packed.at[j, pl.ds(start, size), :], T, 48, 48, s.h_send, s.h_recv)
-    last.begin()
+    last = Gather(
+        LEGS, lambda j, start, size: s.packed.at[j, pl.ds(start, size), :], T, 48, 48, s.h_send, s.h_recv
+    )
+    last.begin("RO", "LO", "YO")
     out[...] = jnp.zeros_like(out)
     for k in range(1, DP):
         column_landed(k).wait_recv()
@@ -700,17 +809,20 @@
         ends.peer(k).wait_send()
     for k in range(1, DP):
         column_copy(k).wait_send()
+    for k in range(2):
+        teacher_move(k).wait_send()
+    for ky, kt in peers:
+        stream_move(ky, kt).wait_send()
+        mid_move(ky, kt).wait_send()
     for k in range(1, TP):
-        move(1, k, s.strm.at[t], s.strm.at[t]).wait_send()
-        part_move(2, k).wait_send()
-        move(3, k, s.gained.at[t], s.gained.at[t]).wait_send()
+        gained_move(k).wait_send()
 
 
 def split_kernel(packed, grad_c, grad_b, grad_x, grad_dt):
     grad_c[...] = packed[:, 0:512]
     grad_b[...] = packed[:, 512:640]
     grad_x[...] = packed[:, 640:768]
-    grad_dt[...] = packed[:, 768 : 768 + HEADS]
+    grad_dt[...] = jnp.transpose(packed[:, 768:896])[0:HEADS, :]
 
 
 VM = pl.BlockSpec(memory_space=pltpu.VMEM)
@@ -741,18 +853,19 @@
         resid, teacher_mixed, gain_mix, gain_mlp, w_c, w_b, w_x, w_dt.T, dt_bias, decay_rate, skip, w_out,
         w_gate, w_up,
     )
-    return pl.pallas_call(
+    grad_c, grad_b, grad_x, grad_dt = pl.pallas_call(
         split_kernel,
         out_shape=(
             struct((ROWS, 512), F32),
             struct((ROWS, 128), F32),
             struct((ROWS, 128), F32),
-            struct((ROWS, HEADS), F32),
+            struct((HEADS, ROWS), F32),
         ),
         in_specs=[VM],
         out_specs=(VM,) * 4,
         name="split",
     )(packed)
+    return grad_c, grad_b, grad_x, grad_dt.T
 
 
 def solution(mesh):

time: 244 us -> 216 us (0.89)
  Pallas kernels: 242 us -> 215 us
    pallas_call x1, Pallas kernels: 239 us -> 213 us  [local(): pl.pallas_call(whole_kernel, out_shape=struct((ROWS, PACK), F32), in_spec...]
where the time goes in v3:
time: 216 us; the launch traced here: 215 us
  Pallas kernels  215 us (100%)
    pallas_call x1, Pallas kernels, local(): pl.pallas_call(whole_kernel, out_shape=struct((ROWS, PACK), F32), in_spec...  213 us

profile of v3, /device:TPU:1, one launch (start us, length us, event | category | flops | bytes accessed | tf_op | source)
XLA Modules:
  0.0 215.5 jit_solution(9179453098561802108)
XLA Ops:
  0.6 212.8 %whole.1.packed = f32[256,896]{1,0:T(8,128)} custom-call(bf16[128,4096]{1,0:T(8,128)(2,1)} %resid.1, bf16[128,4096]{1,0:T(8,128)(2,1)} %teacher.1, f32[1,4096]{1,0:T(1,128)} %bitcast.5, f32[1,4096]{1,0:T(1,128)} %bitcast.6, bf16[4096,512]{1,0:T(8,128)(2,1)} %w_c.1, bf16[4096,128]{1,0:T(8,128)(2,1)} %w_b.1, bf16[4096,128]{1,0:T(8,128)(2,1)} %w_x.1, ...), custom_call_target="tpu_custom_call" | custom-call | tf_op jit(solution)/shard_map/whole/pallas_call | solution.py:842
  213.4 2.1 split.1

commit v4 on v3

--- a/solution.py
+++ b/solution.py
@@ -266,7 +266,9 @@
     "strm": pltpu.VMEM((2, TP, T, WIDTH), BF16),
     "gained": pltpu.VMEM((TP, T, WIDTH), BF16),
     "grads": pltpu.VMEM((2 * T, HID), BF16),
+    "squares": pltpu.VMEM((2, T, 128), F32),
     "out_grad": pltpu.VMEM((T, WIDTH), F32),
+    "along": pltpu.VMEM((T, WIDTH), F32),
     "b_state": pltpu.VMEM((8, 128, WIDTH), BF16),
     "b_sums": pltpu.VMEM((2, 128, WIDTH), BF16),
     "packed": pltpu.VMEM((DP, T, PACK), BF16),
@@ -303,16 +305,17 @@
 
 def normalise(ref, rows, gain):
     def square(k, total):
-        part = ref[rows, chunk(k)].astype(F32)
+        part = ref[rows, chunk(k, 512)].astype(F32)
         return total + jnp.sum(part * part, axis=1, keepdims=True)
 
-    scale = lax.rsqrt(lax.fori_loop(0, 16, square, jnp.zeros((T, 1), F32)) / D + EPS)
+    scale = lax.rsqrt(lax.fori_loop(0, 8, square, jnp.zeros((T, 1), F32)) / D + EPS)
 
     def write(k, _):
-        ref[rows, chunk(k)] = (ref[rows, chunk(k)].astype(F32) * scale * gain[:, chunk(k)]).astype(BF16)
+        at = chunk(k, 512)
+        ref[rows, at] = (ref[rows, at].astype(F32) * scale * gain[:, at]).astype(BF16)
         return 0
 
-    lax.fori_loop(0, 16, write, 0)
+    lax.fori_loop(0, 8, write, 0)
 
 
 def state_weights(decays, m, forward):
@@ -372,6 +375,8 @@
             pl.semaphore_signal(
                 sem, inc=1, device_id={"dp": dp, "tensor": (t + k) % TP}, device_id_type=MESH
             )
+    loads[4].wait()
+    normalise(s.nin, slice(None), gain_mix)
     pl.semaphore_wait(sem, DP - 1 + 2 * (TP - 1))
     for copy in loads[0:4]:
         copy.wait()
@@ -389,21 +394,20 @@
 
     bias_row, rate_row, skip_row = spread(bias), spread(rate), spread(skip)
     params = jnp.concatenate([bias_row, rate_row, skip_row, jnp.zeros((5, 128), F32)], axis=0)
-    loads[4].wait()
-    normalise(s.nin, slice(None), gain_mix)
     for copy in loads[5:9]:
         copy.wait()
     s.proj[...] = jnp.zeros_like(s.proj)
 
     def project(k, _):
-        rows = s.nin[:, chunk(k)]
-        s.proj[:, 0:512] += jnp.dot(rows, s.v_wc[chunk(k), :], preferred_element_type=F32)
-        s.proj[:, 512:640] += jnp.dot(rows, s.v_wb[chunk(k), :], preferred_element_type=F32)
-        s.proj[:, 640:768] += jnp.dot(rows, s.v_wx[chunk(k), :], preferred_element_type=F32)
-        s.proj[:, 768 : 768 + HEADS] += mm_t(rows, s.v_wdt[:, chunk(k)])
+        at = chunk(k, 1024)
+        rows = s.nin[:, at]
+        s.proj[:, 0:512] += jnp.dot(rows, s.v_wc[at, :], preferred_element_type=F32)
+        s.proj[:, 512:640] += jnp.dot(rows, s.v_wb[at, :], preferred_element_type=F32)
+        s.proj[:, 640:768] += jnp.dot(rows, s.v_wx[at, :], preferred_element_type=F32)
+        s.proj[:, 768 : 768 + HEADS] += mm_t(rows, s.v_wdt[:, at])
         return 0
 
-    lax.fori_loop(0, 16, project, 0)
+    lax.fori_loop(0, 4, project, 0)
     s.read[...] = s.proj[:, 0:512].astype(BF16)
     inject, values = s.proj[:, 512:640], s.proj[:, 640:768]
     raw = s.proj[:, 768:896]
@@ -439,7 +443,7 @@
             dst_ref=ref,
             send_sem=s.a_send.at[k],
             recv_sem=s.a_recv.at[k],
-            device_id={"dp": other},
+            device_id={"dp": other, "tensor": (t + 4 * k) % TP},
             device_id_type=MESH,
         )
 
@@ -450,11 +454,12 @@
             dst_ref=ref,
             send_sem=s.a_send.at[k],
             recv_sem=s.a_recv.at[k],
-            device_id={"dp": other},
+            device_id={"dp": other, "tensor": (t + 4 * k) % TP},
             device_id_type=MESH,
         )
 
     teacher_move(0).start()
+    teacher_move(1).start()
     ends.gathered()
     states.gathered()
     inside, whole, lead = state_weights(s.decays, m, True)
@@ -515,7 +520,6 @@
         return 0
 
     lax.fori_loop(1, TP, out_send, 0)
-    teacher_move(1).start()
     stream = out_part(t) + s.v_resid[...].astype(F32)
     gather.arrive("RO2")
     gather.arrive("LO1")
@@ -570,44 +574,51 @@
     use(1, -1)
     gather.side_arrive("LX1", "LX2")
     use(1, 1)
-    for ky, kt in peers:
-        stream_landed(ky, kt).wait_recv()
-
-    def square(p, totals):
-        parts = [s.strm[yy, p].astype(F32) for yy in range(2)]
-        return tuple(
-            total + jnp.sum(part * part, axis=1, keepdims=True) for total, part in zip(totals, parts)
-        )
-
-    none = jnp.zeros((T, 1), F32)
-    squares = lax.fori_loop(0, TP, square, (none, none))
-    scales = [lax.rsqrt(total / D + EPS) for total in squares]
-    scale = jnp.where(y == 0, scales[0], scales[1])
-
-    def write(p, _):
+
+    s.acc[lower_rows, :] = jnp.zeros((2 * T, HID), F32)
+    s.squares[...] = jnp.zeros_like(s.squares)
+    late = gather.block(1, 2, 0) // 2
+
+    def student(p):
         for yy in range(2):
-            s.lhs[pl.ds((2 + yy) * T, T), columns(p)] = (
-                s.strm[yy, p].astype(F32) * scales[yy] * gain_mlp[:, columns(p)]
-            ).astype(BF16)
+            part = s.strm[yy, p].astype(F32)
+            s.squares[yy] += jnp.broadcast_to(jnp.sum(part * part, axis=1, keepdims=True), (T, 128))
+            s.lhs[pl.ds((2 + yy) * T, T), columns(p)] = (part * gain_mlp[:, columns(p)]).astype(BF16)
+
+        def one(n, _):
+            at = chunk(n)
+            s.acc[lower_rows, at] += jnp.dot(
+                s.lhs[lower_rows, chunk(2 * p)], s.held[2 * p, :, at], preferred_element_type=F32
+            ) + jnp.dot(
+                s.lhs[lower_rows, chunk(2 * p + 1)], s.held[2 * p + 1, :, at], preferred_element_type=F32
+            )
+            return 0
+
+        lax.fori_loop(0, HID // 256, one, 0)
+
+    def student_early(kt, _):
+        @pl.when(kt > 0)
+        def _():
+            stream_landed(0, kt).wait_recv()
+
+        stream_landed(1, kt).wait_recv()
+        p = (t - kt + TP) % TP
+
+        @pl.when(p != late)
+        def _():
+            student(p)
+
         return 0
 
-    lax.fori_loop(0, TP, write, 0)
+    lax.fori_loop(0, TP, student_early, 0)
     gather.arrive("RXA")
     gather.arrive("LXB")
     gather.side_arrive("RXA", "LXB")
     use(1, 2)
-
-    def student(n, _):
-        at = chunk(n)
-        total = jnp.zeros((2 * T, 256), F32)
-        for j in range(DP):
-            total = total + jnp.dot(
-                s.lhs[lower_rows, pl.ds(j * 256, 256)], s.held[j, :, at], preferred_element_type=F32
-            )
-        s.acc[lower_rows, at] = total
-        return 0
-
-    lax.fori_loop(0, HID // 256, student, 0)
+    student(late)
+    scales = [lax.rsqrt(s.squares[yy, :, 0:1] / D + EPS) for yy in range(2)]
+    scale = jnp.where(y == 0, scales[0], scales[1])
+    both = jnp.concatenate(scales, axis=0)
 
     def column_copy(k):
         to = (me + k) % DP
@@ -635,7 +646,7 @@
         at, beside = chunk(n, 128), pl.ds(pl.multiple_of(half + n * 128, 128), 128)
         aim_gate = s.acc[upper_rows, at]
         aim = aim_gate * jax.nn.sigmoid(aim_gate) * s.acc[upper_rows, beside]
-        gate, up = s.acc[lower_rows, at], s.acc[lower_rows, beside]
+        gate, up = s.acc[lower_rows, at] * both, s.acc[lower_rows, beside] * both
         sigma = jax.nn.sigmoid(gate)
         silu = gate * sigma
         grad = (2.0 / math.sqrt(FF)) * (silu * up - aim)
@@ -667,6 +678,13 @@
     for k in range(1, DP):
         column_copy(k).start()
     s.cols[me] = s.nin_t[me]
+    s.along[...] = jnp.zeros_like(s.along)
+
+    def stream_part(p, _):
+        s.along[...] += mm_t(s.strm[y, p], s.v_out[:, columns(p)])
+        return 0
+
+    lax.fori_loop(0, TP, stream_part, 0)
     mid = s.p_send[y, 0].astype(F32)
     for ky, kt in peers:
         mid_move(ky, kt).wait_recv()
@@ -674,22 +692,21 @@
     s.gained[t] = (mid * gain_mlp[:, columns(t)]).astype(BF16)
     for k in range(1, TP):
         gained_move(k).start()
-    for k in range(1, TP):
-        gained_landed(k).wait_recv()
-
-    def product(p, total):
-        return total + jnp.sum(s.gained[p].astype(F32) * s.strm[y, p].astype(F32), axis=1, keepdims=True)
-
-    inner = lax.fori_loop(0, TP, product, jnp.zeros((T, 1), F32))
+    s.out_grad[...] = jnp.zeros_like(s.out_grad)
+
+    def unproject(kt, inner):
+        @pl.when(kt > 0)
+        def _():
+            gained_landed(kt).wait_recv()
+
+        p = (t - kt + TP) % TP
+        part = s.gained[p]
+        s.out_grad[...] += mm_t(part, s.v_out[:, columns(p)])
+        return inner + jnp.sum(part.astype(F32) * s.strm[y, p].astype(F32), axis=1, keepdims=True)
+
+    inner = lax.fori_loop(0, TP, unproject, jnp.zeros((T, 1), F32))
     pull = scale * scale * scale * (inner / D)
-    s.out_grad[...] = jnp.zeros_like(s.out_grad)
-
-    def unproject(p, _):
-        delta = (s.gained[p].astype(F32) * scale - s.strm[y, p].astype(F32) * pull).astype(BF16)
-        s.out_grad[...] += mm_t(delta, s.v_out[:, columns(p)])
-        return 0
-
-    lax.fori_loop(0, TP, unproject, 0)
+    s.out_grad[...] = s.out_grad[...] * scale - s.along[...] * pull
 
     inject, values = s.proj[:, 512:640], s.proj[:, 640:768]
     raw = s.proj[:, 768:896]

time: 216 us -> 204 us (0.944)
  Pallas kernels: 215 us -> 202 us
    pallas_call x1, Pallas kernels: 213 us -> 200 us  [local(): pl.pallas_call(whole_kernel, out_shape=struct((ROWS, PACK), F32), in_spec...]
where the time goes in v4:
time: 204 us; the launch traced here: 203 us
  Pallas kernels  202 us (99%)
    pallas_call x1, Pallas kernels, local(): pl.pallas_call(whole_kernel, out_shape=struct((ROWS, PACK), F32), in_spec...  200 us

profile of v4, /device:TPU:1, one launch (start us, length us, event | category | flops | bytes accessed | tf_op | source)
XLA Modules:
  0.0 203.1 jit_solution(10633116250583831738)
XLA Ops:
  0.6 200.3 %whole.1.packed = f32[256,896]{1,0:T(8,128)} custom-call(bf16[128,4096]{1,0:T(8,128)(2,1)} %resid.1, bf16[128,4096]{1,0:T(8,128)(2,1)} %teacher.1, f32[1,4096]{1,0:T(1,128)} %bitcast.5, f32[1,4096]{1,0:T(1,128)} %bitcast.6, bf16[4096,512]{1,0:T(8,128)(2,1)} %w_c.1, bf16[4096,128]{1,0:T(8,128)(2,1)} %w_b.1, bf16[4096,128]{1,0:T(8,128)(2,1)} %w_x.1, ...), custom_call_target="tpu_custom_call" | custom-call | tf_op jit(solution)/shard_map/whole/pallas_call | solution.py:859
  201.0 2.1 %split.1 = (f32[256,512]{1,0:T(8,128)}, f32[256,128]{1,0:T(8,128)}, f32[256,128]{1,0:T(8,128)}, f32[4,256]{1,0:T(4,128)}) custom-call(f32[256,896]{1,0:T(8,128)} %whole.1.packed), custom_call_target="tpu_custom_call" | custom-call | tf_op jit(solution)/shard_map/split/pallas_call | solution.py:873

commit v5 on v4

--- a/solution.py
+++ b/solution.py
@@ -244,7 +244,7 @@
     "v_wb": pltpu.VMEM((D, 128), BF16),
     "v_wx": pltpu.VMEM((D, 128), BF16),
     "v_wdt": pltpu.VMEM((HEADS, D), BF16),
-    "v_out": pltpu.VMEM((512, D), BF16),
+    "v_out": pltpu.VMEM((TP, 512, WIDTH), BF16),
     "v_resid": pltpu.VMEM((T, WIDTH), BF16),
     "nin": pltpu.VMEM((T, D), BF16),
     "nin_t": pltpu.VMEM((DP, 256, T), BF16),
@@ -261,9 +261,18 @@
     "mixer_out": pltpu.VMEM((T, WIDTH), BF16),
     "fade": pltpu.VMEM((HEADS, T, T), F32),
     "plain": pltpu.VMEM((HEADS, T, T), F32),
-    "p_send": pltpu.VMEM((2, TP, T, WIDTH), BF16),
-    "p_recv": pltpu.VMEM((2, TP, T, WIDTH), BF16),
-    "strm": pltpu.VMEM((2, TP, T, WIDTH), BF16),
+    "p_send": pltpu.VMEM((TP, T, WIDTH), BF16),
+    "p_recv": pltpu.VMEM((TP, T, WIDTH), BF16),
+    "str_a": pltpu.VMEM((4, 4, T // 2, WIDTH), BF16),
+    "str_b": pltpu.VMEM((4, 4, T // 2, WIDTH), BF16),
+    "mid_a": pltpu.VMEM((4, 4, T // 2, WIDTH), BF16),
+    "mid_b": pltpu.VMEM((4, 4, T // 2, WIDTH), BF16),
+    "got_a": pltpu.VMEM((3, 4, T // 2, WIDTH), BF16),
+    "got_b": pltpu.VMEM((3, 4, T // 2, WIDTH), BF16),
+    "sum_a": pltpu.VMEM((4, T // 2, WIDTH), BF16),
+    "sum_b": pltpu.VMEM((4, T // 2, WIDTH), BF16),
+    "end_a": pltpu.VMEM((3, T // 2, WIDTH), BF16),
+    "end_b": pltpu.VMEM((3, T // 2, WIDTH), BF16),
     "gained": pltpu.VMEM((TP, T, WIDTH), BF16),
     "grads": pltpu.VMEM((2 * T, HID), BF16),
     "squares": pltpu.VMEM((2, T, 128), F32),
@@ -275,7 +284,7 @@
     "dread": pltpu.VMEM((T, WIDTH), F32),
     "dinject": pltpu.VMEM((T, 128), F32),
     "dvalue": pltpu.VMEM((T, 128), F32),
-    "in_sem": pltpu.SemaphoreType.DMA((12,)),
+    "in_sem": pltpu.SemaphoreType.DMA((11 + TP,)),
     "g_send": pltpu.SemaphoreType.DMA((NSEM_HALF,)),
     "g_recv": pltpu.SemaphoreType.DMA((NSEM_HALF,)),
     "a_send": pltpu.SemaphoreType.DMA((2,)),
@@ -290,8 +299,12 @@
     "b_recv": pltpu.SemaphoreType.DMA((8,)),
     "c_send": pltpu.SemaphoreType.DMA((DP - 1,)),
     "c_recv": pltpu.SemaphoreType.DMA((DP - 1,)),
-    "t_send": pltpu.SemaphoreType.DMA((4, DP)),
-    "t_recv": pltpu.SemaphoreType.DMA((4, DP)),
+    "t_send": pltpu.SemaphoreType.DMA((2, TP)),
+    "t_recv": pltpu.SemaphoreType.DMA((2, TP)),
+    "p1_send": pltpu.SemaphoreType.DMA((12,)),
+    "p1_recv": pltpu.SemaphoreType.DMA((12,)),
+    "p2_send": pltpu.SemaphoreType.DMA((12,)),
+    "p2_recv": pltpu.SemaphoreType.DMA((12,)),
 }
 
 
@@ -304,18 +317,14 @@
 
 
 def normalise(ref, rows, gain):
-    def square(k, total):
-        part = ref[rows, chunk(k, 512)].astype(F32)
-        return total + jnp.sum(part * part, axis=1, keepdims=True)
-
-    scale = lax.rsqrt(lax.fori_loop(0, 8, square, jnp.zeros((T, 1), F32)) / D + EPS)
-
-    def write(k, _):
-        at = chunk(k, 512)
+    total = jnp.zeros((T, 1), F32)
+    for k in range(8):
+        part = ref[rows, k * 512 : (k + 1) * 512].astype(F32)
+        total = total + jnp.sum(part * part, axis=1, keepdims=True)
+    scale = lax.rsqrt(total / D + EPS)
+    for k in range(8):
+        at = slice(k * 512, (k + 1) * 512)
         ref[rows, at] = (ref[rows, at].astype(F32) * scale * gain[:, at]).astype(BF16)
-        return 0
-
-    lax.fori_loop(0, 8, write, 0)
 
 
 def state_weights(decays, m, forward):
@@ -361,9 +370,8 @@
         (w_x, s.v_wx),
         (w_dt, s.v_wdt),
         (teacher, s.lhs.at[mine, :]),
-        (w_out, s.v_out),
         (resid.at[:, columns(t)], s.v_resid),
-    )
+    ) + tuple((w_out.at[:, p * WIDTH : (p + 1) * WIDTH], s.v_out.at[p]) for p in range(TP))
     loads = [pltpu.make_async_copy(a, b, s.in_sem.at[k]) for k, (a, b) in enumerate(pairs)]
     for copy in loads:
         copy.start()
@@ -396,18 +404,12 @@
     params = jnp.concatenate([bias_row, rate_row, skip_row, jnp.zeros((5, 128), F32)], axis=0)
     for copy in loads[5:9]:
         copy.wait()
-    s.proj[...] = jnp.zeros_like(s.proj)
-
-    def project(k, _):
-        at = chunk(k, 1024)
-        rows = s.nin[:, at]
-        s.proj[:, 0:512] += jnp.dot(rows, s.v_wc[at, :], preferred_element_type=F32)
-        s.proj[:, 512:640] += jnp.dot(rows, s.v_wb[at, :], preferred_element_type=F32)
-        s.proj[:, 640:768] += jnp.dot(rows, s.v_wx[at, :], preferred_element_type=F32)
-        s.proj[:, 768 : 768 + HEADS] += mm_t(rows, s.v_wdt[:, at])
-        return 0
-
-    lax.fori_loop(0, 4, project, 0)
+    rows = s.nin[...]
+    s.proj[:, 0:512] = jnp.dot(rows, s.v_wc[...], preferred_element_type=F32)
+    s.proj[:, 512:640] = jnp.dot(rows, s.v_wb[...], preferred_element_type=F32)
+    s.proj[:, 640:768] = jnp.dot(rows, s.v_wx[...], preferred_element_type=F32)
+    s.proj[:, 768:896] = jnp.zeros((T, 128), F32)
+    s.proj[:, 768 : 768 + HEADS] = mm_t(rows, s.v_wdt[...])
     s.read[...] = s.proj[:, 0:512].astype(BF16)
     inject, values = s.proj[:, 512:640], s.proj[:, 640:768]
     raw = s.proj[:, 768:896]
@@ -476,46 +478,71 @@
         grown = jnp.exp(decay[:, h : h + 1]) * mm(s.read[:, head(h)], entering)
         s.mixer_out[:, head(h)] = (s.through[:, head(h)] + grown).astype(BF16)
 
-    def move(phase, ky, kt, src, dst):
+    def move(phase, kt, src, dst):
         return pltpu.make_async_remote_copy(
             src_ref=src,
             dst_ref=dst,
-            send_sem=s.t_send.at[phase, ky * TP + kt],
-            recv_sem=s.t_recv.at[phase, ky * TP + kt],
-            device_id={"dp": other if ky else me, "tensor": (t + kt) % TP},
+            send_sem=s.t_send.at[phase, kt],
+            recv_sem=s.t_recv.at[phase, kt],
+            device_id={"tensor": (t + kt) % TP},
             device_id_type=MESH,
         )
 
     def out_move(kt):
-        return move(0, 0, kt, s.p_send.at[0, kt], s.p_recv.at[0, kt])
-
-    def stream_move(ky, kt):
-        return move(1, ky, kt, s.strm.at[y, t], s.strm.at[y, t])
-
-    def stream_landed(ky, kt):
-        at = s.strm.at[(1 - y) if ky else y, (t - kt + TP) % TP]
-        return move(1, ky, kt, at, at)
-
-    def mid_move(ky, kt):
-        return move(2, ky, kt, s.p_send.at[(1 - y) if ky else y, kt], s.p_recv.at[ky, kt])
+        return move(0, kt, s.p_send.at[kt], s.p_recv.at[kt])
 
     def gained_move(kt):
-        return move(3, 0, kt, s.gained.at[t], s.gained.at[t])
+        return move(1, kt, s.gained.at[t], s.gained.at[t])
 
     def gained_landed(kt):
         at = s.gained.at[(t - kt + TP) % TP]
-        return move(3, 0, kt, at, at)
-
-    peers = [(ky, kt) for kt in range(TP) for ky in range(2) if ky + kt > 0]
+        return move(1, kt, at, at)
+
+    px, py = t % 4, (t // 4) * 2 + y
+
+    def plane(sems, leg, over_x, k, src, dst):
+        xx = (px + k) % 4 if over_x else px
+        yy = py if over_x else (py + k) % 4
+        return pltpu.make_async_remote_copy(
+            src_ref=src,
+            dst_ref=dst,
+            send_sem=sems[0].at[3 * leg + k - 1],
+            recv_sem=sems[1].at[3 * leg + k - 1],
+            device_id={"dp": (yy % 2) * 8 + m, "tensor": (yy // 2) * 4 + xx},
+            device_id_type=MESH,
+        )
+
+    def stream_leg(leg, k, landing=False):
+        d = (4 - k) if landing else 0
+        ref = (
+            s.str_a.at[py, (px + d) % 4],
+            s.str_b.at[px, (py + d) % 4],
+            s.str_a.at[(py + d) % 4],
+            s.str_b.at[(px + d) % 4],
+        )[leg]
+        return plane((s.p1_send, s.p1_recv), leg, leg in (0, 3), k, ref, ref)
+
+    def mid_leg(leg, k):
+        src, dst = (
+            (s.mid_a.at[(px + k) % 4], s.got_a.at[k - 1]),
+            (s.mid_b.at[(py + k) % 4], s.got_b.at[k - 1]),
+            (s.sum_a.at[(py + k) % 4], s.end_a.at[k - 1]),
+            (s.sum_b.at[(px + k) % 4], s.end_b.at[k - 1]),
+        )[leg]
+        return plane((s.p2_send, s.p2_recv), leg, leg in (0, 3), k, src, dst)
+
+    def stream_block(yy, p):
+        row, col = 2 * (p // 4) + yy, p % 4
+        return jnp.concatenate([s.str_a[row, col], s.str_b[col, row]], axis=0)
 
     def out_part(p):
-        return jnp.dot(s.mixer_out[...], s.v_out[:, columns(p)], preferred_element_type=F32)
-
-    loads[10].wait()
-    loads[11].wait()
+        return jnp.dot(s.mixer_out[...], s.v_out[p], preferred_element_type=F32)
+
+    for copy in loads[10:]:
+        copy.wait()
 
     def out_send(k, _):
-        s.p_send[0, k] = out_part((t + k) % TP).astype(BF16)
+        s.p_send[k] = out_part((t + k) % TP).astype(BF16)
         out_move(k).start()
         return 0
 
@@ -525,26 +552,22 @@
     gather.arrive("LO1")
     for k in range(1, TP):
         out_move(k).wait_recv()
-        stream = stream + s.p_recv[0, k].astype(F32)
-    s.strm[y, t] = stream.astype(BF16)
-    for ky, kt in peers:
-        stream_move(ky, kt).start()
+        stream = stream + s.p_recv[k].astype(F32)
+    half_rows = T // 2
+    s.str_a[py, px] = stream[0:half_rows].astype(BF16)
+    s.str_b[px, py] = stream[half_rows:T].astype(BF16)
+    for k in (2, 1, 3):
+        stream_leg(0, k).start()
+        stream_leg(1, k).start()
 
     upper_rows, lower_rows = pl.ds(0, 2 * T), pl.ds(2 * T, 2 * T)
 
     def use(flip, dz):
         base = gather.block(flip, dz, 0)
 
-        def one(n, _):
-            at = chunk(n)
-            s.acc[upper_rows, at] += jnp.dot(
-                s.lhs[upper_rows, chunk(base)], s.held[base, :, at], preferred_element_type=F32
-            ) + jnp.dot(
-                s.lhs[upper_rows, chunk(base + 1)], s.held[base + 1, :, at], preferred_element_type=F32
-            )
-            return 0
-
-        lax.fori_loop(0, HID // 256, one, 0)
+        s.acc[upper_rows, :] += jnp.dot(
+            s.lhs[upper_rows, chunk(base)], s.held[base], preferred_element_type=F32
+        ) + jnp.dot(s.lhs[upper_rows, chunk(base + 1)], s.held[base + 1], preferred_element_type=F32)
 
     def turn(k, _):
         s.nin_t[k] = jnp.transpose(s.nin[:, chunk(k)].astype(F32)).astype(BF16)
@@ -552,16 +575,24 @@
 
     lax.fori_loop(0, DP, turn, 0)
     s.acc[upper_rows, :] = jnp.zeros((2 * T, HID), F32)
-    gather.arrive("RX1", "RXA")
-    gather.arrive("LX2", "LXB")
-    gather.arrive("RA")
-    gather.arrive("LB")
     teacher_landed(0).wait_recv()
     teacher_landed(1).wait_recv()
     gather.side_arrive("own")
     use(0, 0)
     gather.side_arrive("YO1", "YO2")
     use(1, 0)
+    for k in (2, 1, 3):
+        stream_leg(0, k, True).wait_recv()
+    for k in (2, 1, 3):
+        stream_leg(2, k).start()
+    for k in (2, 1, 3):
+        stream_leg(1, k, True).wait_recv()
+    for k in (2, 1, 3):
+        stream_leg(3, k).start()
+    gather.arrive("RX1", "RXA")
+    gather.arrive("LX2", "LXB")
+    gather.arrive("RA")
+    gather.arrive("LB")
     gather.side_arrive("RO1", "RO2")
     use(0, -1)
     gather.side_arrive("LO1", "LO2")
@@ -575,47 +606,28 @@
     gather.side_arrive("LX1", "LX2")
     use(1, 1)
 
-    s.acc[lower_rows, :] = jnp.zeros((2 * T, HID), F32)
+    for leg in (2, 3):
+        for k in (2, 1, 3):
+            stream_leg(leg, k, True).wait_recv()
     s.squares[...] = jnp.zeros_like(s.squares)
-    late = gather.block(1, 2, 0) // 2
-
-    def student(p):
+
+    def student_rows(p, _):
         for yy in range(2):
-            part = s.strm[yy, p].astype(F32)
+            part = stream_block(yy, p).astype(F32)
             s.squares[yy] += jnp.broadcast_to(jnp.sum(part * part, axis=1, keepdims=True), (T, 128))
             s.lhs[pl.ds((2 + yy) * T, T), columns(p)] = (part * gain_mlp[:, columns(p)]).astype(BF16)
-
-        def one(n, _):
-            at = chunk(n)
-            s.acc[lower_rows, at] += jnp.dot(
-                s.lhs[lower_rows, chunk(2 * p)], s.held[2 * p, :, at], preferred_element_type=F32
-            ) + jnp.dot(
-                s.lhs[lower_rows, chunk(2 * p + 1)], s.held[2 * p + 1, :, at], preferred_element_type=F32
-            )
-            return 0
-
-        lax.fori_loop(0, HID // 256, one, 0)
-
-    def student_early(kt, _):
-        @pl.when(kt > 0)
-        def _():
-            stream_landed(0, kt).wait_recv()
-
-        stream_landed(1, kt).wait_recv()
-        p = (t - kt + TP) % TP
-
-        @pl.when(p != late)
-        def _():
-            student(p)
-
         return 0
 
-    lax.fori_loop(0, TP, student_early, 0)
+    lax.fori_loop(0, TP, student_rows, 0)
     gather.arrive("RXA")
     gather.arrive("LXB")
     gather.side_arrive("RXA", "LXB")
     use(1, 2)
-    student(late)
+    for n in range(HID // 256):
+        at = slice(n * 256, (n + 1) * 256)
+        s.acc[lower_rows, at] = jnp.dot(
+            s.lhs[lower_rows, :], s.held[:, :, at].reshape(D, 256), preferred_element_type=F32
+        )
     scales = [lax.rsqrt(s.squares[yy, :, 0:1] / D + EPS) for yy in range(2)]
     scale = jnp.where(y == 0, scales[0], scales[1])
     both = jnp.concatenate(scales, axis=0)
@@ -642,8 +654,8 @@
             device_id_type=MESH,
         )
 
-    def hidden(n, _):
-        at, beside = chunk(n, 128), pl.ds(pl.multiple_of(half + n * 128, 128), 128)
+    for n in range(half // 128):
+        at, beside = slice(n * 128, (n + 1) * 128), slice(half + n * 128, half + (n + 1) * 128)
         aim_gate = s.acc[upper_rows, at]
         aim = aim_gate * jax.nn.sigmoid(aim_gate) * s.acc[upper_rows, beside]
         gate, up = s.acc[lower_rows, at] * both, s.acc[lower_rows, beside] * both
@@ -652,43 +664,82 @@
         grad = (2.0 / math.sqrt(FF)) * (silu * up - aim)
         s.grads[:, at] = (grad * up * sigma * (1.0 + gate * (1.0 - sigma))).astype(BF16)
         s.grads[:, beside] = (grad * silu).astype(BF16)
+
+    def back(yh, xx):
+        for i in range(2):
+            part = mm_t(s.grads[...], s.held[2 * (yh * 4 + xx) + i]).astype(BF16)
+            lanes_at = slice(i * 256, (i + 1) * 256)
+            for yy in range(2):
+                s.mid_a[xx, 2 * yh + yy, :, lanes_at] = part[yy * T : yy * T + half_rows, :]
+                s.mid_b[2 * yh + yy, xx, :, lanes_at] = part[yy * T + half_rows : (yy + 1) * T, :]
+
+    def back_far(xx, _):
+        back(1 - t // 4, xx)
         return 0
 
-    lax.fori_loop(0, half // 128, hidden, 0)
-
-    for k in range(1, TP):
-        out_move(k).wait_send()
-
-    def back(kt):
-        p = (t + kt) % TP
-        for i in range(2):
-            part = mm_t(s.grads[...], s.held[2 * p + i]).astype(BF16)
-            for yy in range(2):
-                s.p_send[yy, kt, :, i * 256 : (i + 1) * 256] = part[yy * T : (yy + 1) * T, :]
-
-    def back_send(kt, _):
-        back(kt)
-        mid_move(0, kt).start()
-        mid_move(1, kt).start()
-        return 0
-
-    lax.fori_loop(1, TP, back_send, 0)
-    back(0)
-    mid_move(1, 0).start()
+    lax.fori_loop(0, 4, back_far, 0)
+    mid_leg(1, 2).start()
+
+    @pl.when(y == 0)
+    def _():
+        mid_leg(1, 3).start()
+
+    @pl.when(y == 1)
+    def _():
+        mid_leg(1, 1).start()
+
+    back(t // 4, (px + 2) % 4)
+    mid_leg(0, 2).start()
+    back(t // 4, (px + 1) % 4)
+    mid_leg(0, 1).start()
+    back(t // 4, (px + 3) % 4)
+    mid_leg(0, 3).start()
+    back(t // 4, px)
+
+    @pl.when(y == 0)
+    def _():
+        mid_leg(1, 1).start()
+
+    @pl.when(y == 1)
+    def _():
+        mid_leg(1, 3).start()
+
     for k in range(1, DP):
         column_copy(k).start()
     s.cols[me] = s.nin_t[me]
     s.along[...] = jnp.zeros_like(s.along)
 
     def stream_part(p, _):
-        s.along[...] += mm_t(s.strm[y, p], s.v_out[:, columns(p)])
+        s.along[...] += mm_t(stream_block(y, p), s.v_out[p])
         return 0
 
     lax.fori_loop(0, TP, stream_part, 0)
-    mid = s.p_send[y, 0].astype(F32)
-    for ky, kt in peers:
-        mid_move(ky, kt).wait_recv()
-        mid = mid + s.p_recv[ky, kt].astype(F32)
+
+    def fold(own, got, sums):
+        for at in range(4):
+            total = own[at].astype(F32)
+            for k in range(3):
+                total = total + got[k, at].astype(F32)
+            sums[at] = total.astype(BF16)
+
+    for k in (2, 1, 3):
+        mid_leg(0, k).wait_recv()
+    fold(s.mid_a.at[px], s.got_a, s.sum_a)
+    for k in (2, 1, 3):
+        mid_leg(2, k).start()
+    for k in (2, 1, 3):
+        mid_leg(1, k).wait_recv()
+    fold(s.mid_b.at[py], s.got_b, s.sum_b)
+    for k in (2, 1, 3):
+        mid_leg(3, k).start()
+    parts = []
+    for leg, own, ends_of in ((2, s.sum_a.at[py], s.end_a), (3, s.sum_b.at[px], s.end_b)):
+        total = own[...].astype(F32)
+        for k in (2, 1, 3):
+            mid_leg(leg, k).wait_recv()
+            total = total + ends_of[k - 1].astype(F32)
+        parts.append(total)
+    mid = jnp.concatenate(parts, axis=0)
     s.gained[t] = (mid * gain_mlp[:, columns(t)]).astype(BF16)
     for k in range(1, TP):
         gained_move(k).start()
@@ -701,8 +752,8 @@
 
         p = (t - kt + TP) % TP
         part = s.gained[p]
-        s.out_grad[...] += mm_t(part, s.v_out[:, columns(p)])
-        return inner + jnp.sum(part.astype(F32) * s.strm[y, p].astype(F32), axis=1, keepdims=True)
+        s.out_grad[...] += mm_t(part, s.v_out[p])
+        return inner + jnp.sum(part.astype(F32) * stream_block(y, p).astype(F32), axis=1, keepdims=True)
 
     inner = lax.fori_loop(0, TP, unproject, jnp.zeros((T, 1), F32))
     pull = scale * scale * scale * (inner / D)
@@ -828,10 +879,12 @@
         column_copy(k).wait_send()
     for k in range(2):
         teacher_move(k).wait_send()
-    for ky, kt in peers:
-        stream_move(ky, kt).wait_send()
-        mid_move(ky, kt).wait_send()
+    for leg in range(4):
+        for k in (1, 2, 3):
+            stream_leg(leg, k).wait_send()
+            mid_leg(leg, k).wait_send()
     for k in range(1, TP):
+        out_move(k).wait_send()
         gained_move(k).wait_send()
 
 

time: 204 us -> 180 us (0.88)
  Pallas kernels: 202 us -> 179 us
    pallas_call x1, Pallas kernels: 200 us -> 177 us  [local(): pl.pallas_call(whole_kernel, out_shape=struct((ROWS, PACK), F32), in_spec...]
where the time goes in v5:
time: 180 us
  Pallas kernels  179 us (99%)
    pallas_call x1, Pallas kernels, local(): pl.pallas_call(whole_kernel, out_shape=struct((ROWS, PACK), F32), in_spec...  177 us

profile of v5, /device:TPU:1, one launch (start us, length us, event | category | flops | bytes accessed | tf_op | source)
XLA Modules:
  0.0 179.9 jit_solution(17891862348695217354)
XLA Ops:
  0.6 177.2 %whole.1.packed = f32[256,896]{1,0:T(8,128)} custom-call(bf16[128,4096]{1,0:T(8,128)(2,1)} %resid.1, bf16[128,4096]{1,0:T(8,128)(2,1)} %teacher.1, f32[1,4096]{1,0:T(1,128)} %bitcast.5, f32[1,4096]{1,0:T(1,128)} %bitcast.6, bf16[4096,512]{1,0:T(8,128)(2,1)} %w_c.1, bf16[4096,128]{1,0:T(8,128)(2,1)} %w_b.1, bf16[4096,128]{1,0:T(8,128)(2,1)} %w_x.1, ...), custom_call_target="tpu_custom_call" | custom-call | tf_op jit(solution)/shard_map/whole/pallas_call | solution.py:912
  177.8 2.1 %split.1 = (f32[256,512]{1,0:T(8,128)}, f32[256,128]{1,0:T(8,128)}, f32[256,128]{1,0:T(8,128)}, f32[4,256]{1,0:T(4,128)}) custom-call(f32[256,896]{1,0:T(8,128)} %whole.1.packed), custom_call_target="tpu_custom_call" | custom-call | tf_op jit(solution)/shard_map/split/pallas_call | solution.py:926

commit v6 on v5

v6 whole, which is shorter than its diff:
```python
import math
from types import SimpleNamespace

import jax
import jax.numpy as jnp
from jax import lax
from jax.experimental import pallas as pl
from jax.experimental.pallas import tpu as pltpu
from jax.sharding import PartitionSpec as P

D = 4096
FF = 14336
EPS = 1e-05
T = 128
HEADS = 4
DP = 16
TP = 8
HID = 1792
ROWS = 256
WIDTH = 512
PACK = 896
F32 = jnp.float32
BF16 = jnp.bfloat16
MESH = pl.DeviceIdType.MESH
MIB = 1024 * 1024

RIGHT, LEFT, ACROSS, SIDE = range(4)
FULL, PART, REST, HALF_A, HALF_B, REST_A, REST_B, HALF_A1, HALF_A2, HALF_B1, HALF_B2 = range(11)
RO, LO, YO, RQ, LQ, RA, LB, YL, YR, RQA, LQB, YO2, RO1, RO2, RO3, LO1, LO2, LO3, YO1, RX1, RX2, LX1, LX2, RXA, LXB, OWN = range(26)

LEGS = {
    RO: (RIGHT, 0, 0, FULL, 0, -1),
    LO: (LEFT, 0, 0, FULL, 0, 1),
    YO: (ACROSS, 0, 0, FULL, 1, 0),
    RQ: (RIGHT, 1, 0, REST, 1, -1),
    LQ: (LEFT, 1, 0, REST, 1, 1),
    RA: (RIGHT, 0, -1, HALF_A, 0, 2),
    LB: (LEFT, 0, 1, HALF_B, 0, 2),
    YL: (ACROSS, 0, -1, PART, 1, -1),
    YR: (ACROSS, 0, 1, PART, 1, 1),
    RQA: (RIGHT, 1, -1, REST_A, 1, 2),
    LQB: (LEFT, 1, 1, REST_B, 1, 2),
    YO2: (ACROSS, 0, 2, PART, 1, 2),
}
HALVES = {
    RO1: (RIGHT, 0, 0, HALF_A, 0, -1),
    RO2: (RIGHT, 0, 0, HALF_B1, 0, -1),
    RO3: (RIGHT, 0, 0, HALF_B2, 0, -1),
    LO2: (LEFT, 0, 0, HALF_B, 0, 1),
    LO1: (LEFT, 0, 0, HALF_A1, 0, 1),
    LO3: (LEFT, 0, 0, HALF_A2, 0, 1),
    YO1: (ACROSS, 0, 0, HALF_A, 1, 0),
    YO2: (ACROSS, 0, 0, HALF_B, 1, 0),
    RX1: (RIGHT, 1, 0, HALF_A, 1, -1),
    RX2: (RIGHT, 1, 0, HALF_B, 1, -1),
    LX1: (LEFT, 1, 0, HALF_A, 1, 1),
    LX2: (LEFT, 1, 0, HALF_B, 1, 1),
    RA: (RIGHT, 0, -1, HALF_A, 0, 2),
    LB: (LEFT, 0, 1, HALF_B, 0, 2),
    RXA: (RIGHT, 1, -1, HALF_A, 1, 2),
    LXB: (LEFT, 1, 1, HALF_B, 1, 2),
}
NSEM = 2 * len(LEGS) + 1
NSEM_HALF = 2 * len(HALVES) + 1


def place():
    me = lax.axis_index("dp")
    return me, me // 8, (me % 8) // 2, me % 2


class Gather:
    def __init__(self, legs, piece, rows, p, qa, send, recv, give=None):
        self.legs, self.order = legs, list(legs)
        self.piece, self.send, self.recv, self.give = piece, send, recv, give
        self.me, self.y, self.z, self.c = place()
        half = rows // 2
        self.rows = {
            FULL: (0, rows),
            PART: (0, p),
            REST: (p, rows - p),
            HALF_A: (0, half),
            HALF_B: (half, rows - half),
            HALF_A1: (0, half // 2),
            HALF_A2: (half // 2, half - half // 2),
            HALF_B1: (half, half // 2),
            HALF_B2: (half + half // 2, half - half // 2),
            REST_A: (p, qa),
            REST_B: (p + qa, rows - p - qa),
        }

    def block(self, flip, dz, core):
        y = self.y + flip - 2 * flip * self.y
        return y * 8 + ((self.z + dz + 4) % 4) * 2 + core

    def target(self, name):
        if name == RIGHT:
            return self.block(0, 1, self.c)
        if name == LEFT:
            return self.block(0, -1, self.c)
        if name == ACROSS:
            return self.block(1, 0, self.c)
        return self.block(0, 0, 1 - self.c)

    def copy(self, src, ref, sem, to):
        return pltpu.make_async_remote_copy(
            src_ref=src,
            dst_ref=ref,
            send_sem=self.send.at[sem],
            recv_sem=self.recv.at[sem],
            device_id={"dp": to},
            device_id_type=MESH,
        )

    def leg(self, name):
        to, flip, dz, rows, _, _ = self.legs[name]
        ref = self.piece(self.block(flip, dz, self.c), *self.rows[rows])
        src = ref
        if to == ACROSS and self.give is not None:
            src = self.give(*self.rows[rows])
        return self.copy(src, ref, self.order.index(name), self.target(to))

    def landed(self, name):
        to, _, _, rows, flip, dz = self.legs[name]
        ref = self.piece(self.block(flip, dz, self.c), *self.rows[rows])
        return self.copy(ref, ref, self.order.index(name), self.target(to))

    def side(self, name, core):
        if name == OWN:
            flip, dz, rows, sem = 0, 0, FULL, len(self.order)
        else:
            _, _, _, rows, flip, dz = self.legs[name]
            sem = len(self.order) + 1 + self.order.index(name)
        ref = self.piece(self.block(flip, dz, core), *self.rows[rows])
        return self.copy(ref, ref, sem, self.target(SIDE))

    def begin(self, *names):
        for name in names:
            self.leg(name).start()
        self.side(OWN, self.c).start()

    def arrive(self, name, *then):
        self.landed(name).wait_recv()
        for other in then:
            self.leg(other).start()
        self.side(name, self.c).start()

    def side_arrive(self, *names):
        for name in names:
            self.side(name, 1 - self.c).wait_recv()

    def finish(self):
        for name in self.order:
            self.leg(name).wait_send()
        for name in [OWN] + self.order:
            self.side(name, self.c).wait_send()


def iota(axis):
    return lax.broadcasted_iota(jnp.int32, (T, T), axis)


def mm(a, b):
    return jnp.dot(a.astype(BF16), b.astype(BF16), preferred_element_type=F32)


def mm_t(a, b):
    return lax.dot_general(
        a.astype(BF16), b.astype(BF16), (((1,), (1,)), ((), ())), preferred_element_type=F32
    )


def softplus(v):
    return jnp.maximum(v, 0.0) + jnp.log1p(jnp.exp(-jnp.abs(v)))


def steps_of(raw, params):
    step = softplus(raw + params[0:1, :])
    lower = (iota(0) >= iota(1)).astype(F32)
    decay = jnp.dot(
        lower, -step * params[1:2, :], preferred_element_type=F32, precision=lax.Precision.HIGHEST
    )
    return step, decay, jnp.transpose(step), jnp.transpose(decay)


def head(k):
    return slice(k * 128, (k + 1) * 128)


class States:
    def __init__(self, own, sib, chips, result, out, send, recv):
        self.own, self.sib, self.chips, self.result, self.out = own, sib, chips, result, out
        self.send, self.recv = send, recv
        self.me, self.y, self.z, self.c = place()
        self.q = self.me // 2
        self.mine = pl.ds(pl.multiple_of(self.c * 256, 256), 256)
        self.rest = pl.ds(pl.multiple_of((1 - self.c) * 256, 256), 256)

    def copy(self, src, dst, sem, to):
        return pltpu.make_async_remote_copy(
            src_ref=src,
            dst_ref=dst,
            send_sem=self.send.at[sem],
            recv_sem=self.recv.at[sem],
            device_id={"dp": to},
            device_id_type=MESH,
        )

    def share(self):
        return self.copy(self.own.at[:, self.rest], self.sib, 0, self.q * 2 + 1 - self.c)

    def peer(self, k, landing=False):
        at = self.chips.at[(self.q + 8 - k) % 8 if landing else self.q]
        return self.copy(at, at, k, ((self.q + k) % 8) * 2 + self.c)

    def hand(self, landing=False):
        lanes = self.rest if landing else self.mine
        return self.copy(self.result, self.out.at[:, lanes], 8, self.q * 2 + 1 - self.c)

    def wide(self, row):
        pick = [jnp.where(self.c == 0, row[:, i : i + 1], row[:, 2 + i : 3 + i]) for i in range(2)]
        lane = lax.broadcasted_iota(jnp.int32, (1, 256), 1)
        return jnp.where(lane < 128, pick[0], pick[1])

    def pair(self):
        mine, theirs = self.own[:, self.mine].astype(F32), self.sib[...].astype(F32)
        return jnp.where(self.c == 0, mine, theirs), jnp.where(self.c == 0, theirs, mine)

    def join(self, ends, forward):
        self.share().wait_recv()
        first, second = self.pair()
        if forward:
            total = self.wide(jnp.exp(ends[1])) * first + second
        else:
            total = first + self.wide(jnp.exp(ends[0])) * second
        self.chips[self.q] = total.astype(BF16)
        for k in (4, 1, 7, 2, 6, 3, 5):
            self.peer(k).start()

    def solve(self, ends, weights, forward):
        for k in range(1, 8):
            self.peer(k, True).wait_recv()
        total = jnp.zeros((128, 256), F32)
        for j in range(8):
            total = total + self.wide(weights[j : j + 1, :]) * self.chips[j].astype(F32)
        first, second = self.pair()
        if forward:
            near, far = total, self.wide(jnp.exp(ends[0])) * total + first
        else:
            near, far = second + self.wide(jnp.exp(ends[1])) * total, total
        self.result[...] = jnp.where(self.c == 0, far, near).astype(BF16)
        self.hand().start()
        self.out[:, self.mine] = jnp.where(self.c == 0, near, far).astype(BF16)

    def finish(self):
        self.share().wait_send()
        for k in range(1, 8):
            self.peer(k).wait_send()
        self.hand().wait_send()


def state_weights(decays, q, put):
    ends = [decays[2 * j, 0:1, :] + decays[2 * j + 1, 0:1, :] for j in range(8)]
    for at, order in enumerate((range(7, -1, -1), range(8))):
        run = jnp.zeros((1, 128), F32)
        for j in order:
            reached = ((j < q) if at == 0 else (j > q)).astype(F32)
            put[at, j : j + 1, :] = reached * jnp.exp(run)
            run = run + reached * ends[j]


def spread(scalars):
    lane = lax.broadcasted_iota(jnp.int32, (1, 128), 1)
    row = jnp.zeros((1, 128), F32)
    for h in range(HEADS):
        row = jnp.where(lane == h, scalars[h], row)
    return row


SCRATCH = dict(
    held=pltpu.VMEM((DP, ROWS, HID), BF16),
    give=pltpu.VMEM((ROWS, HID), BF16),
    v_wc=pltpu.VMEM((D, 512), BF16),
    v_wb=pltpu.VMEM((D, 128), BF16),
    v_wx=pltpu.VMEM((D, 128), BF16),
    v_wdt=pltpu.VMEM((HEADS, D), BF16),
    v_out=pltpu.VMEM((TP, 512, WIDTH), BF16),
    v_resid=pltpu.VMEM((T, WIDTH), BF16),
    nin=pltpu.VMEM((T, D), BF16),
    lhs=pltpu.VMEM((4 * T, D), BF16),
    acc=pltpu.VMEM((4 * T, HID), F32),
    proj=pltpu.VMEM((T, PACK), F32),
    read=pltpu.VMEM((T, WIDTH), BF16),
    state=pltpu.VMEM((128, WIDTH), BF16),
    sib=pltpu.VMEM((128, 256), BF16),
    chips=pltpu.VMEM((8, 128, 256), BF16),
    result=pltpu.VMEM((128, 256), BF16),
    decays=pltpu.VMEM((DP, 8, 128), F32),
    weights=pltpu.VMEM((2, 8, 128), F32),
    steps=pltpu.VMEM((4, T, 128), F32),
    read_t=pltpu.VMEM((HEADS, 128, T), BF16),
    enter=pltpu.VMEM((128, WIDTH), BF16),
    through=pltpu.VMEM((T, WIDTH), F32),
    mixer_out=pltpu.VMEM((T, WIDTH), BF16),
    fade=pltpu.VMEM((HEADS, T, T), F32),
    plain=pltpu.VMEM((HEADS, T, T), F32),
    p_send=pltpu.VMEM((TP, T, WIDTH), BF16),
    p_recv=pltpu.VMEM((TP, T, WIDTH), BF16),
    str_a=pltpu.VMEM((4, 4, T // 2, WIDTH), BF16),
    str_b=pltpu.VMEM((4, 4, T // 2, WIDTH), BF16),
    mid_a=pltpu.VMEM((4, 4, T // 2, WIDTH), BF16),
    mid_b=pltpu.VMEM((4, 4, T // 2, WIDTH), BF16),
    got_a=pltpu.VMEM((3, 4, T // 2, WIDTH), BF16),
    got_b=pltpu.VMEM((3, 4, T // 2, WIDTH), BF16),
    sum_a=pltpu.VMEM((4, T // 2, WIDTH), BF16),
    sum_b=pltpu.VMEM((4, T // 2, WIDTH), BF16),
    end_a=pltpu.VMEM((3, T // 2, WIDTH), BF16),
    end_b=pltpu.VMEM((3, T // 2, WIDTH), BF16),
    gained=pltpu.VMEM((TP, T, WIDTH), BF16),
    grads=pltpu.VMEM((2 * T, HID), BF16),
    squares=pltpu.VMEM((2, T, 128), F32),
    out_grad=pltpu.VMEM((T, WIDTH), F32),
    along=pltpu.VMEM((T, WIDTH), F32),
    b_state=pltpu.VMEM((128, WIDTH), BF16),
    b_sib=pltpu.VMEM((128, 256), BF16),
    b_chips=pltpu.VMEM((8, 128, 256), BF16),
    b_result=pltpu.VMEM((128, 256), BF16),
    behind=pltpu.VMEM((128, WIDTH), BF16),
    packed=pltpu.VMEM((DP, T, PACK - WIDTH), BF16),
    read4=pltpu.VMEM((HEADS * T, 128), BF16),
    weight4=pltpu.VMEM((HEADS * T, T), BF16),
    grad4=pltpu.VMEM((HEADS * T, 128), BF16),
    dscore4=pltpu.VMEM((HEADS * T, T), BF16),
    across=pltpu.VMEM((HEADS, T, 128), F32),
    dinject=pltpu.VMEM((T, 128), F32),
    dvalue=pltpu.VMEM((T, 128), F32),
    in_sem=pltpu.SemaphoreType.DMA((11 + TP,)),
    g_send=pltpu.SemaphoreType.DMA((NSEM_HALF,)),
    g_recv=pltpu.SemaphoreType.DMA((NSEM_HALF,)),
    a_send=pltpu.SemaphoreType.DMA((2,)),
    a_recv=pltpu.SemaphoreType.DMA((2,)),
    h_send=pltpu.SemaphoreType.DMA((NSEM,)),
    h_recv=pltpu.SemaphoreType.DMA((NSEM,)),
    i_send=pltpu.SemaphoreType.DMA((NSEM,)),
    i_recv=pltpu.SemaphoreType.DMA((NSEM,)),
    s_send=pltpu.SemaphoreType.DMA((9,)),
    s_recv=pltpu.SemaphoreType.DMA((9,)),
    d_send=pltpu.SemaphoreType.DMA((DP - 1,)),
    d_recv=pltpu.SemaphoreType.DMA((DP - 1,)),
    b_send=pltpu.SemaphoreType.DMA((9,)),
    b_recv=pltpu.SemaphoreType.DMA((9,)),
    c_send=pltpu.SemaphoreType.DMA((DP - 1,)),
    c_recv=pltpu.SemaphoreType.DMA((DP - 1,)),
    t_send=pltpu.SemaphoreType.DMA((2, TP)),
    t_recv=pltpu.SemaphoreType.DMA((2, TP)),
    p1_send=pltpu.SemaphoreType.DMA((12,)),
    p1_recv=pltpu.SemaphoreType.DMA((12,)),
    p2_send=pltpu.SemaphoreType.DMA((12,)),
    p2_recv=pltpu.SemaphoreType.DMA((12,)),
)


def chunk(k, size=256):
    return pl.ds(pl.multiple_of(k * size, size), size)


def columns(p):
    return chunk(p, WIDTH)


def normalise(ref, rows, gain):
    total = jnp.zeros((T, 1), F32)
    for k in range(8):
        part = ref[rows, k * 512 : (k + 1) * 512].astype(F32)
        total = total + jnp.sum(part * part, axis=1, keepdims=True)
    scale = lax.rsqrt(total / D + EPS)
    for k in range(8):
        at = slice(k * 512, (k + 1) * 512)
        ref[rows, at] = (ref[rows, at].astype(F32) * scale * gain[:, at]).astype(BF16)


def whole_kernel(
    resid, teacher, gain_mix, gain_mlp, w_c, w_b, w_x, w_dt, bias, rate, skip, w_out, w_gate, w_up, out, *scratch
):
    s = SimpleNamespace(**dict(zip(SCRATCH, scratch)))
    me, y, z, c = place()
    m = me % 8
    t = lax.axis_index("tensor")
    other = (1 - y) * 8 + m
    half = HID // 2
    keep = pl.ds(pl.multiple_of(y * half, 128), half)
    rest = pl.ds(pl.multiple_of((1 - y) * half, 128), half)
    mine = pl.ds(pl.multiple_of(y * T, T), T)
    pairs = (
        (w_gate.at[:, keep], s.held.at[me, :, 0:half]),
        (w_up.at[:, keep], s.held.at[me, :, half:HID]),
        (w_gate.at[:, rest], s.give.at[:, 0:half]),
        (w_up.at[:, rest], s.give.at[:, half:HID]),
        (resid, s.nin),
        (w_c, s.v_wc),
        (w_b, s.v_wb),
        (w_x, s.v_wx),
        (w_dt, s.v_wdt),
        (teacher, s.lhs.at[mine, :]),
        (resid.at[:, columns(t)], s.v_resid),
    ) + tuple((w_out.at[:, p * WIDTH : (p + 1) * WIDTH], s.v_out.at[p]) for p in range(TP))
    loads = [pltpu.make_async_copy(a, b, s.in_sem.at[k]) for k, (a, b) in enumerate(pairs)]
    for copy in loads:
        copy.start()
    sem = pltpu.get_barrier_semaphore()
    for k in range(1, DP):
        pl.semaphore_signal(sem, inc=1, device_id={"dp": (me + k) % DP}, device_id_type=MESH)
    for k in range(1, TP):
        for dp in (me, other):
            pl.semaphore_signal(
                sem, inc=1, device_id={"dp": dp, "tensor": (t + k) % TP}, device_id_type=MESH
            )
    loads[4].wait()
    normalise(s.nin, slice(None), gain_mix)
    pl.semaphore_wait(sem, DP - 1 + 2 * (TP - 1))
    for copy in loads[0:4]:
        copy.wait()
    gather = Gather(
        HALVES,
        lambda j, start, size: s.held.at[j, pl.ds(start, size), :],
        ROWS,
        112,
        64,
        s.g_send,
        s.g_recv,
        lambda start, size: s.give.at[pl.ds(start, size), :],
    )
    gather.begin(RO1, LO2, YO1)

    bias_row, rate_row, skip_row = spread(bias), spread(rate), spread(skip)
    params = jnp.concatenate([bias_row, rate_row, skip_row, jnp.zeros((5, 128), F32)], axis=0)
    for copy in loads[5:9]:
        copy.wait()
    rows = s.nin[...]
    s.proj[:, 0:512] = jnp.dot(rows, s.v_wc[...], preferred_element_type=F32)
    s.proj[:, 512:640] = jnp.dot(rows, s.v_wb[...], preferred_element_type=F32)
    s.proj[:, 640:768] = jnp.dot(rows, s.v_wx[...], preferred_element_type=F32)
    s.proj[:, 768:896] = jnp.zeros((T, 128), F32)
    s.proj[:, 768 : 768 + HEADS] = mm_t(rows, s.v_wdt[...])
    s.read[...] = s.proj[:, 0:512].astype(BF16)
    inject, values = s.proj[:, 512:640], s.proj[:, 640:768]
    raw = s.proj[:, 768:896]
    gather.leg(RO2).start()
    gather.leg(LO1).start()
    step, decay, step_t, decay_t = steps_of(raw, params)
    s.decays[me] = jnp.broadcast_to(decay[T - 1 : T, :], (8, 128))

    def ends_move(k):
        ref = s.decays.at[me]
        return pltpu.make_async_remote_copy(
            src_ref=ref,
            dst_ref=ref,
            send_sem=s.d_send.at[k - 1],
            recv_sem=s.d_recv.at[k - 1],
            device_id={"dp": (me + k) % DP},
            device_id_type=MESH,
        )

    def ends_landed(k):
        ref = s.decays.at[(me - k + DP) % DP]
        return pltpu.make_async_remote_copy(
            src_ref=ref,
            dst_ref=ref,
            send_sem=s.d_send.at[k - 1],
            recv_sem=s.d_recv.at[k - 1],
            device_id={"dp": (me + k) % DP},
            device_id_type=MESH,
        )

    for k in range(1, DP):
        ends_move(k).start()
    causal = iota(0) >= iota(1)
    inject_t = jnp.transpose(inject)
    for h in range(HEADS):
        s.read4[head(h), :] = s.read[:, head(h)]
    score = mm_t(s.read4[...], inject)
    pulls = []
    for h in range(HEADS):
        row, col, step_row = decay_t[h : h + 1, :], decay[:, h : h + 1], step_t[h : h + 1, :]
        s.fade[h] = jnp.exp(jnp.where(causal, col - row, -1e30))
        s.plain[h] = s.fade[h] * score[head(h), :]
        s.weight4[head(h), :] = (s.plain[h] * step_row).astype(BF16)
        pulls.append(inject_t * (jnp.exp(row[:, T - 1 : T] - row) * step_row))
    carried = mm(jnp.concatenate(pulls, axis=0), values)
    for h in range(HEADS):
        s.state[:, head(h)] = carried[head(h), :].astype(BF16)
    q = me // 2
    states = States(s.state, s.sib, s.chips, s.result, s.enter, s.s_send, s.s_recv)
    states.share().start()
    through = mm(s.weight4[...], values)
    for h in range(HEADS):
        s.through[:, head(h)] = through[head(h), :] + skip_row[:, h : h + 1] * values
    for k, value in enumerate((step, decay, step_t, decay_t)):
        s.steps[k] = value
    ends_landed(jnp.where(c == 0, DP - 1, 1)).wait_recv()
    chip_ends = [s.decays[2 * q + i, 0:1, :] for i in range(2)]
    states.join(chip_ends, True)
    gather.leg(YO2).start()
    gather.leg(RO3).start()
    gather.leg(LO3).start()

    loads[9].wait()
    normalise(s.lhs, mine, gain_mlp)
    gather.arrive(RO1, RA)
    gather.arrive(LO2, LB)
    gather.arrive(YO1, RX1, LX1)

    def teacher_move(k):
        ref = s.lhs.at[pl.ds(pl.multiple_of(y * T + k * (T // 2), T // 2), T // 2), :]
        return pltpu.make_async_remote_copy(
            src_ref=ref,
            dst_ref=ref,
            send_sem=s.a_send.at[k],
            recv_sem=s.a_recv.at[k],
            device_id={"dp": other, "tensor": (t + 4 * k) % TP},
            device_id_type=MESH,
        )

    def teacher_landed(k):
        ref = s.lhs.at[pl.ds(pl.multiple_of((1 - y) * T + k * (T // 2), T // 2), T // 2), :]
        return pltpu.make_async_remote_copy(
            src_ref=ref,
            dst_ref=ref,
            send_sem=s.a_send.at[k],
            recv_sem=s.a_recv.at[k],
            device_id={"dp": other, "tensor": (t + 4 * k) % TP},
            device_id_type=MESH,
        )

    for k in range(2, DP - 1):
        ends_landed(k).wait_recv()
    ends_landed(jnp.where(c == 0, 1, DP - 1)).wait_recv()
    state_weights(s.decays, q, s.weights)
    states.solve(chip_ends, s.weights[0], True)
    states.hand(True).wait_recv()
    for h in range(HEADS):
        grown = jnp.exp(decay[:, h : h + 1]) * mm(s.read[:, head(h)], s.enter[:, head(h)])
        s.mixer_out[:, head(h)] = (s.through[:, head(h)] + grown).astype(BF16)

    def move(phase, kt, src, dst):
        return pltpu.make_async_remote_copy(
            src_ref=src,
            dst_ref=dst,
            send_sem=s.t_send.at[phase, kt],
            recv_sem=s.t_recv.at[phase, kt],
            device_id={"tensor": (t + kt) % TP},
            device_id_type=MESH,
        )

    def out_move(kt):
        return move(0, kt, s.p_send.at[kt], s.p_recv.at[kt])

    def gained_move(kt):
        return move(1, kt, s.gained.at[t], s.gained.at[t])

    def gained_landed(kt):
        at = s.gained.at[(t - kt + TP) % TP]
        return move(1, kt, at, at)

    px, py = t % 4, (t // 4) * 2 + y

    def plane(sems, leg, over_x, k, src, dst):
        xx = (px + k) % 4 if over_x else px
        yy = py if over_x else (py + k) % 4
        return pltpu.make_async_remote_copy(
            src_ref=src,
            dst_ref=dst,
            send_sem=sems[0].at[3 * leg + k - 1],
            recv_sem=sems[1].at[3 * leg + k - 1],
            device_id={"dp": (yy % 2) * 8 + m, "tensor": (yy // 2) * 4 + xx},
            device_id_type=MESH,
        )

    def stream_leg(leg, k, landing=False):
        d = (4 - k) if landing else 0
        ref = (
            s.str_a.at[py, (px + d) % 4],
            s.str_b.at[px, (py + d) % 4],
            s.str_a.at[(py + d) % 4],
            s.str_b.at[(px + d) % 4],
        )[leg]
        return plane((s.p1_send, s.p1_recv), leg, leg in (0, 3), k, ref, ref)

    def mid_leg(leg, k):
        src, dst = (
            (s.mid_a.at[(px + k) % 4], s.got_a.at[k - 1]),
            (s.mid_b.at[(py + k) % 4], s.got_b.at[k - 1]),
            (s.sum_a.at[(py + k) % 4], s.end_a.at[k - 1]),
            (s.sum_b.at[(px + k) % 4], s.end_b.at[k - 1]),
        )[leg]
        return plane((s.p2_send, s.p2_recv), leg, leg in (0, 3), k, src, dst)

    def stream_block(yy, p):
        row, col = 2 * (p // 4) + yy, p % 4
        return jnp.concatenate([s.str_a[row, col], s.str_b[col, row]], axis=0)

    def out_part(p):
        return jnp.dot(s.mixer_out[...], s.v_out[p], preferred_element_type=F32)

    for copy in loads[10:]:
        copy.wait()

    def out_send(k, _):
        s.p_send[k] = out_part((t + k) % TP).astype(BF16)
        out_move(k).start()
        return 0

    lax.fori_loop(1, TP, out_send, 0)
    stream = out_part(t) + s.v_resid[...].astype(F32)
    gather.arrive(YO2, LX2, RX2)
    gather.arrive(RO2)
    gather.arrive(LO1)
    gather.arrive(RO3)
    gather.arrive(LO3)
    for k in range(1, TP):
        out_move(k).wait_recv()
        stream = stream + s.p_recv[k].astype(F32)
    half_rows = T // 2
    s.str_a[py, px] = stream[0:half_rows].astype(BF16)
    s.str_b[px, py] = stream[half_rows:T].astype(BF16)
    for k in (2, 1, 3):
        stream_leg(0, k).start()
        stream_leg(1, k).start()

    def column_copy(k):
        to = (k // 8 + y) % 2 * 8 + (m + k) % 8
        return pltpu.make_async_remote_copy(
            src_ref=s.v_wx.at[chunk(to), :],
            dst_ref=s.v_wb.at[chunk(me), :],
            send_sem=s.c_send.at[k - 1],
            recv_sem=s.c_recv.at[k - 1],
            device_id={"dp": to},
            device_id_type=MESH,
        )

    def column_landed(k):
        at = (k // 8 + y) % 2 * 8 + (m - k + DP) % 8
        return pltpu.make_async_remote_copy(
            src_ref=s.v_wx.at[chunk(at), :],
            dst_ref=s.v_wb.at[chunk(at), :],
            send_sem=s.c_send.at[k - 1],
            recv_sem=s.c_recv.at[k - 1],
            device_id={"dp": at},
            device_id_type=MESH,
        )

    near, far = range(1, 8), range(8, DP)

    upper_rows, lower_rows = pl.ds(0, 2 * T), pl.ds(2 * T, 2 * T)

    def use(flip, dz, rows=upper_rows):
        base = gather.block(flip, dz, 0)
        s.acc[rows, :] += jnp.dot(
            s.lhs[rows, chunk(base)], s.held[base], preferred_element_type=F32
        ) + jnp.dot(s.lhs[rows, chunk(base + 1)], s.held[base + 1], preferred_element_type=F32)

    def turn(k, _):
        s.v_wx[chunk(k), :] = jnp.transpose(s.nin[:, chunk(k)].astype(F32)).astype(BF16)
        return 0

    lax.fori_loop(0, DP, turn, 0)
    growth_t = jnp.exp(s.steps[3])
    for h in range(HEADS):
        s.read_t[h] = (jnp.transpose(s.read[:, head(h)].astype(F32)) * growth_t[h : h + 1, :]).astype(BF16)
    s.acc[...] = jnp.zeros_like(s.acc)
    for k in (2, 1, 3):
        stream_leg(0, k, True).wait_recv()
    for k in (2, 1, 3):
        stream_leg(2, k).start()
    for k in (2, 1, 3):
        stream_leg(1, k, True).wait_recv()
    for k in (2, 1, 3):
        stream_leg(3, k).start()
    teacher_move(0).start()
    teacher_move(1).start()
    gather.arrive(RX1, RXA)
    gather.arrive(RA)
    gather.arrive(LB)
    gather.arrive(LX1)
    gather.arrive(LX2, LXB)
    gather.arrive(RX2)

    for leg in (2, 3):
        for k in (2, 1, 3):
            stream_leg(leg, k, True).wait_recv()
    s.squares[...] = jnp.zeros_like(s.squares)

    def student_rows(p, _):
        for yy in range(2):
            part = stream_block(yy, p).astype(F32)
            s.squares[yy] += jnp.broadcast_to(jnp.sum(part * part, axis=1, keepdims=True), (T, 128))
            s.lhs[pl.ds((2 + yy) * T, T), columns(p)] = (part * gain_mlp[:, columns(p)]).astype(BF16)
        return 0

    lax.fori_loop(0, TP, student_rows, 0)

    def student(i, _):
        use(i % 2, jnp.where(i < 2, 0, jnp.where(i < 4, 3, jnp.where(i < 6, 1, 2))), lower_rows)
        return 0

    gather.side_arrive(OWN, YO1, YO2, RO1, RO2, RO3, LO1, LO2, LO3, RA, LB, RX1, RX2, LX1, LX2)
    lax.fori_loop(0, 7, student, 0)
    teacher_landed(0).wait_recv()
    teacher_landed(1).wait_recv()
    for k in far:
        column_copy(k).start()
    gather.arrive(RXA)
    gather.arrive(LXB)

    def teach(i, _):
        use(i % 2, jnp.where(i < 2, 0, jnp.where(i < 4, 3, jnp.where(i < 6, 1, 2))))
        return 0

    lax.fori_loop(0, 7, teach, 0)
    gather.side_arrive(RXA, LXB)
    use(1, 2, slice(None))
    scales = [lax.rsqrt(s.squares[yy, :, 0:1] / D + EPS) for yy in range(2)]
    scale = jnp.where(y == 0, scales[0], scales[1])
    both = jnp.concatenate(scales, axis=0)

    for n in range(half // 128):
        at, beside = slice(n * 128, (n + 1) * 128), slice(half + n * 128, half + (n + 1) * 128)
        aim_gate = s.acc[upper_rows, at]
        aim = aim_gate * jax.nn.sigmoid(aim_gate) * s.acc[upper_rows, beside]
        gate, up = s.acc[lower_rows, at] * both, s.acc[lower_rows, beside] * both
        sigma = jax.nn.sigmoid(gate)
        silu = gate * sigma
        grad = (2.0 / math.sqrt(FF)) * (silu * up - aim)
        s.grads[:, at] = (grad * up * sigma * (1.0 + gate * (1.0 - sigma))).astype(BF16)
        s.grads[:, beside] = (grad * silu).astype(BF16)

    def back(yh, xx):
        for i in range(2):
            part = mm_t(s.grads[...], s.held[2 * (yh * 4 + xx) + i]).astype(BF16)
            lanes_at = slice(i * 256, (i + 1) * 256)
            for yy in range(2):
                s.mid_a[xx, 2 * yh + yy, :, lanes_at] = part[yy * T : yy * T + half_rows, :]
                s.mid_b[2 * yh + yy, xx, :, lanes_at] = part[yy * T + half_rows : (yy + 1) * T, :]

    def back_far(xx, _):
        back(1 - t // 4, xx)
        return 0

    lax.fori_loop(0, 4, back_far, 0)
    mid_leg(1, 2).start()

    @pl.when(y == 0)
    def _():
        mid_leg(1, 3).start()

    @pl.when(y == 1)
    def _():
        mid_leg(1, 1).start()

    back(t // 4, (px + 2) % 4)
    mid_leg(0, 2).start()
    back(t // 4, (px + 1) % 4)
    mid_leg(0, 1).start()
    back(t // 4, (px + 3) % 4)
    mid_leg(0, 3).start()
    back(t // 4, px)

    @pl.when(y == 0)
    def _():
        mid_leg(1, 1).start()

    @pl.when(y == 1)
    def _():
        mid_leg(1, 3).start()

    for k in near:
        column_copy(k).start()
    s.v_wb[chunk(me), :] = s.v_wx[chunk(me), :]
    s.along[...] = jnp.zeros_like(s.along)

    def stream_part(p, _):
        s.along[...] += mm_t(stream_block(y, p), s.v_out[p])
        return 0

    lax.fori_loop(0, TP, stream_part, 0)

    def fold(own, got, sums):
        for at in range(4):
            total = own[at].astype(F32)
            for k in range(3):
                total = total + got[k, at].astype(F32)
            sums[at] = total.astype(BF16)

    for k in (2, 1, 3):
        mid_leg(0, k).wait_recv()
    fold(s.mid_a.at[px], s.got_a, s.sum_a)
    for k in (2, 1, 3):
        mid_leg(2, k).start()
    for k in (2, 1, 3):
        mid_leg(1, k).wait_recv()
    fold(s.mid_b.at[py], s.got_b, s.sum_b)
    for k in (2, 1, 3):
        mid_leg(3, k).start()
    parts = []
    for leg, own, ends_of in ((2, s.sum_a.at[py], s.end_a), (3, s.sum_b.at[px], s.end_b)):
        total = own[...].astype(F32)
        for k in (2, 1, 3):
            mid_leg(leg, k).wait_recv()
            total = total + ends_of[k - 1].astype(F32)
        parts.append(total)
    mid = jnp.concatenate(parts, axis=0)
    s.gained[t] = (mid * gain_mlp[:, columns(t)]).astype(BF16)
    for k in range(1, TP):
        gained_move(k).start()
    s.out_grad[...] = jnp.zeros_like(s.out_grad)

    def unproject(kt, inner):
        @pl.when(kt > 0)
        def _():
            gained_landed(kt).wait_recv()

        p = (t - kt + TP) % TP
        part = s.gained[p]
        s.out_grad[...] += mm_t(part, s.v_out[p])
        return inner + jnp.sum(part.astype(F32) * stream_block(y, p).astype(F32), axis=1, keepdims=True)

    inner = lax.fori_loop(0, TP, unproject, jnp.zeros((T, 1), F32))
    pull = scale * scale * scale * (inner / D)
    s.out_grad[...] = s.out_grad[...] * scale - s.along[...] * pull

    inject, values = s.proj[:, 512:640], s.proj[:, 640:768]
    raw = s.proj[:, 768:896]
    step, decay, step_t, decay_t = [s.steps[k] for k in range(4)]
    growth = jnp.exp(decay)
    for h in range(HEADS):
        s.b_state[:, head(h)] = mm(s.read_t[h], s.out_grad[:, head(h)]).astype(BF16)
    states_back = States(s.b_state, s.b_sib, s.b_chips, s.b_result, s.behind, s.b_send, s.b_recv)
    states_back.share().start()
    early = Gather(
        LEGS, lambda j, start, size: s.v_wc.at[pl.ds(pl.multiple_of(j * T + start, 16), size), :], T, 48, 48, s.h_send, s.h_recv
    )
    last = Gather(
        LEGS, lambda j, start, size: s.packed.at[j, pl.ds(start, size), :], T, 48, 48, s.i_send, s.i_recv
    )
    lanes = lax.broadcasted_iota(jnp.int32, (1, 128), 1)
    for h in range(HEADS):
        s.grad4[head(h), :] = s.out_grad[:, head(h)].astype(BF16)
    dweight = mm_t(s.grad4[...], values)
    for h in range(HEADS):
        s.dscore4[head(h), :] = (dweight[head(h), :] * s.fade[h] * step_t[h : h + 1, :]).astype(BF16)
        s.across[h] = growth[:, h : h + 1] * mm_t(s.grad4[head(h), :], s.enter[:, head(h)])
    inner_read = mm(s.dscore4[...], inject)
    chip_ends = [s.decays[2 * q + i, 0:1, :] for i in range(2)]
    states_back.join(chip_ends, False)
    for h in range(HEADS):
        s.v_wc[chunk(me, T), head(h)] = (inner_read[head(h), :] + s.across[h]).astype(BF16)
    early.begin(RO, LO, YO)
    step_rows, decay_rows, decay_cols = [], [], []
    skipped = jnp.zeros((T, 128), F32)
    for h in range(HEADS):
        step_row = step_t[h : h + 1, :]
        direct = dweight[head(h), :] * s.plain[h]
        skipped = skipped + skip_row[:, h : h + 1] * s.out_grad[:, head(h)]
        column = jnp.sum(direct, axis=0, keepdims=True)
        step_rows.append(column)
        decay_rows.append(-column * step_row)
        both_ways = direct * step_row + s.across[h] * s.read[:, head(h)].astype(F32)
        decay_cols.append(jnp.sum(both_ways, axis=1, keepdims=True))
    rows_dot = (((0,), (0,)), ((), ()))
    s.dinject[...] = lax.dot_general(s.dscore4[...], s.read4[...], rows_dot, preferred_element_type=F32)
    s.dvalue[...] = skipped + lax.dot_general(
        s.weight4[...], s.grad4[...], rows_dot, preferred_element_type=F32
    )
    states_back.solve(chip_ends, s.weights[1], False)
    early.arrive(YO, RQ, LQ)
    early.arrive(RO, RA, YL)
    early.arrive(LO, LB, YR)
    states_back.hand(True).wait_recv()
    dstep = jnp.zeros((T, 128), F32)
    ddecay = jnp.zeros((T, 128), F32)
    drawn_values = mm(inject, s.behind[...])
    dinject, dvalue = s.dinject[...], s.dvalue[...]
    final = (lax.broadcasted_iota(jnp.int32, (T, 1), 0) == T - 1).astype(F32)
    tails = jnp.exp(decay[T - 1 : T, :] - decay)
    for h in range(HEADS):
        tail_col = tails[:, h : h + 1]
        scaled_col = tail_col * step[:, h : h + 1]
        pulled = mm_t(values, s.behind[:, head(h)])
        dinject = dinject + scaled_col * pulled
        dvalue = dvalue + scaled_col * drawn_values[:, head(h)]
        drawn = tail_col * jnp.sum(inject * pulled, axis=1, keepdims=True)
        moved = drawn * step[:, h : h + 1]
        product = s.behind[:, head(h)].astype(F32) * s.enter[:, head(h)].astype(F32)
        kept = jnp.exp(decay[T - 1 : T, h : h + 1]) * jnp.sum(
            jnp.sum(product, axis=0, keepdims=True), axis=1, keepdims=True
        )
        end = kept + jnp.sum(moved, axis=0, keepdims=True)
        onehot = (lanes == h).astype(F32)
        dstep = dstep + drawn * onehot
        ddecay = ddecay + (decay_cols[h] - moved + final * end) * onehot
    s.packed[me, :, 0:128] = dinject.astype(BF16)
    s.packed[me, :, 128:256] = dvalue.astype(BF16)
    zero = jnp.zeros((128 - HEADS, 128), F32)
    dstep = dstep + jnp.transpose(jnp.concatenate(step_rows + [zero], axis=0))
    ddecay = ddecay + jnp.transpose(jnp.concatenate(decay_rows + [zero], axis=0))
    upper = (iota(0) <= iota(1)).astype(F32)
    later = jnp.dot(upper, ddecay, preferred_element_type=F32, precision=lax.Precision.HIGHEST)
    draw = (dstep - rate_row * later) * jax.nn.sigmoid(raw + bias_row)
    s.packed[me, :, 256:384] = draw.astype(BF16)

    last.begin(RO, LO, YO)
    out[...] = jnp.zeros_like(out)
    for k in range(1, DP):
        column_landed(k).wait_recv()

    def add(lanes_at, base, first, second):
        out[:, lanes_at] += jnp.dot(s.v_wb[chunk(base), :], first, preferred_element_type=F32) + jnp.dot(
            s.v_wb[chunk(base + 1), :], second, preferred_element_type=F32
        )

    def add_c(flip, dz):
        base = early.block(flip, dz, 0)
        add(slice(0, WIDTH), base, s.v_wc[chunk(base, T), :], s.v_wc[chunk(base + 1, T), :])

    def add_rest(flip, dz):
        base = last.block(flip, dz, 0)
        add(slice(WIDTH, PACK), base, s.packed[base], s.packed[base + 1])

    early.arrive(RQ, RQA)
    early.arrive(LQ, LQB)
    early.arrive(RA, YO2)
    early.arrive(LB)
    early.arrive(YL)
    early.arrive(YR)
    early.side_arrive(OWN)
    add_c(0, 0)
    early.side_arrive(YO)
    add_c(1, 0)
    last.arrive(YO, RQ, LQ)
    last.arrive(RO, RA, YL)
    last.arrive(LO, LB, YR)
    early.arrive(RQA)
    early.arrive(LQB)
    early.arrive(YO2)
    early.side_arrive(RO)
    add_c(0, -1)
    early.side_arrive(LO)
    add_c(0, 1)
    last.arrive(RQ, RQA)
    last.arrive(LQ, LQB)
    last.arrive(RA, YO2)
    last.arrive(LB)
    last.arrive(YL)
    last.arrive(YR)
    early.side_arrive(RA, LB)
    add_c(0, 2)
    early.side_arrive(RQ, YL)
    add_c(1, -1)
    early.side_arrive(LQ, YR)
    add_c(1, 1)
    early.side_arrive(RQA, LQB, YO2)
    add_c(1, 2)
    last.arrive(RQA)
    last.arrive(LQB)
    last.arrive(YO2)
    last.side_arrive(OWN)
    add_rest(0, 0)
    last.side_arrive(YO)
    add_rest(1, 0)
    last.side_arrive(RO)
    add_rest(0, -1)
    last.side_arrive(LO)
    add_rest(0, 1)
    last.side_arrive(RA, LB)
    add_rest(0, 2)
    last.side_arrive(RQ, YL)
    add_rest(1, -1)
    last.side_arrive(LQ, YR)
    add_rest(1, 1)
    last.side_arrive(RQA, LQB, YO2)
    add_rest(1, 2)

    gather.finish()
    early.finish()
    last.finish()
    states.finish()
    states_back.finish()
    for k in range(1, DP):
        ends_move(k).wait_send()
        column_copy(k).wait_send()
    for k in range(2):
        teacher_move(k).wait_send()
    for leg in range(4):
        for k in (1, 2, 3):
            stream_leg(leg, k).wait_send()
            mid_leg(leg, k).wait_send()
    for k in range(1, TP):
        out_move(k).wait_send()
        gained_move(k).wait_send()


def split_kernel(packed, grad_c, grad_b, grad_x, grad_dt):
    grad_c[...] = packed[:, 0:512]
    grad_b[...] = packed[:, 512:640]
    grad_x[...] = packed[:, 640:768]
    grad_dt[...] = jnp.transpose(packed[:, 768:896])[0:HEADS, :]


VM = pl.BlockSpec(memory_space=pltpu.VMEM)
SM = pl.BlockSpec(memory_space=pltpu.SMEM)
ANY = pl.BlockSpec(memory_space=pl.ANY)


def struct(shape, dtype):
    return jax.ShapeDtypeStruct(shape, dtype)


def local(
    resid, teacher_mixed, gain_mix, gain_mlp, w_c, w_b, w_x, w_dt, dt_bias, decay_rate, skip, w_out,
    w_gate, w_up,
):
    gain_mix, gain_mlp = gain_mix.reshape(1, D), gain_mlp.reshape(1, D)
    packed = pl.pallas_call(
        whole_kernel,
        out_shape=struct((ROWS, PACK), F32),
        in_specs=[ANY, ANY, VM, VM, ANY, ANY, ANY, ANY, SM, SM, SM, ANY, ANY, ANY],
        out_specs=VM,
        scratch_shapes=list(SCRATCH.values()),
        compiler_params=pltpu.CompilerParams(
            collective_id=0, has_side_effects=True, vmem_limit_bytes=63 * MIB
        ),
        name="whole",
    )(
        resid, teacher_mixed, gain_mix, gain_mlp, w_c, w_b, w_x, w_dt.T, dt_bias, decay_rate, skip, w_out,
        w_gate, w_up,
    )
    grad_c, grad_b, grad_x, grad_dt = pl.pallas_call(
        split_kernel,
        out_shape=(
            struct((ROWS, 512), F32),
            struct((ROWS, 128), F32),
            struct((ROWS, 128), F32),
            struct((HEADS, ROWS), F32),
        ),
        in_specs=[VM],
        out_specs=(VM,) * 4,
        name="split",
    )(packed)
    return grad_c, grad_b, grad_x, grad_dt.T


def solution(mesh):
    in_specs = (
        P("dp", None),
        P("dp", None),
        P(),
        P(),
        P(None, "tensor"),
        P(None, "tensor"),
        P(None, "tensor"),
        P(None, "tensor"),
        P("tensor"),
        P("tensor"),
        P("tensor"),
        P("tensor", None),
        P("dp", "tensor"),
        P("dp", "tensor"),
    )
    out_specs = (P("dp", "tensor"), P("dp", "tensor"), P("dp", "tensor"), P("dp", "tensor"))
    return jax.shard_map(local, mesh=mesh, in_specs=in_specs, out_specs=out_specs, check_vma=False)
```

time: 180 us -> 160 us (0.89)
  Pallas kernels: 179 us -> 159 us
    pallas_call x1, Pallas kernels: 177 us -> 157 us  [local(): pl.pallas_call(whole_kernel, out_shape=struct((ROWS, PACK), F32), in_spec...]
where the time goes in v6:
time: 160 us
  Pallas kernels  159 us (99%)
    pallas_call x1, Pallas kernels, local(): pl.pallas_call(whole_kernel, out_shape=struct((ROWS, PACK), F32), in_spec...  157 us

profile of v6, /device:TPU:1, one launch (start us, length us, event | category | flops | bytes accessed | tf_op | source)
XLA Modules:
  0.0 160.1 jit_solution(3492779521033360010)
XLA Ops:
  0.6 157.4 %whole.1.packed = f32[256,896]{1,0:T(8,128)} custom-call(bf16[128,4096]{1,0:T(8,128)(2,1)} %resid.1, bf16[128,4096]{1,0:T(8,128)(2,1)} %teacher.1, f32[1,4096]{1,0:T(1,128)} %bitcast.5, f32[1,4096]{1,0:T(1,128)} %bitcast.6, bf16[4096,512]{1,0:T(8,128)(2,1)} %w_c.1, bf16[4096,128]{1,0:T(8,128)(2,1)} %w_b.1, bf16[4096,128]{1,0:T(8,128)(2,1)} %w_x.1, ...), custom_call_target="tpu_custom_call" | custom-call | tf_op jit(solution)/shard_map/whole/pallas_call | solution.py:1023
  158.0 2.1 %split.1 = (f32[256,512]{1,0:T(8,128)}, f32[256,128]{1,0:T(8,128)}, f32[256,128]{1,0:T(8,128)}, f32[4,256]{1,0:T(4,128)}) custom-call(f32[256,896]{1,0:T(8,128)} %whole.1.packed), custom_call_target="tpu_custom_call" | custom-call | tf_op jit(solution)/shard_map/split/pallas_call | solution.py:1037

commit v7 on v6

--- a/solution.py
+++ b/solution.py
@@ -337,8 +337,8 @@
     in_sem=pltpu.SemaphoreType.DMA((11 + TP,)),
     g_send=pltpu.SemaphoreType.DMA((NSEM_HALF,)),
     g_recv=pltpu.SemaphoreType.DMA((NSEM_HALF,)),
-    a_send=pltpu.SemaphoreType.DMA((2,)),
-    a_recv=pltpu.SemaphoreType.DMA((2,)),
+    a_send=pltpu.SemaphoreType.DMA((1,)),
+    a_recv=pltpu.SemaphoreType.DMA((1,)),
     h_send=pltpu.SemaphoreType.DMA((NSEM,)),
     h_recv=pltpu.SemaphoreType.DMA((NSEM,)),
     i_send=pltpu.SemaphoreType.DMA((NSEM,)),
@@ -431,6 +431,19 @@
         lambda start, size: s.give.at[pl.ds(start, size), :],
     )
     gather.begin(RO1, LO2, YO1)
+    theirs = pl.ds(pl.multiple_of((1 - y) * T, T), T)
+
+    def teacher_move(rows):
+        return pltpu.make_async_remote_copy(
+            src_ref=teacher,
+            dst_ref=s.lhs.at[rows, :],
+            send_sem=s.a_send.at[0],
+            recv_sem=s.a_recv.at[0],
+            device_id={"dp": other, "tensor": (t + 4) % TP},
+            device_id_type=MESH,
+        )
+
+    teacher_move(mine).start()
 
     bias_row, rate_row, skip_row = spread(bias), spread(rate), spread(skip)
     params = jnp.concatenate([bias_row, rate_row, skip_row, jnp.zeros((5, 128), F32)], axis=0)
@@ -510,28 +523,6 @@
     gather.arrive(LO2, LB)
     gather.arrive(YO1, RX1, LX1)
 
-    def teacher_move(k):
-        ref = s.lhs.at[pl.ds(pl.multiple_of(y * T + k * (T // 2), T // 2), T // 2), :]
-        return pltpu.make_async_remote_copy(
-            src_ref=ref,
-            dst_ref=ref,
-            send_sem=s.a_send.at[k],
-            recv_sem=s.a_recv.at[k],
-            device_id={"dp": other, "tensor": (t + 4 * k) % TP},
-            device_id_type=MESH,
-        )
-
-    def teacher_landed(k):
-        ref = s.lhs.at[pl.ds(pl.multiple_of((1 - y) * T + k * (T // 2), T // 2), T // 2), :]
-        return pltpu.make_async_remote_copy(
-            src_ref=ref,
-            dst_ref=ref,
-            send_sem=s.a_send.at[k],
-            recv_sem=s.a_recv.at[k],
-            device_id={"dp": other, "tensor": (t + 4 * k) % TP},
-            device_id_type=MESH,
-        )
-
     for k in range(2, DP - 1):
         ends_landed(k).wait_recv()
     ends_landed(jnp.where(c == 0, 1, DP - 1)).wait_recv()
@@ -668,6 +659,8 @@
     for h in range(HEADS):
         s.read_t[h] = (jnp.transpose(s.read[:, head(h)].astype(F32)) * growth_t[h : h + 1, :]).astype(BF16)
     s.acc[...] = jnp.zeros_like(s.acc)
+    teacher_move(theirs).wait_recv()
+    normalise(s.lhs, theirs, gain_mlp)
     for k in (2, 1, 3):
         stream_leg(0, k, True).wait_recv()
     for k in (2, 1, 3):
@@ -676,14 +669,25 @@
         stream_leg(1, k, True).wait_recv()
     for k in (2, 1, 3):
         stream_leg(3, k).start()
-    teacher_move(0).start()
-    teacher_move(1).start()
     gather.arrive(RX1, RXA)
     gather.arrive(RA)
     gather.arrive(LB)
     gather.arrive(LX1)
+    gather.side_arrive(OWN, YO1, YO2, RO1, RO2, RO3, LO1, LO2, LO3)
+
+    def teach(i, _):
+        use(jnp.where(i == 1, 1, 0), jnp.where(i < 2, 0, jnp.where(i == 2, 3, 1)))
+        return 0
+
+    lax.fori_loop(0, 4, teach, 0)
+    gather.side_arrive(RA, LB)
+    use(0, 2)
     gather.arrive(LX2, LXB)
     gather.arrive(RX2)
+    gather.side_arrive(RX1, RX2)
+    use(1, -1)
+    gather.side_arrive(LX1, LX2)
+    use(1, 1)
 
     for leg in (2, 3):
         for k in (2, 1, 3):
@@ -703,20 +707,12 @@
         use(i % 2, jnp.where(i < 2, 0, jnp.where(i < 4, 3, jnp.where(i < 6, 1, 2))), lower_rows)
         return 0
 
-    gather.side_arrive(OWN, YO1, YO2, RO1, RO2, RO3, LO1, LO2, LO3, RA, LB, RX1, RX2, LX1, LX2)
     lax.fori_loop(0, 7, student, 0)
-    teacher_landed(0).wait_recv()
-    teacher_landed(1).wait_recv()
     for k in far:
         column_copy(k).start()
     gather.arrive(RXA)
     gather.arrive(LXB)
 
-    def teach(i, _):
-        use(i % 2, jnp.where(i < 2, 0, jnp.where(i < 4, 3, jnp.where(i < 6, 1, 2))))
-        return 0
-
-    lax.fori_loop(0, 7, teach, 0)
     gather.side_arrive(RXA, LXB)
     use(1, 2, slice(None))
     scales = [lax.rsqrt(s.squares[yy, :, 0:1] / D + EPS) for yy in range(2)]
@@ -988,8 +984,7 @@
     for k in range(1, DP):
         ends_move(k).wait_send()
         column_copy(k).wait_send()
-    for k in range(2):
-        teacher_move(k).wait_send()
+    teacher_move(mine).wait_send()
     for leg in range(4):
         for k in (1, 2, 3):
             stream_leg(leg, k).wait_send()

time: 160 us -> 158 us (0.988)
  Pallas kernels: 159 us -> 157 us
    pallas_call x1, Pallas kernels: 157 us -> 155 us  [local(): pl.pallas_call(whole_kernel, out_shape=struct((ROWS, PACK), F32), in_spec...]
where the time goes in v7:
time: 158 us; the launch traced here: 157 us
  Pallas kernels  157 us (99%)
    pallas_call x1, Pallas kernels, local(): pl.pallas_call(whole_kernel, out_shape=struct((ROWS, PACK), F32), in_spec...  155 us

profile of v7, /device:TPU:1, one launch (start us, length us, event | category | flops | bytes accessed | tf_op | source)
XLA Modules:
  0.0 157.4 jit_solution(1259090033964784528)
XLA Ops:
  0.6 154.7 %whole.1.packed = f32[256,896]{1,0:T(8,128)} custom-call(bf16[128,4096]{1,0:T(8,128)(2,1)} %resid.1, bf16[128,4096]{1,0:T(8,128)(2,1)} %teacher.1, f32[1,4096]{1,0:T(1,128)} %bitcast.5, f32[1,4096]{1,0:T(1,128)} %bitcast.6, bf16[4096,512]{1,0:T(8,128)(2,1)} %w_c.1, bf16[4096,128]{1,0:T(8,128)(2,1)} %w_b.1, bf16[4096,128]{1,0:T(8,128)(2,1)} %w_x.1, ...), custom_call_target="tpu_custom_call" | custom-call | tf_op jit(solution)/shard_map/whole/pallas_call | solution.py:1018
  155.4 2.1 %split.1 = (f32[256,512]{1,0:T(8,128)}, f32[256,128]{1,0:T(8,128)}, f32[256,128]{1,0:T(8,128)}, f32[4,256]{1,0:T(4,128)}) custom-call(f32[256,896]{1,0:T(8,128)} %whole.1.packed), custom_call_target="tpu_custom_call" | custom-call | tf_op jit(solution)/shard_map/split/pallas_call | solution.py:1032

commit v8 on v7

--- a/solution.py
+++ b/solution.py
@@ -188,7 +188,8 @@
 
 
 class States:
-    def __init__(self, own, sib, chips, result, out, send, recv):
+    def __init__(self, own, sib, chips, result, out, send, recv, cross=None):
+        self.cross = cross
         self.own, self.sib, self.chips, self.result, self.out = own, sib, chips, result, out
         self.send, self.recv = send, recv
         self.me, self.y, self.z, self.c = place()
@@ -213,6 +214,13 @@
         at = self.chips.at[(self.q + 8 - k) % 8 if landing else self.q]
         return self.copy(at, at, k, ((self.q + k) % 8) * 2 + self.c)
 
+    def row_peer(self, k, landing=False):
+        at = self.chips.at[self.y * 4 + (self.z + (4 - k if landing else 0)) % 4]
+        return self.copy(at, at, k, self.y * 8 + ((self.z + k) % 4) * 2 + self.c)
+
+    def over(self):
+        return self.copy(self.cross.at[0], self.cross.at[1], 4, (1 - self.y) * 8 + self.me % 8)
+
     def hand(self, landing=False):
         lanes = self.rest if landing else self.mine
         return self.copy(self.result, self.out.at[:, lanes], 8, self.q * 2 + 1 - self.c)
@@ -234,15 +242,33 @@
         else:
             total = first + self.wide(jnp.exp(ends[0])) * second
         self.chips[self.q] = total.astype(BF16)
-        for k in (4, 1, 7, 2, 6, 3, 5):
-            self.peer(k).start()
+        if forward:
+            for k in (2, 1, 3):
+                self.row_peer(k).start()
+        else:
+            for k in (4, 1, 7, 2, 6, 3, 5):
+                self.peer(k).start()
 
     def solve(self, ends, weights, forward):
-        for k in range(1, 8):
-            self.peer(k, True).wait_recv()
         total = jnp.zeros((128, 256), F32)
-        for j in range(8):
-            total = total + self.wide(weights[j : j + 1, :]) * self.chips[j].astype(F32)
+        if forward:
+            for k in range(1, 4):
+                self.row_peer(k, True).wait_recv()
+            whole = jnp.zeros((128, 256), F32)
+            for j in range(4):
+                part = self.chips[self.y * 4 + j].astype(F32)
+                total = total + self.wide(weights[j : j + 1, :]) * part
+                whole = whole + self.wide(weights[4 + j : 5 + j, :]) * part
+            self.cross[0] = whole.astype(BF16)
+            self.over().start()
+            self.over().wait_recv()
+            before = self.wide(weights[8:9, :]) * self.cross[1].astype(F32)
+            total = total + jnp.where(self.y == 1, before, 0.0)
+        else:
+            for k in range(1, 8):
+                self.peer(k, True).wait_recv()
+            for j in range(8):
+                total = total + self.wide(weights[j : j + 1, :]) * self.chips[j].astype(F32)
         first, second = self.pair()
         if forward:
             near, far = total, self.wide(jnp.exp(ends[0])) * total + first
@@ -254,19 +280,31 @@
 
     def finish(self):
         self.share().wait_send()
-        for k in range(1, 8):
-            self.peer(k).wait_send()
+        if self.cross is not None:
+            for k in range(1, 4):
+                self.row_peer(k).wait_send()
+            self.over().wait_send()
+        else:
+            for k in range(1, 8):
+                self.peer(k).wait_send()
         self.hand().wait_send()
 
 
-def state_weights(decays, q, put):
-    ends = [decays[2 * j, 0:1, :] + decays[2 * j + 1, 0:1, :] for j in range(8)]
-    for at, order in enumerate((range(7, -1, -1), range(8))):
-        run = jnp.zeros((1, 128), F32)
-        for j in order:
-            reached = ((j < q) if at == 0 else (j > q)).astype(F32)
-            put[at, j : j + 1, :] = reached * jnp.exp(run)
-            run = run + reached * ends[j]
+def state_weights(decays, y, z, put):
+    run_in, run_all = jnp.zeros((1, 128), F32), jnp.zeros((1, 128), F32)
+    for j in reversed(range(4)):
+        reached = (j < z).astype(F32)
+        put[0, j : j + 1, :] = reached * jnp.exp(run_in)
+        put[0, 4 + j : 5 + j, :] = jnp.exp(run_all)
+        end = decays[(y * 4 + j) * 2, 0:1, :] + decays[(y * 4 + j) * 2 + 1, 0:1, :]
+        run_in = run_in + reached * end
+        run_all = run_all + end
+    put[0, 8:9, :] = jnp.exp(run_in)
+    run = jnp.zeros((1, 128), F32)
+    for j in range(8):
+        reached = (j > y * 4 + z).astype(F32)
+        put[1, j : j + 1, :] = reached * jnp.exp(run)
+        run = run + reached * (decays[2 * j, 0:1, :] + decays[2 * j + 1, 0:1, :])
 
 
 def spread(scalars):
@@ -296,7 +334,8 @@
     chips=pltpu.VMEM((8, 128, 256), BF16),
     result=pltpu.VMEM((128, 256), BF16),
     decays=pltpu.VMEM((DP, 8, 128), F32),
-    weights=pltpu.VMEM((2, 8, 128), F32),
+    cross=pltpu.VMEM((2, 128, 256), BF16),
+    weights=pltpu.VMEM((2, 16, 128), F32),
     steps=pltpu.VMEM((4, T, 128), F32),
     read_t=pltpu.VMEM((HEADS, 128, T), BF16),
     enter=pltpu.VMEM((128, WIDTH), BF16),
@@ -405,7 +444,7 @@
         (resid.at[:, columns(t)], s.v_resid),
     ) + tuple((w_out.at[:, p * WIDTH : (p + 1) * WIDTH], s.v_out.at[p]) for p in range(TP))
     loads = [pltpu.make_async_copy(a, b, s.in_sem.at[k]) for k, (a, b) in enumerate(pairs)]
-    for copy in loads:
+    for copy in loads[0:5]:
         copy.start()
     sem = pltpu.get_barrier_semaphore()
     for k in range(1, DP):
@@ -415,8 +454,6 @@
             pl.semaphore_signal(
                 sem, inc=1, device_id={"dp": dp, "tensor": (t + k) % TP}, device_id_type=MESH
             )
-    loads[4].wait()
-    normalise(s.nin, slice(None), gain_mix)
     pl.semaphore_wait(sem, DP - 1 + 2 * (TP - 1))
     for copy in loads[0:4]:
         copy.wait()
@@ -444,6 +481,10 @@
         )
 
     teacher_move(mine).start()
+    for copy in loads[5:]:
+        copy.start()
+    loads[4].wait()
+    normalise(s.nin, slice(None), gain_mix)
 
     bias_row, rate_row, skip_row = spread(bias), spread(rate), spread(skip)
     params = jnp.concatenate([bias_row, rate_row, skip_row, jnp.zeros((5, 128), F32)], axis=0)
@@ -503,7 +544,7 @@
     for h in range(HEADS):
         s.state[:, head(h)] = carried[head(h), :].astype(BF16)
     q = me // 2
-    states = States(s.state, s.sib, s.chips, s.result, s.enter, s.s_send, s.s_recv)
+    states = States(s.state, s.sib, s.chips, s.result, s.enter, s.s_send, s.s_recv, s.cross)
     states.share().start()
     through = mm(s.weight4[...], values)
     for h in range(HEADS):
@@ -521,12 +562,12 @@
     normalise(s.lhs, mine, gain_mlp)
     gather.arrive(RO1, RA)
     gather.arrive(LO2, LB)
-    gather.arrive(YO1, RX1, LX1)
+    gather.arrive(YO1, RX1)
 
     for k in range(2, DP - 1):
         ends_landed(k).wait_recv()
     ends_landed(jnp.where(c == 0, 1, DP - 1)).wait_recv()
-    state_weights(s.decays, q, s.weights)
+    state_weights(s.decays, y, z, s.weights)
     states.solve(chip_ends, s.weights[0], True)
     states.hand(True).wait_recv()
     for h in range(HEADS):
@@ -603,7 +644,7 @@
 
     lax.fori_loop(1, TP, out_send, 0)
     stream = out_part(t) + s.v_resid[...].astype(F32)
-    gather.arrive(YO2, LX2, RX2)
+    gather.arrive(YO2, LX2, RX2, LX1)
     gather.arrive(RO2)
     gather.arrive(LO1)
     gather.arrive(RO3)
@@ -659,6 +700,8 @@
     for h in range(HEADS):
         s.read_t[h] = (jnp.transpose(s.read[:, head(h)].astype(F32)) * growth_t[h : h + 1, :]).astype(BF16)
     s.acc[...] = jnp.zeros_like(s.acc)
+    gather.arrive(RX1, RXA)
+    gather.arrive(LX2, LXB)
     teacher_move(theirs).wait_recv()
     normalise(s.lhs, theirs, gain_mlp)
     for k in (2, 1, 3):
@@ -669,10 +712,8 @@
         stream_leg(1, k, True).wait_recv()
     for k in (2, 1, 3):
         stream_leg(3, k).start()
-    gather.arrive(RX1, RXA)
     gather.arrive(RA)
     gather.arrive(LB)
-    gather.arrive(LX1)
     gather.side_arrive(OWN, YO1, YO2, RO1, RO2, RO3, LO1, LO2, LO3)
 
     def teach(i, _):
@@ -682,7 +723,7 @@
     lax.fori_loop(0, 4, teach, 0)
     gather.side_arrive(RA, LB)
     use(0, 2)
-    gather.arrive(LX2, LXB)
+    gather.arrive(LX1)
     gather.arrive(RX2)
     gather.side_arrive(RX1, RX2)
     use(1, -1)
@@ -707,12 +748,13 @@
         use(i % 2, jnp.where(i < 2, 0, jnp.where(i < 4, 3, jnp.where(i < 6, 1, 2))), lower_rows)
         return 0
 
-    lax.fori_loop(0, 7, student, 0)
+    lax.fori_loop(0, 4, student, 0)
+    gather.arrive(RXA)
+    gather.arrive(LXB)
+    lax.fori_loop(4, 7, student, 0)
+
     for k in far:
         column_copy(k).start()
-    gather.arrive(RXA)
-    gather.arrive(LXB)
-
     gather.side_arrive(RXA, LXB)
     use(1, 2, slice(None))
     scales = [lax.rsqrt(s.squares[yy, :, 0:1] / D + EPS) for yy in range(2)]

time: 158 us -> 155 us (0.981)
  Pallas kernels: 157 us -> 154 us
    pallas_call x1, Pallas kernels: 155 us -> 152 us  [local(): pl.pallas_call(whole_kernel, out_shape=struct((ROWS, PACK), F32), in_spec...]
where the time goes in v8:
time: 155 us; the launch traced here: 154 us
  Pallas kernels  154 us (99%)
    pallas_call x1, Pallas kernels, local(): pl.pallas_call(whole_kernel, out_shape=struct((ROWS, PACK), F32), in_spec...  152 us

profile of v8, /device:TPU:1, one launch (start us, length us, event | category | flops | bytes accessed | tf_op | source)
XLA Modules:
  0.0 154.3 jit_solution(12505600436290736748)
XLA Ops:
  0.6 151.6 %whole.1.packed = f32[256,896]{1,0:T(8,128)} custom-call(bf16[128,4096]{1,0:T(8,128)(2,1)} %resid.1, bf16[128,4096]{1,0:T(8,128)(2,1)} %teacher.1, f32[1,4096]{1,0:T(1,128)} %bitcast.5, f32[1,4096]{1,0:T(1,128)} %bitcast.6, bf16[4096,512]{1,0:T(8,128)(2,1)} %w_c.1, bf16[4096,128]{1,0:T(8,128)(2,1)} %w_b.1, bf16[4096,128]{1,0:T(8,128)(2,1)} %w_x.1, ...), custom_call_target="tpu_custom_call" | custom-call | tf_op jit(solution)/shard_map/whole/pallas_call | solution.py:1060
  152.2 2.1 %split.1 = (f32[256,512]{1,0:T(8,128)}, f32[256,128]{1,0:T(8,128)}, f32[256,128]{1,0:T(8,128)}, f32[4,256]{1,0:T(4,128)}) custom-call(f32[256,896]{1,0:T(8,128)} %whole.1.packed), custom_call_target="tpu_custom_call" | custom-call | tf_op jit(solution)/shard_map/split/pallas_call | solution.py:1074

commit v9 on v8

--- a/solution.py
+++ b/solution.py
@@ -755,8 +755,12 @@
 
     for k in far:
         column_copy(k).start()
+    def use_one(block):
+        s.acc[...] += jnp.dot(s.lhs[:, chunk(block)], s.held[block], preferred_element_type=F32)
+
+    use_one(gather.block(1, 2, c))
     gather.side_arrive(RXA, LXB)
-    use(1, 2, slice(None))
+    use_one(gather.block(1, 2, 1 - c))
     scales = [lax.rsqrt(s.squares[yy, :, 0:1] / D + EPS) for yy in range(2)]
     scale = jnp.where(y == 0, scales[0], scales[1])
     both = jnp.concatenate(scales, axis=0)

time: 155 us -> 155 us (level)
  no operation moved by 1% of the time
where the time goes in v9:
time: 155 us; the launch traced here: 154 us
  Pallas kernels  154 us (99%)
    pallas_call x1, Pallas kernels, local(): pl.pallas_call(whole_kernel, out_shape=struct((ROWS, PACK), F32), in_spec...  152 us

profile of v9, /device:TPU:1, one launch (start us, length us, event | category | flops | bytes accessed | tf_op | source)
XLA Modules:
  0.0 154.3 jit_solution(18162124315675931221)
XLA Ops:
  0.6 151.6 %whole.1.packed = f32[256,896]{1,0:T(8,128)} custom-call(bf16[128,4096]{1,0:T(8,128)(2,1)} %resid.1, bf16[128,4096]{1,0:T(8,128)(2,1)} %teacher.1, f32[1,4096]{1,0:T(1,128)} %bitcast.5, f32[1,4096]{1,0:T(1,128)} %bitcast.6, bf16[4096,512]{1,0:T(8,128)(2,1)} %w_c.1, bf16[4096,128]{1,0:T(8,128)(2,1)} %w_b.1, bf16[4096,128]{1,0:T(8,128)(2,1)} %w_x.1, ...), custom_call_target="tpu_custom_call" | custom-call | tf_op jit(solution)/shard_map/whole/pallas_call | solution.py:1064
  152.2 2.1 %split.1 = (f32[256,512]{1,0:T(8,128)}, f32[256,128]{1,0:T(8,128)}, f32[256,128]{1,0:T(8,128)}, f32[4,256]{1,0:T(4,128)}) custom-call(f32[256,896]{1,0:T(8,128)} %whole.1.packed), custom_call_target="tpu_custom_call" | custom-call | tf_op jit(solution)/shard_map/split/pallas_call | solution.py:1078
